TPU v7x, 512 devices: a whole 4x4x16 slice. The times are simulated.
512 devices in a mesh: dp: 32 (over z, core), mp: 16 (over x, y).
Axes of the slice: x: 4, y: 4, z: 16, core: 2. Of those that a mesh axis runs over, the one named last changes fastest.
Arguments:
- activations: bfloat16 [32768, 6144], P('dp', 'mp'), may hold values from -0.1875 to 0.1875
- hidden: bfloat16 [12288, 32768], P('mp', 'dp'), may hold values from -6 to 6
- feedback: float32 [12288, 6144], P('dp', 'mp'), may hold values from -6 to 6
- momentum: float32 [12288, 6144], P('dp', 'mp'), may hold values from -4 to 4
- q_start: float32 [12288, 8], replicated, may hold values from -6 to 6
Outputs:
- new_feedback: float32 [12288, 6144], P('dp', 'mp')
- new_momentum: float32 [12288, 6144], P('dp', 'mp')
- q_next: float32 [12288, 8], replicated
All inputs are finite; a program needn't handle non-finite values.
Results may differ from a plain program's by a relative error of at most 0.0003.
Values may be sent and summed in bfloat16 or wider, within the bound.
No kernel may reach another device: no remote copies, remote signals or barrier semaphores. Data moves between devices by JAX's collectives and lax.ppermute only.
A program may use at most 64 MiB of HBM per device.

v0:
```python
import jax
import jax.numpy as jnp
from jax import lax
from jax.sharding import PartitionSpec as P

decay_rate = 0.9


def spread(block, axis, owner):
    block = jnp.where(lax.axis_index(axis) == owner, block, jnp.zeros_like(block))
    return lax.psum(block, axis)


def lower_factor(gram_mat):
    return jnp.linalg.cholesky(gram_mat)


def apply_inverse(factor, rows_part):
    return lax.linalg.triangular_solve(
        factor, rows_part, left_side=False, lower=True, transpose_a=True
    )


def per_device(activations, hidden, feedback, momentum, q_start):
    high = lax.Precision.HIGHEST
    cols_mp = hidden.shape[0]
    cols_dp = feedback.shape[0]
    replica = lax.axis_index("dp")
    shard = lax.axis_index("mp")
    own_start = replica * cols_dp
    root_dev = own_start // cols_mp
    inner_start = own_start % cols_mp
    piece = lax.dynamic_slice_in_dim(hidden, inner_start, cols_dp, 0)
    own_hidden = spread(piece, "mp", root_dev)
    own_grad = jnp.dot(own_hidden, activations, preferred_element_type=jnp.float32)
    act_wide = activations.astype(jnp.float32)
    hid_wide = hidden.astype(jnp.float32)
    q_block = lax.dynamic_slice_in_dim(q_start, shard * cols_mp, cols_mp, 0)
    q_owned = lax.dynamic_slice_in_dim(q_start, own_start, cols_dp, 0)
    token_part = jnp.einsum("ct,cr->tr", hid_wide, q_block, precision=high)
    token_q = lax.psum(token_part, "mp")
    p_part = jnp.einsum("td,tr->dr", act_wide, token_q, precision=high)
    p_part = p_part + jnp.einsum("cd,cr->dr", feedback, q_owned, precision=high)
    p_sum = lax.psum(p_part, "dp")
    gram_part = jnp.einsum("dr,ds->rs", p_sum, p_sum, precision=high)
    gram_mat = lax.psum(gram_part, "mp")
    factor = lower_factor(gram_mat)
    ortho = apply_inverse(factor, p_sum)
    proj_part = jnp.dot(act_wide, ortho, precision=high)
    token_o = lax.psum(proj_part, "mp")
    hid_term = jnp.einsum("ct,tr->cr", hid_wide, token_o, precision=high)
    err_term = jnp.dot(feedback, ortho, precision=high)
    blank = jnp.zeros(q_start.shape, jnp.float32)
    q_terms = lax.dynamic_update_slice_in_dim(blank, hid_term, shard * cols_mp, 0)
    q_terms = q_terms + lax.dynamic_update_slice_in_dim(blank, err_term, own_start, 0)
    q_next = lax.psum(q_terms, ("dp", "mp")) / lax.axis_size("dp")
    q_rows = lax.dynamic_slice_in_dim(q_next, own_start, cols_dp, 0)
    approx = jnp.einsum("cr,dr->cd", q_rows, ortho, precision=high)
    new_feedback = own_grad + feedback - approx
    new_momentum = decay_rate * momentum + approx
    return (new_feedback, new_momentum, q_next)


def solution(mesh):
    placed = (P("dp", "mp"), P("mp", "dp"), P("dp", "mp"), P("dp", "mp"), P())
    return jax.shard_map(
        per_device,
        mesh=mesh,
        in_specs=placed,
        out_specs=(P("dp", "mp"), P("dp", "mp"), P()),
        check_vma=False,
    )
```

profile of v0, /device:TPU:6, one launch (start us, length us, event | category | flops | bytes accessed | tf_op | source)
XLA Modules:
  0.0 881.8 jit_solution(11010110934067688833)
XLA Ops:
  7.2 2.3 convolution_bitcast_fusion
  9.5 67.7 %psum.43 = f32[1024,8]{0,1:T(8,128)S(1)} all-reduce(f32[1024,8]{0,1:T(8,128)S(1)} %convolution_bitcast_fusion), channel_id=1, replica_groups=mesh['dp'=32,'mp'=16] {'mp'}, use_global_device_ids=true, to_apply=%region_1.2 | all-reduce | flops 8192 | bytes 65536 | tf_op jit(solution)/shard_map/psum | solution.py:41
  77.2 1.1 fusion.8
  78.3 0.4 fusion.2
  78.8 96.4 %psum.44 = f32[384,8]{0,1:T(8,128)S(1)} all-reduce(f32[384,8]{0,1:T(8,128)S(1)} %fusion.2), channel_id=1, replica_groups=mesh['dp'=32,'mp'=16] {'dp'}, use_global_device_ids=true, to_apply=%region_2.3 | all-reduce | flops 3072 | bytes 24576 | tf_op jit(solution)/shard_map/psum | solution.py:44
  175.1 0.1 fusion.17
  175.2 36.4 %psum.45 = f32[8,8]{0,1:T(8,128)S(1)} all-reduce(f32[8,8]{0,1:T(8,128)S(1)} %fusion.17), channel_id=1, replica_groups=mesh['dp'=32,'mp'=16] {'mp'}, use_global_device_ids=true, to_apply=%region_3.4 | all-reduce | flops 64 | bytes 512 | tf_op jit(solution)/shard_map/psum | solution.py:46
  211.7 0.1 copy.9
  211.7 0.7 cholesky.16
  212.5 0.6 compare_reduce_fusion
  213.1 0.6 fusion.10
  213.8 0.6 custom-call.6
  214.4 0.2 fusion.11
  214.6 0.7 convolution_bitcast_fusion.1
  215.3 70.5 %psum.46 = f32[1024,8]{0,1:T(8,128)S(1)} all-reduce(f32[1024,8]{0,1:T(8,128)S(1)} %convolution_bitcast_fusion.1), channel_id=1, replica_groups=mesh['dp'=32,'mp'=16] {'mp'}, use_global_device_ids=true, to_apply=%region_6.7 | all-reduce | flops 8192 | bytes 65536 | tf_op jit(solution)/shard_map/psum | solution.py:50
  285.8 1.3 fusion.1
  287.2 0.6 fusion.4
  287.8 0.8 copy-done.3
  288.7 1.2 dynamic-slice_select_fusion
  289.9 464.7 %all-reduce.5.cloned.1.call-done = f32[12288,8]{0,1:T(8,128)} async-done(((f32[12288,8]{0,1:T(8,128)}), f32[12288,8]{0,1:T(8,128)}) %all-reduce.5.cloned.1.call-update) | async-done | bytes 393232 | tf_op jit(solution)/shard_map/psum | solution.py:56
  754.6 1.0 broadcast_multiply_fusion
  755.6 1.5 multiply_add_fusion
  757.2 115.2 %all-reduce.3.cloned.1.call-done = bf16[384,1024]{1,0:T(8,128)(2,1)} async-done(((bf16[384,1024]{1,0:T(8,128)(2,1)}), bf16[384,1024]{1,0:T(8,128)(2,1)}) %all-reduce.3.cloned.1.call-update) | async-done | bytes 786448 | tf_op jit(solution)/shard_map/psum | solution.py:11
  872.4 2.5 fusion
  (18 shorter events, 0.2 us)
Async XLA Ops:
  7.2 71.2 %copy-start = (bf16[1024,384]{1,0:T(8,128)(2,1)S(1)}, bf16[1024,384]{1,0:T(8,128)(2,1)}, u32[]{:S(2)}) copy-start(bf16[1024,384]{1,0:T(8,128)(2,1)} %param.5) | copy-start | bytes 2359300
  7.2 70.1 %copy-start.2 = (f32[384,384]{1,0:T(8,128)S(1)}, f32[384,384]{1,0:T(8,128)}, u32[]{:S(2)}) copy-start(f32[384,384]{1,0:T(8,128)} %param.7) | copy-start | bytes 1769476
  7.2 747.4 %all-reduce.5.cloned.1.call-start = ((), (), s32[]{:S(2)}) async-start(), calls=%async_computation.1 | async-start | bytes 786432 | tf_op jit(solution)/shard_map/psum | solution.py:56
  9.5 276.3 %copy-start.1 = (bf16[768,1024]{1,0:T(8,128)(2,1)S(1)}, bf16[768,1024]{1,0:T(8,128)(2,1)}, u32[]{:S(2)}) copy-start(bf16[768,1024]{1,0:T(8,128)(2,1)} %param.6) | copy-start | bytes 4718596
  287.8 0.8 copy-start.3
  288.6 583.8 %all-reduce.3.cloned.1.call-start = ((), (), s32[]{:S(2)}) async-start(), calls=%async_computation | async-start | bytes 1572864 | tf_op jit(solution)/shard_map/psum | solution.py:11
  288.7 466.9 %copy-start.4 = (f32[384,384]{1,0:T(8,128)S(1)}, f32[384,384]{1,0:T(8,128)}, u32[]{:S(2)}) copy-start(f32[384,384]{1,0:T(8,128)} %param.8) | copy-start | bytes 1769476
  755.6 119.3 %copy-start.5 = (f32[12288,8]{0,1:T(8,128)}, f32[12288,8]{0,1:T(8,128)S(1)}, u32[]{:S(2)}) copy-start(f32[12288,8]{0,1:T(8,128)S(1)} %broadcast_multiply_fusion) | copy-start | bytes 1179652
Sparse Core Ops, SparseCore 0:
  288.7 465.8 all-reduce.4
  758.2 114.1 all-reduce.2
where the time goes:
time: 882 us
  waiting for transfers between devices  580 us (66%)
  blocking collectives  271 us (31%)
  between operations  14.2 us (2%)
  matrix products  10.8 us (1%)
    psum x1, waiting for transfers between devices, per_device(): q_next = lax.psum(q_terms, ('dp', 'mp')) / lax.axis_size('dp')  465 us
    psum x1, waiting for transfers between devices, spread(): return lax.psum(block, axis)  115 us
    psum x1, blocking collectives, per_device(): p_sum = lax.psum(p_part, 'dp')  96.4 us
    psum x1, blocking collectives, per_device(): token_o = lax.psum(proj_part, 'mp')  70.5 us
    psum x1, blocking collectives, per_device(): token_q = lax.psum(token_part, 'mp')  67.7 us
    psum x1, blocking collectives, per_device(): gram_mat = lax.psum(gram_part, 'mp')  36.4 us
  transfers between devices with their start and end apart: 2, of which 2 were waited for; matrix products, arithmetic and copies ran while one was open for 0% of the time, Pallas kernels for 0%

commit v1 on v0

v1 whole, which is shorter than its diff:
```python
import jax
import jax.numpy as jnp
from jax import lax
from jax.sharding import Mesh, PartitionSpec as P

decay_rate = 0.9
high = lax.Precision.HIGHEST


def split_parts(x):
    a = lax.reduce_precision(x, 8, 7)
    r = x - a
    b = lax.reduce_precision(r, 8, 7)
    c = r - b
    return jnp.concatenate([a, b, c], 0).astype(jnp.bfloat16)


def thin_dot(x, wide, dims):
    y = lax.dot_general(
        split_parts(x), wide, (dims, ((), ())), preferred_element_type=jnp.float32
    )
    r = x.shape[0]
    return (y[2 * r :] + y[r : 2 * r]) + y[:r]


def copies(x, axes, count):
    return lax.all_to_all(jnp.broadcast_to(x[None], (count,) + x.shape), axes, 0, 0)


def per_device(activations, hidden, feedback, momentum, q_start):
    nz, nc, nx, ny = (lax.axis_size(a) for a in ("z", "c", "x", "y"))
    plane = ("x", "y")
    n_dp, n_mp = nz * nc, nx * ny
    z, core = lax.axis_index("z"), lax.axis_index("c")
    replica = z * nc + core
    shard = lax.axis_index("x") * ny + lax.axis_index("y")
    rank = q_start.shape[1]
    cols_mp, toks = hidden.shape
    cols_dp = feedback.shape[0]
    width = activations.shape[1]
    own_start = replica * cols_dp
    root_dev = own_start // cols_mp
    piece = lax.dynamic_slice_in_dim(hidden, own_start % cols_mp, cols_dp, 0)
    piece = jnp.where(shard == root_dev, piece, jnp.zeros_like(piece))
    own_hidden = lax.psum(piece, plane)

    q_rows = q_start.T
    q_block = lax.dynamic_slice_in_dim(q_rows, shard * cols_mp, cols_mp, 1)
    q_owned = lax.dynamic_slice_in_dim(q_rows, own_start, cols_dp, 1)
    token_part = thin_dot(q_block, hidden, ((1,), (0,)))
    token_q = copies(token_part, plane, n_mp).sum(0)
    p_err = jnp.dot(q_owned, feedback, precision=high)
    p_part = thin_dot(token_q, activations, ((1,), (0,))) + p_err
    p_pair = lax.all_gather(p_part, "c").sum(0)
    p_sum = copies(p_pair, "z", nz).sum(0)

    u_part = thin_dot(p_sum, activations, ((1,), (1,)))
    err_part = lax.dot_general(
        p_sum, feedback, (((1,), (1,)), ((), ())), precision=high
    )
    gram_part = lax.dot_general(p_sum, p_sum, (((1,), (1,)), ((), ())), precision=high)
    packed = jnp.concatenate(
        [u_part, err_part, jnp.pad(gram_part, ((0, 0), (0, 128 - rank)))], 1
    )
    packed = copies(packed, plane, n_mp).sum(0)
    u = packed[:, :toks]
    err = packed[:, toks : toks + cols_dp]
    gram_mat = packed[:, toks + cols_dp : toks + cols_dp + rank]
    factor = jnp.linalg.cholesky(gram_mat)
    inverse = lax.linalg.triangular_solve(
        factor, jnp.eye(rank, dtype=jnp.float32), left_side=True, lower=True
    )
    hid = thin_dot(u, hidden, ((1,), (1,)))
    hid = hid.reshape(rank, nc, cols_mp // nc)
    mine = (shard == root_dev) & (jnp.arange(nc) == core)
    hid = hid + jnp.where(mine[None, :, None], err[:, None, :], 0.0)
    hid = hid.reshape(rank, cols_mp)
    half = lax.all_gather(hid, "c").sum(0)
    half = lax.dynamic_slice_in_dim(half, core * cols_dp, cols_dp, 1)
    half = copies(half, "z", nz).sum(0)
    block = jnp.dot(inverse, half, precision=high) / n_dp
    blocks = copies(block, ("x", "y", "c"), n_dp)
    q_next = jnp.transpose(blocks, (1, 0, 2)).reshape(rank, -1).T
    q_mine = lax.dynamic_index_in_dim(blocks, replica, 0, keepdims=False)
    ortho = jnp.dot(inverse, p_sum, precision=high)
    approx = lax.dot_general(q_mine, ortho, (((0,), (0,)), ((), ())), precision=high)
    own_grad = jnp.dot(own_hidden, activations, preferred_element_type=jnp.float32)
    new_feedback = own_grad + feedback - approx
    new_momentum = decay_rate * momentum + approx
    return (new_feedback, new_momentum, q_next)


def solution(mesh):
    grid = Mesh(mesh.devices.reshape(16, 2, 4, 4), ("z", "c", "x", "y"))
    dp, mp = ("z", "c"), ("x", "y")
    placed = (P(dp, mp), P(mp, dp), P(dp, mp), P(dp, mp), P())
    return jax.shard_map(
        per_device,
        mesh=grid,
        in_specs=placed,
        out_specs=(P(dp, mp), P(dp, mp), P()),
        check_vma=False,
    )
```

time: 882 us -> 196 us (0.22)
  the two profiles are of different devices: /device:TPU:6 before, /device:TPU:33 now
where the time goes in v1:
time: 196 us; the launch traced here: 194 us
  waiting for transfers between devices  101 us (52%)
  blocking collectives  38.3 us (20%)
  starting transfers between devices  21.2 us (11%)
  between operations  14.3 us (7%)
  matrix products  9.12 us (5%)
  other arithmetic  6.04 us (3%)
  local copies, waits for them, and re-layouts  4.28 us (2%)
    psum x1, waiting for transfers between devices, per_device(): own_hidden = lax.psum(piece, plane)  55.7 us
    all_to_all x4, waiting for transfers between devices, copies(): lax.all_to_all(jnp.broadcast_to(x[None], (count,) + x.shape), axes, 0, 0)  45.5 us
    all_to_all x1, blocking collectives, copies(): lax.all_to_all(jnp.broadcast_to(x[None], (count,) + x.shape), axes, 0, 0)  30.5 us
    all_to_all x4, starting transfers between devices, copies(): lax.all_to_all(jnp.broadcast_to(x[None], (count,) + x.shape), axes, 0, 0)  21.2 us
    all_gather x1, blocking collectives, per_device(): half = lax.all_gather(hid, 'c').sum(0)  4.09 us
  transfers between devices with their start and end apart: 5, of which 5 were waited for; matrix products, arithmetic and copies ran while one was open for 5% of the time, Pallas kernels for 0%

profile of v1, /device:TPU:33, one launch (start us, length us, event | category | flops | bytes accessed | tf_op | source)
XLA Modules:
  0.0 194.4 jit_solution(7941692049965186659)
XLA Ops:
  7.2 0.8 reduce-precision_convert_fusion.5
  8.0 1.7 fusion.13
  9.8 0.8 broadcast_in_dim.64
  10.6 6.8 %all-to-all-start = ((f32[16,8,1024]{2,1,0:T(8,128)}), f32[16,8,1024]{2,1,0:T(8,128)S(1)}, u32[]{:S(2)}, u32[]{:S(2)}) async-start(f32[16,8,1024]{2,1,0:T(8,128)} %broadcast_in_dim.64), calls=%async_computation | async-start | bytes 1048576 | tf_op jit(solution)/shard_map/all_to_all | solution.py:27
  17.4 10.3 %all-to-all-done = f32[16,8,1024]{2,1,0:T(8,128)S(1)} async-done(((f32[16,8,1024]{2,1,0:T(8,128)}), f32[16,8,1024]{2,1,0:T(8,128)S(1)}, u32[]{:S(2)}, u32[]{:S(2)}) %all-to-all-start) | async-done | bytes 524320 | tf_op jit(solution)/shard_map/all_to_all | solution.py:27
  28.0 1.1 convolution_add_fusion.1
  29.0 3.7 %all-gather = f32[16,384]{1,0:T(8,128)S(1)} all-gather(f32[8,384]{1,0:T(8,128)S(1)} %convolution_add_fusion.1), channel_id=2, replica_groups=mesh['z'=16,'c'=2,'x'=4,'y'=4] {'c'}, dimensions={0}, use_global_device_ids=true | all-gather | bytes 36864 | tf_op jit(solution)/shard_map/all_gather | solution.py:54
  32.7 30.5 %all_to_all.25 = f32[16,8,384]{2,1,0:T(8,128)S(1)} all-to-all(f32[16,8,384]{2,1,0:T(8,128)S(1)} %broadcast_in_dim.65), channel_id=1, replica_groups=mesh['z'=16,'c'=2,'x'=4,'y'=4] {'z'}, dimensions={0} | all-to-all | bytes 393216 | tf_op jit(solution)/shard_map/all_to_all | solution.py:27
  64.5 1.0 broadcast_in_dim.66
  65.5 4.3 %all-to-all-start.2 = ((f32[16,8,1536]{2,1,0:T(8,128)}), f32[16,8,1536]{2,1,0:T(8,128)}, u32[]{:S(2)}, u32[]{:S(2)}) async-start(f32[16,8,1536]{2,1,0:T(8,128)} %broadcast_in_dim.66), calls=%async_computation.2 | async-start | bytes 1572864 | tf_op jit(solution)/shard_map/all_to_all | solution.py:27
  69.9 1.1 dynamic-slice_select_fusion
  71.1 11.4 %all-to-all-done.2 = f32[16,8,1536]{2,1,0:T(8,128)} async-done(((f32[16,8,1536]{2,1,0:T(8,128)}), f32[16,8,1536]{2,1,0:T(8,128)}, u32[]{:S(2)}, u32[]{:S(2)}) %all-to-all-start.2) | async-done | bytes 786464 | tf_op jit(solution)/shard_map/all_to_all | solution.py:27
  82.6 1.2 reduce_sum.57
  84.4 4.1 %all-gather.1 = f32[16,768]{1,0:T(8,128)S(1)} all-gather(f32[8,768]{1,0:T(8,128)S(1)} %fusion.22), channel_id=3, replica_groups=mesh['z'=16,'c'=2,'x'=4,'y'=4] {'c'}, dimensions={0}, use_global_device_ids=true | all-gather | bytes 73728 | tf_op jit(solution)/shard_map/all_gather | solution.py:78
  89.2 5.5 %all-to-all-start.3 = ((f32[16,8,384]{2,1,0:T(8,128)}), f32[16,8,384]{2,1,0:T(8,128)S(1)}, u32[]{:S(2)}, u32[]{:S(2)}) async-start(f32[16,8,384]{2,1,0:T(8,128)} %broadcast_in_dim.73), calls=%async_computation.3 | async-start | bytes 393216 | tf_op jit(solution)/shard_map/all_to_all | solution.py:27
  94.8 0.7 cholesky.17
  97.6 13.2 %all-to-all-done.3 = f32[16,8,384]{2,1,0:T(8,128)S(1)} async-done(((f32[16,8,384]{2,1,0:T(8,128)}), f32[16,8,384]{2,1,0:T(8,128)S(1)}, u32[]{:S(2)}, u32[]{:S(2)}) %all-to-all-start.3) | async-done | bytes 196640 | tf_op jit(solution)/shard_map/all_to_all | solution.py:27
  111.0 0.8 broadcast_in_dim.74
  111.8 4.6 %all-to-all-start.4 = ((f32[32,8,384]{2,1,0:T(8,128)}), f32[32,8,384]{2,1,0:T(8,128)S(1)}, u32[]{:S(2)}, u32[]{:S(2)}) async-start(f32[32,8,384]{2,1,0:T(8,128)} %broadcast_in_dim.74), calls=%async_computation.4 | async-start | bytes 786432 | tf_op jit(solution)/shard_map/all_to_all | solution.py:27
  116.5 10.5 %all-to-all-done.4 = f32[32,8,384]{2,1,0:T(8,128)S(1)} async-done(((f32[32,8,384]{2,1,0:T(8,128)}), f32[32,8,384]{2,1,0:T(8,128)S(1)}, u32[]{:S(2)}, u32[]{:S(2)}) %all-to-all-start.4) | async-done | bytes 393248 | tf_op jit(solution)/shard_map/all_to_all | solution.py:27
  127.0 1.5 multiply_add_fusion
  128.6 55.7 %all-reduce.3.cloned.1.call-done = bf16[384,1024]{1,0:T(8,128)(2,1)} async-done(((bf16[384,1024]{1,0:T(8,128)(2,1)}), bf16[384,1024]{1,0:T(8,128)(2,1)}) %all-reduce.3.cloned.1.call-update) | async-done | bytes 786448 | tf_op jit(solution)/shard_map/psum | solution.py:45
  184.3 2.5 %fusion = f32[384,384]{1,0:T(8,128)} fusion(f32[384,384]{1,0:T(8,128)S(1)} %get-tuple-element.16, f32[384,384]{1,0:T(8,128)S(1)} %copy-done.2, bf16[384,1024]{1,0:T(8,128)(2,1)} %all-reduce.3.cloned.1.call-done, bf16[1024,384]{1,0:T(8,128)(2,1)S(1)} %copy-done), kind=kOutput, calls=%fused_computation.1 | convolution fusion | flops 302284800 | bytes 3342336 | tf_op jit(solution)/shard_map/dot_general | solution.py:87
  186.8 0.7 copy.23
  (45 shorter events, 5.5 us)
Async XLA Ops:
  7.2 20.6 %copy-start = (bf16[1024,384]{1,0:T(8,128)(2,1)S(1)}, bf16[1024,384]{1,0:T(8,128)(2,1)}, u32[]{:S(2)}) copy-start(bf16[1024,384]{1,0:T(8,128)(2,1)} %param.5) | copy-start | bytes 2359300
  9.7 18.2 %copy-start.2 = (f32[384,384]{1,0:T(8,128)S(1)}, f32[384,384]{1,0:T(8,128)}, u32[]{:S(2)}) copy-start(f32[384,384]{1,0:T(8,128)} %param.7) | copy-start | bytes 1769476
  10.6 17.1 %all-to-all-start = ((f32[16,8,1024]{2,1,0:T(8,128)}), f32[16,8,1024]{2,1,0:T(8,128)S(1)}, u32[]{:S(2)}, u32[]{:S(2)}) async-start(f32[16,8,1024]{2,1,0:T(8,128)} %broadcast_in_dim.64), calls=%async_computation | async-start | bytes 1048576 | tf_op jit(solution)/shard_map/all_to_all | solution.py:27
  64.1 5.8 %copy-start.1 = (bf16[768,1024]{1,0:T(8,128)(2,1)S(1)}, bf16[768,1024]{1,0:T(8,128)(2,1)}, u32[]{:S(2)}) copy-start(bf16[768,1024]{1,0:T(8,128)(2,1)} %param.6) | copy-start | bytes 4718596
  65.5 17.1 %all-to-all-start.2 = ((f32[16,8,1536]{2,1,0:T(8,128)}), f32[16,8,1536]{2,1,0:T(8,128)}, u32[]{:S(2)}, u32[]{:S(2)}) async-start(f32[16,8,1536]{2,1,0:T(8,128)} %broadcast_in_dim.66), calls=%async_computation.2 | async-start | bytes 1572864 | tf_op jit(solution)/shard_map/all_to_all | solution.py:27
  69.8 114.5 %all-reduce.3.cloned.1.call-start = ((), (), s32[]{:S(2)}) async-start(), calls=%async_computation.5 | async-start | bytes 1572864 | tf_op jit(solution)/shard_map/psum | solution.py:45
  84.4 42.6 %copy-start.3 = (f32[384,384]{1,0:T(8,128)S(1)}, f32[384,384]{1,0:T(8,128)}, u32[]{:S(2)}) copy-start(f32[384,384]{1,0:T(8,128)} %param.8) | copy-start | bytes 1769476
  89.2 21.6 %all-to-all-start.3 = ((f32[16,8,384]{2,1,0:T(8,128)}), f32[16,8,384]{2,1,0:T(8,128)S(1)}, u32[]{:S(2)}, u32[]{:S(2)}) async-start(f32[16,8,384]{2,1,0:T(8,128)} %broadcast_in_dim.73), calls=%async_computation.3 | async-start | bytes 393216 | tf_op jit(solution)/shard_map/all_to_all | solution.py:27
  111.8 15.3 %all-to-all-start.4 = ((f32[32,8,384]{2,1,0:T(8,128)}), f32[32,8,384]{2,1,0:T(8,128)S(1)}, u32[]{:S(2)}, u32[]{:S(2)}) async-start(f32[32,8,384]{2,1,0:T(8,128)} %broadcast_in_dim.74), calls=%async_computation.4 | async-start | bytes 786432 | tf_op jit(solution)/shard_map/all_to_all | solution.py:27
Sparse Core Ops, SparseCore 0:
  73.9 110.3 all-reduce.2

commit v2 on v1

--- a/solution.py
+++ b/solution.py
@@ -1,5 +1,6 @@
 import jax
 import jax.numpy as jnp
+import numpy as np
 from jax import lax
 from jax.sharding import Mesh, PartitionSpec as P
 
@@ -27,6 +28,33 @@
     return lax.all_to_all(jnp.broadcast_to(x[None], (count,) + x.shape), axes, 0, 0)
 
 
+def tie(x, after):
+    return lax.optimization_barrier((x, after))[0]
+
+
+def tree_rounds(nz, nc, nx, ny):
+    def device(z, c, x, y):
+        return ((z * nc + c) * nx + x) * ny + y
+
+    rounds = []
+    known = {c: [(0, 0)] for c in range(nc)}
+    steps = ((nx // 2, 0), (0, ny // 2), (nx // 4, 0), (0, ny // 4))
+    for step in steps:
+        pairs = []
+        for c in range(nc):
+            dx, dy = step if c == 0 else (step[1], step[0])
+            fresh = [((a + dx) % nx, (b + dy) % ny) for a, b in known[c]]
+            for z in range(nz):
+                ox, oy = z // ny, z % ny
+                for (a, b), (e, f) in zip(known[c], fresh):
+                    source = device(z, c, (ox + a) % nx, (oy + b) % ny)
+                    target = device(z, c, (ox + e) % nx, (oy + f) % ny)
+                    pairs.append((source, target))
+            known[c] = known[c] + fresh
+        rounds.append(pairs)
+    return rounds
+
+
 def per_device(activations, hidden, feedback, momentum, q_start):
     nz, nc, nx, ny = (lax.axis_size(a) for a in ("z", "c", "x", "y"))
     plane = ("x", "y")
@@ -40,18 +68,28 @@
     width = activations.shape[1]
     own_start = replica * cols_dp
     root_dev = own_start // cols_mp
-    piece = lax.dynamic_slice_in_dim(hidden, own_start % cols_mp, cols_dp, 0)
-    piece = jnp.where(shard == root_dev, piece, jnp.zeros_like(piece))
-    own_hidden = lax.psum(piece, plane)
+    rounds = tree_rounds(nz, nc, nx, ny)
+    me = lax.axis_index(("z", "c", "x", "y"))
+
+    def send(held, k):
+        got = lax.ppermute(held, ("z", "c", "x", "y"), rounds[k])
+        takers = np.zeros(nz * nc * nx * ny, np.bool_)
+        takers[[t for _, t in rounds[k]]] = True
+        return got, jnp.asarray(takers)[me]
 
     q_rows = q_start.T
     q_block = lax.dynamic_slice_in_dim(q_rows, shard * cols_mp, cols_mp, 1)
     q_owned = lax.dynamic_slice_in_dim(q_rows, own_start, cols_dp, 1)
     token_part = thin_dot(q_block, hidden, ((1,), (0,)))
+    hid_late = tie(hidden, token_part)
+    held = lax.dynamic_slice_in_dim(hid_late, core * cols_dp, cols_dp, 0)
+    got, takes = send(held, 0)
     token_q = copies(token_part, plane, n_mp).sum(0)
     p_err = jnp.dot(q_owned, feedback, precision=high)
     p_part = thin_dot(token_q, activations, ((1,), (0,))) + p_err
     p_pair = lax.all_gather(p_part, "c").sum(0)
+    held = jnp.where(takes, tie(got, p_pair), held)
+    got, takes = send(held, 1)
     p_sum = copies(p_pair, "z", nz).sum(0)
 
     u_part = thin_dot(p_sum, activations, ((1,), (1,)))
@@ -62,6 +100,8 @@
     packed = jnp.concatenate(
         [u_part, err_part, jnp.pad(gram_part, ((0, 0), (0, 128 - rank)))], 1
     )
+    held = jnp.where(takes, tie(got, packed), held)
+    got, takes = send(held, 2)
     packed = copies(packed, plane, n_mp).sum(0)
     u = packed[:, :toks]
     err = packed[:, toks : toks + cols_dp]
@@ -77,15 +117,19 @@
     hid = hid.reshape(rank, cols_mp)
     half = lax.all_gather(hid, "c").sum(0)
     half = lax.dynamic_slice_in_dim(half, core * cols_dp, cols_dp, 1)
+    held = jnp.where(takes, tie(got, half), held)
+    got, takes = send(held, 3)
     half = copies(half, "z", nz).sum(0)
     block = jnp.dot(inverse, half, precision=high) / n_dp
+    held = jnp.where(takes, tie(got, block), held)
+    own_grad = jnp.dot(held, activations, preferred_element_type=jnp.float32)
+    base = own_grad + feedback
     blocks = copies(block, ("x", "y", "c"), n_dp)
     q_next = jnp.transpose(blocks, (1, 0, 2)).reshape(rank, -1).T
     q_mine = lax.dynamic_index_in_dim(blocks, replica, 0, keepdims=False)
     ortho = jnp.dot(inverse, p_sum, precision=high)
     approx = lax.dot_general(q_mine, ortho, (((0,), (0,)), ((), ())), precision=high)
-    own_grad = jnp.dot(own_hidden, activations, preferred_element_type=jnp.float32)
-    new_feedback = own_grad + feedback - approx
+    new_feedback = base - approx
     new_momentum = decay_rate * momentum + approx
     return (new_feedback, new_momentum, q_next)
 

time: 196 us -> 127 us (0.65)
  waiting for transfers between devices: 101 us -> 46.6 us
  blocking collectives: 38.3 us -> 7.62 us
  starting transfers between devices: 21.2 us -> 42.5 us
  between operations: 14.3 us -> 0.91 us
  other arithmetic: 6.04 us -> 11.5 us
  local copies, waits for them, and re-layouts: 4.28 us -> 8.33 us
    psum x1 -> x0, waiting for transfers between devices: 55.7 us -> none  [per_device(): own_hidden = lax.psum(piece, plane)]
    all_to_all x1 -> x0, blocking collectives: 30.5 us -> none  [copies(): lax.all_to_all(jnp.broadcast_to(x[None], (count,) + x.shape), axes, 0, 0)]
    all_to_all x4 -> x5, starting transfers between devices: 21.2 us -> 35.8 us  [copies(): lax.all_to_all(jnp.broadcast_to(x[None], (count,) + x.shape), axes, 0, 0)]
    ppermute x0 -> x4, starting transfers between devices: none -> 6.7 us  [send(): got = lax.ppermute(held, ('z', 'c', 'x', 'y'), rounds[k])]
    select_n x1 -> x3, other arithmetic: 1.14 us -> 6.58 us  [the longest x1 2.78 us: per_device(): held = jnp.where(takes, tie(got, packed), held)]
    dynamic_slice x0 -> x5, local copies, waits for them, and re-layouts: none -> 3.32 us  [the longest x4 2.38 us: send(): return (got, jnp.asarray(takers)[me])]
    all_to_all x4 -> x5, waiting for transfers between devices: 45.5 us -> 46.6 us  [copies(): lax.all_to_all(jnp.broadcast_to(x[None], (count,) + x.shape), axes, 0, 0)]
  transfers between devices with their start and end apart: 5 -> 9, of which waited for: 5 -> 5; matrix products, arithmetic and copies ran while one was open for 5% -> 18% of each run, Pallas kernels for 0% -> 0%
where the time goes in v2:
time: 127 us; the launch traced here: 126 us
  waiting for transfers between devices  46.6 us (37%)
  starting transfers between devices  42.5 us (33%)
  other arithmetic  11.5 us (9%)
  matrix products  8.73 us (7%)
  local copies, waits for them, and re-layouts  8.33 us (7%)
  blocking collectives  7.62 us (6%)
    all_to_all x5, waiting for transfers between devices, copies(): lax.all_to_all(jnp.broadcast_to(x[None], (count,) + x.shape), axes, 0, 0)  46.6 us
    all_to_all x5, starting transfers between devices, copies(): lax.all_to_all(jnp.broadcast_to(x[None], (count,) + x.shape), axes, 0, 0)  35.8 us
    ppermute x4, starting transfers between devices, send(): got = lax.ppermute(held, ('z', 'c', 'x', 'y'), rounds[k])  6.7 us
    broadcast_in_dim x5, local copies, waits for them, and re-layouts, copies(): jnp.broadcast_to(x[None], (count,) + x.shape)  4.02 us
    all_gather x1, blocking collectives, per_device(): half = lax.all_gather(hid, 'c').sum(0)  3.96 us
    all_gather x1, blocking collectives, per_device(): p_pair = lax.all_gather(p_part, 'c').sum(0)  3.67 us
    dot_general x4, matrix products, thin_dot(): lax.dot_general(split_parts(x), wide, (dims, ((), ())), preferred_element...  2.94 us
    select_n x1, other arithmetic, per_device(): held = jnp.where(takes, tie(got, packed), held)  2.78 us
  transfers between devices with their start and end apart: 9, of which 5 were waited for; matrix products, arithmetic and copies ran while one was open for 18% of the time, Pallas kernels for 0%

profile of v2, /device:TPU:33, one launch (start us, length us, event | category | flops | bytes accessed | tf_op | source)
XLA Modules:
  0.0 126.2 jit_solution(3232483875665338600)
XLA Ops:
  1.5 1.8 %fusion.15 = f32[24,1024]{1,0:T(8,128)S(1)} fusion(bf16[768,1024]{1,0:T(8,128)(2,1)} %param.10, bf16[8,768]{1,0:T(8,128)(2,1)S(1)} %get-tuple-element.14, bf16[8,768]{1,0:T(8,128)(2,1)S(1)} %get-tuple-element.15, bf16[8,768]{1,0:T(8,128)(2,1)S(1)} %get-tuple-element.13), kind=kOutput, calls=%fused_computation.33 | convolution fusion | flops 37859328 | bytes 1708032 | tf_op jit(solution)/shard_map/dot_general | solution.py:20
  4.2 6.8 %all-to-all-start = ((f32[16,8,1024]{2,1,0:T(8,128)}), f32[16,8,1024]{2,1,0:T(8,128)S(1)}, u32[]{:S(2)}, u32[]{:S(2)}) async-start(f32[16,8,1024]{2,1,0:T(8,128)} %broadcast_in_dim.60), calls=%async_computation | async-start | bytes 1048576 | tf_op jit(solution)/shard_map/all_to_all | solution.py:28
  11.9 1.7 %collective-permute-start = (bf16[384,1024]{1,0:T(8,128)(2,1)}, bf16[384,1024]{1,0:T(8,128)(2,1)}, u32[]{:S(2)}, u32[]{:S(2)}) collective-permute-start(bf16[384,1024]{1,0:T(8,128)(2,1)} %constant_dynamic-slice_fusion.1), channel_id=1, source_target_pairs={{0,8},{33,41},{66,74},{99,107},{132,140},{165,173},{198,206},{231,... | collective-permute-start | bytes 2359304 | tf_op jit(solution)/shard_map/ppermute | solution.py:75
  13.6 7.6 %all-to-all-done = f32[16,8,1024]{2,1,0:T(8,128)S(1)} async-done(((f32[16,8,1024]{2,1,0:T(8,128)}), f32[16,8,1024]{2,1,0:T(8,128)S(1)}, u32[]{:S(2)}, u32[]{:S(2)}) %all-to-all-start) | async-done | bytes 524320 | tf_op jit(solution)/shard_map/all_to_all | solution.py:28
  21.5 1.1 convolution_add_fusion.1
  22.6 3.7 %all-gather = f32[16,384]{1,0:T(8,128)S(1)} all-gather(f32[8,384]{1,0:T(8,128)S(1)} %convolution_add_fusion.1), channel_id=2, replica_groups=mesh['z'=16,'c'=2,'x'=4,'y'=4] {'c'}, dimensions={0}, use_global_device_ids=true | all-gather | bytes 36864 | tf_op jit(solution)/shard_map/all_gather | solution.py:90
  27.0 14.7 %all-to-all-start.1 = ((f32[16,8,384]{2,1,0:T(8,128)}), f32[16,8,384]{2,1,0:T(8,128)S(1)}, u32[]{:S(2)}, u32[]{:S(2)}) async-start(f32[16,8,384]{2,1,0:T(8,128)} %broadcast_in_dim.61), calls=%async_computation.1 | async-start | bytes 393216 | tf_op jit(solution)/shard_map/all_to_all | solution.py:28
  42.2 1.9 %broadcast_select_fusion = bf16[384,1024]{1,0:T(8,128)(2,1)} fusion(bf16[384,1024]{1,0:T(8,128)(2,1)} %collective-permute-done, pred[]{:T(512)} %bitcast.3, bf16[768,1024]{1,0:T(8,128)(2,1)S(1)} %copy-done.1, s32[]{:T(128)S(6)} %select_n.67), kind=kLoop, calls=%fused_computation.5 | loop fusion | flops 393216 | bytes 2359301 | tf_op jit(solution)/shard_map/jit(_where)/select_n | solution.py:91
  44.1 1.5 %collective-permute-start.1 = (bf16[384,1024]{1,0:T(8,128)(2,1)}, bf16[384,1024]{1,0:T(8,128)(2,1)}, u32[]{:S(2)}, u32[]{:S(2)}) collective-permute-start(bf16[384,1024]{1,0:T(8,128)(2,1)} %broadcast_select_fusion), channel_id=1, source_target_pairs={{0,2},{8,10},{33,35},{41,43},{66,64},{74,72},{99,97},{107,105},{13... | collective-permute-start | bytes 2359304 | tf_op jit(solution)/shard_map/ppermute | solution.py:75
  45.7 12.1 %all-to-all-done.1 = f32[16,8,384]{2,1,0:T(8,128)S(1)} async-done(((f32[16,8,384]{2,1,0:T(8,128)}), f32[16,8,384]{2,1,0:T(8,128)S(1)}, u32[]{:S(2)}, u32[]{:S(2)}) %all-to-all-start.1) | async-done | bytes 196640 | tf_op jit(solution)/shard_map/all_to_all | solution.py:28
  59.9 4.3 %all-to-all-start.2 = ((f32[16,8,1536]{2,1,0:T(8,128)}), f32[16,8,1536]{2,1,0:T(8,128)}, u32[]{:S(2)}, u32[]{:S(2)}) async-start(f32[16,8,1536]{2,1,0:T(8,128)} %broadcast_in_dim.62), calls=%async_computation.2 | async-start | bytes 1572864 | tf_op jit(solution)/shard_map/all_to_all | solution.py:28
  65.6 2.8 %broadcast_select_fusion.1 = bf16[384,1024]{1,0:T(8,128)(2,1)} fusion(bf16[384,1024]{1,0:T(8,128)(2,1)} %collective-permute-done.1, bf16[384,1024]{1,0:T(8,128)(2,1)} %broadcast_select_fusion, pred[]{:T(512)} %bitcast.2), kind=kLoop, calls=%fused_computation.6 | loop fusion | flops 393216 | bytes 2359297 | tf_op jit(solution)/shard_map/jit(_where)/select_n | solution.py:103
  68.3 1.3 %collective-permute-start.2 = (bf16[384,1024]{1,0:T(8,128)(2,1)}, bf16[384,1024]{1,0:T(8,128)(2,1)}, u32[]{:S(2)}, u32[]{:S(2)}) collective-permute-start(bf16[384,1024]{1,0:T(8,128)(2,1)} %broadcast_select_fusion.1), channel_id=1, source_target_pairs={{0,4},{8,12},{2,6},{10,14},{33,37},{41,45},{35,39},{43,47},{66,70}... | collective-permute-start | bytes 2359304 | tf_op jit(solution)/shard_map/ppermute | solution.py:75
  69.6 7.4 %all-to-all-done.2 = f32[16,8,1536]{2,1,0:T(8,128)} async-done(((f32[16,8,1536]{2,1,0:T(8,128)}), f32[16,8,1536]{2,1,0:T(8,128)}, u32[]{:S(2)}, u32[]{:S(2)}) %all-to-all-start.2) | async-done | bytes 786464 | tf_op jit(solution)/shard_map/all_to_all | solution.py:28
  77.1 1.2 reduce_sum.57
  78.9 4.0 %all-gather.1 = f32[16,768]{1,0:T(8,128)S(1)} all-gather(f32[8,768]{1,0:T(8,128)S(1)} %fusion.24), channel_id=3, replica_groups=mesh['z'=16,'c'=2,'x'=4,'y'=4] {'c'}, dimensions={0}, use_global_device_ids=true | all-gather | bytes 73728 | tf_op jit(solution)/shard_map/all_gather | solution.py:118
  84.3 5.5 %all-to-all-start.3 = ((f32[16,8,384]{2,1,0:T(8,128)}), f32[16,8,384]{2,1,0:T(8,128)S(1)}, u32[]{:S(2)}, u32[]{:S(2)}) async-start(f32[16,8,384]{2,1,0:T(8,128)} %broadcast_in_dim.69), calls=%async_computation.3 | async-start | bytes 393216 | tf_op jit(solution)/shard_map/all_to_all | solution.py:28
  91.9 1.9 %broadcast_select_fusion.2 = bf16[384,1024]{1,0:T(8,128)(2,1)S(1)} fusion(bf16[384,1024]{1,0:T(8,128)(2,1)} %collective-permute-done.2, bf16[384,1024]{1,0:T(8,128)(2,1)} %broadcast_select_fusion.1, pred[]{:T(512)} %bitcast.1), kind=kLoop, calls=%fused_computation.7 | loop fusion | flops 393216 | bytes 2359297 | tf_op jit(solution)/shard_map/jit(_where)/select_n | solution.py:120
  93.9 2.2 %collective-permute-start.3 = (bf16[384,1024]{1,0:T(8,128)(2,1)S(1)}, bf16[384,1024]{1,0:T(8,128)(2,1)}, u32[]{:S(2)}, u32[]{:S(2)}) collective-permute-start(bf16[384,1024]{1,0:T(8,128)(2,1)S(1)} %broadcast_select_fusion.2), channel_id=1, source_target_pairs={{0,1},{8,9},{2,3},{10,11},{4,5},{12,13},{6,7},{14,15},{33,34},{41,... | collective-permute-start | bytes 2359304 | tf_op jit(solution)/shard_map/ppermute | solution.py:75
  96.1 9.8 %all-to-all-done.3 = f32[16,8,384]{2,1,0:T(8,128)S(1)} async-done(((f32[16,8,384]{2,1,0:T(8,128)}), f32[16,8,384]{2,1,0:T(8,128)S(1)}, u32[]{:S(2)}, u32[]{:S(2)}) %all-to-all-start.3) | async-done | bytes 196640 | tf_op jit(solution)/shard_map/all_to_all | solution.py:28
  106.8 4.6 %all-to-all-start.4 = ((f32[32,8,384]{2,1,0:T(8,128)}), f32[32,8,384]{2,1,0:T(8,128)S(1)}, u32[]{:S(2)}, u32[]{:S(2)}) async-start(f32[32,8,384]{2,1,0:T(8,128)} %broadcast_in_dim.70), calls=%async_computation.4 | async-start | bytes 786432 | tf_op jit(solution)/shard_map/all_to_all | solution.py:28
  112.2 9.7 %all-to-all-done.4 = f32[32,8,384]{2,1,0:T(8,128)S(1)} async-done(((f32[32,8,384]{2,1,0:T(8,128)}), f32[32,8,384]{2,1,0:T(8,128)S(1)}, u32[]{:S(2)}, u32[]{:S(2)}) %all-to-all-start.4) | async-done | bytes 393248 | tf_op jit(solution)/shard_map/all_to_all | solution.py:28
  121.8 1.5 %multiply_add_fusion = (f32[384,384]{1,0:T(8,128)}, f32[384,384]{1,0:T(8,128)S(1)}) fusion(f32[384,384]{1,0:T(8,128)S(1)} %copy-done.3, f32[8,384]{1,0:T(8,128)S(1)} %fusion.48, f32[32,8,384]{2,1,0:T(8,128)S(1)} %all-to-all-done.4, s32[]{:T(128)S(6)} %select_n.76), kind=kOutput, calls=%fused_computation.9 | convolution fusion | flops 14450688 | bytes 1794052 | tf_op jit(solution)/shard_map/dot_general | solution.py:131
  123.4 2.0 %fusion = f32[384,384]{1,0:T(8,128)} fusion(f32[384,384]{1,0:T(8,128)S(1)} %get-tuple-element.26, f32[384,384]{1,0:T(8,128)S(1)} %copy-done.2, bf16[1024,384]{1,0:T(8,128)(2,1)S(1)} %copy-done, bf16[384,1024]{1,0:T(8,128)(2,1)} %collective-permute-done.3, bf16[384,1024]{1,0:T(8,128)(2,1)S(1)} %broadcast_select_fusion.2, pred[]{:T(512)} %bitcast), kind=kOutput, calls=%fused_computation.1 | convolution fusion | flops 302678016 | bytes 4128769 | tf_op jit(solution)/shard_map/dot_general | solution.py:125
  (66 shorter events, 14.3 us)
Async XLA Ops:
  0.6 20.7 %copy-start = (bf16[1024,384]{1,0:T(8,128)(2,1)S(1)}, bf16[1024,384]{1,0:T(8,128)(2,1)}, u32[]{:S(2)}) copy-start(bf16[1024,384]{1,0:T(8,128)(2,1)} %param.9) | copy-start | bytes 2359300
  1.5 9.5 %copy-start.1 = (bf16[768,1024]{1,0:T(8,128)(2,1)S(1)}, bf16[768,1024]{1,0:T(8,128)(2,1)}, u32[]{:S(2)}) copy-start(bf16[768,1024]{1,0:T(8,128)(2,1)} %param.10) | copy-start | bytes 4718596
  4.2 17.1 %all-to-all-start = ((f32[16,8,1024]{2,1,0:T(8,128)}), f32[16,8,1024]{2,1,0:T(8,128)S(1)}, u32[]{:S(2)}, u32[]{:S(2)}) async-start(f32[16,8,1024]{2,1,0:T(8,128)} %broadcast_in_dim.60), calls=%async_computation | async-start | bytes 1048576 | tf_op jit(solution)/shard_map/all_to_all | solution.py:28
  10.9 10.6 %copy-start.2 = (f32[384,384]{1,0:T(8,128)S(1)}, f32[384,384]{1,0:T(8,128)}, u32[]{:S(2)}) copy-start(f32[384,384]{1,0:T(8,128)} %param.11) | copy-start | bytes 1769476
  11.9 29.7 %copy-start.7 = (pred[512]{0:T(512)(128)(4,1)S(1)}, pred[512]{0:T(512)(128)(4,1)}, u32[]{:S(2)}) copy-start(pred[512]{0:T(512)(128)(4,1)} %constant.104.clone) | copy-start | bytes 1540
  11.9 30.3 %collective-permute-start = (bf16[384,1024]{1,0:T(8,128)(2,1)}, bf16[384,1024]{1,0:T(8,128)(2,1)}, u32[]{:S(2)}, u32[]{:S(2)}) collective-permute-start(bf16[384,1024]{1,0:T(8,128)(2,1)} %constant_dynamic-slice_fusion.1), channel_id=1, source_target_pairs={{0,8},{33,41},{66,74},{99,107},{132,140},{165,173},{198,206},{231,... | collective-permute-start | bytes 2359304 | tf_op jit(solution)/shard_map/ppermute | solution.py:75
  27.0 30.7 %all-to-all-start.1 = ((f32[16,8,384]{2,1,0:T(8,128)}), f32[16,8,384]{2,1,0:T(8,128)S(1)}, u32[]{:S(2)}, u32[]{:S(2)}) async-start(f32[16,8,384]{2,1,0:T(8,128)} %broadcast_in_dim.61), calls=%async_computation.1 | async-start | bytes 393216 | tf_op jit(solution)/shard_map/all_to_all | solution.py:28
  44.1 21.4 %collective-permute-start.1 = (bf16[384,1024]{1,0:T(8,128)(2,1)}, bf16[384,1024]{1,0:T(8,128)(2,1)}, u32[]{:S(2)}, u32[]{:S(2)}) collective-permute-start(bf16[384,1024]{1,0:T(8,128)(2,1)} %broadcast_select_fusion), channel_id=1, source_target_pairs={{0,2},{8,10},{33,35},{41,43},{66,64},{74,72},{99,97},{107,105},{13... | collective-permute-start | bytes 2359304 | tf_op jit(solution)/shard_map/ppermute | solution.py:75
  58.4 5.9 %copy-start.6 = (pred[512]{0:T(512)(128)(4,1)S(1)}, pred[512]{0:T(512)(128)(4,1)}, u32[]{:S(2)}) copy-start(pred[512]{0:T(512)(128)(4,1)} %constant.106.clone) | copy-start | bytes 1540
  58.4 6.5 %copy-start.5 = (pred[512]{0:T(512)(128)(4,1)S(1)}, pred[512]{0:T(512)(128)(4,1)}, u32[]{:S(2)}) copy-start(pred[512]{0:T(512)(128)(4,1)} %constant.105.clone) | copy-start | bytes 1540
  59.9 17.1 %all-to-all-start.2 = ((f32[16,8,1536]{2,1,0:T(8,128)}), f32[16,8,1536]{2,1,0:T(8,128)}, u32[]{:S(2)}, u32[]{:S(2)}) async-start(f32[16,8,1536]{2,1,0:T(8,128)} %broadcast_in_dim.62), calls=%async_computation.2 | async-start | bytes 1572864 | tf_op jit(solution)/shard_map/all_to_all | solution.py:28
  68.3 23.6 %collective-permute-start.2 = (bf16[384,1024]{1,0:T(8,128)(2,1)}, bf16[384,1024]{1,0:T(8,128)(2,1)}, u32[]{:S(2)}, u32[]{:S(2)}) collective-permute-start(bf16[384,1024]{1,0:T(8,128)(2,1)} %broadcast_select_fusion.1), channel_id=1, source_target_pairs={{0,4},{8,12},{2,6},{10,14},{33,37},{41,45},{35,39},{43,47},{66,70}... | collective-permute-start | bytes 2359304 | tf_op jit(solution)/shard_map/ppermute | solution.py:75
  84.3 21.6 %all-to-all-start.3 = ((f32[16,8,384]{2,1,0:T(8,128)}), f32[16,8,384]{2,1,0:T(8,128)S(1)}, u32[]{:S(2)}, u32[]{:S(2)}) async-start(f32[16,8,384]{2,1,0:T(8,128)} %broadcast_in_dim.69), calls=%async_computation.3 | async-start | bytes 393216 | tf_op jit(solution)/shard_map/all_to_all | solution.py:28
  91.9 19.5 %copy-start.4 = (pred[512]{0:T(512)(128)(4,1)S(1)}, pred[512]{0:T(512)(128)(4,1)}, u32[]{:S(2)}) copy-start(pred[512]{0:T(512)(128)(4,1)} %constant.107.clone) | copy-start | bytes 1540
  91.9 29.9 %copy-start.3 = (f32[384,384]{1,0:T(8,128)S(1)}, f32[384,384]{1,0:T(8,128)}, u32[]{:S(2)}) copy-start(f32[384,384]{1,0:T(8,128)} %param.12) | copy-start | bytes 1769476
  93.9 29.5 %collective-permute-start.3 = (bf16[384,1024]{1,0:T(8,128)(2,1)S(1)}, bf16[384,1024]{1,0:T(8,128)(2,1)}, u32[]{:S(2)}, u32[]{:S(2)}) collective-permute-start(bf16[384,1024]{1,0:T(8,128)(2,1)S(1)} %broadcast_select_fusion.2), channel_id=1, source_target_pairs={{0,1},{8,9},{2,3},{10,11},{4,5},{12,13},{6,7},{14,15},{33,34},{41,... | collective-permute-start | bytes 2359304 | tf_op jit(solution)/shard_map/ppermute | solution.py:75
  106.8 15.0 %all-to-all-start.4 = ((f32[32,8,384]{2,1,0:T(8,128)}), f32[32,8,384]{2,1,0:T(8,128)S(1)}, u32[]{:S(2)}, u32[]{:S(2)}) async-start(f32[32,8,384]{2,1,0:T(8,128)} %broadcast_in_dim.70), calls=%async_computation.4 | async-start | bytes 786432 | tf_op jit(solution)/shard_map/all_to_all | solution.py:28

commit v3 on v2

--- a/solution.py
+++ b/solution.py
@@ -1,6 +1,5 @@
 import jax
 import jax.numpy as jnp
-import numpy as np
 from jax import lax
 from jax.sharding import Mesh, PartitionSpec as P
 
@@ -69,13 +68,20 @@
     own_start = replica * cols_dp
     root_dev = own_start // cols_mp
     rounds = tree_rounds(nz, nc, nx, ny)
-    me = lax.axis_index(("z", "c", "x", "y"))
+    off_x = (lax.axis_index("x") - z // ny) % nx
+    off_y = (lax.axis_index("y") - z % ny) % ny
+    first = jnp.where(core == 0, off_x, off_y)
+    second = jnp.where(core == 0, off_y, off_x)
+    turn = jnp.where(first >= 2, 0, -1)
+    turn = jnp.where(second >= 2, 1, turn)
+    turn = jnp.where(first % 2 == 1, 2, turn)
+    turn = jnp.where(second % 2 == 1, 3, turn)
 
     def send(held, k):
-        got = lax.ppermute(held, ("z", "c", "x", "y"), rounds[k])
-        takers = np.zeros(nz * nc * nx * ny, np.bool_)
-        takers[[t for _, t in rounds[k]]] = True
-        return got, jnp.asarray(takers)[me]
+        return lax.ppermute(held, ("z", "c", "x", "y"), rounds[k])
+
+    def take(held, got, k):
+        return jnp.where(turn == k, got, held)
 
     q_rows = q_start.T
     q_block = lax.dynamic_slice_in_dim(q_rows, shard * cols_mp, cols_mp, 1)
@@ -83,14 +89,19 @@
     token_part = thin_dot(q_block, hidden, ((1,), (0,)))
     hid_late = tie(hidden, token_part)
     held = lax.dynamic_slice_in_dim(hid_late, core * cols_dp, cols_dp, 0)
-    got, takes = send(held, 0)
+    got = send(held, 0)
     token_q = copies(token_part, plane, n_mp).sum(0)
     p_err = jnp.dot(q_owned, feedback, precision=high)
     p_part = thin_dot(token_q, activations, ((1,), (0,))) + p_err
     p_pair = lax.all_gather(p_part, "c").sum(0)
-    held = jnp.where(takes, tie(got, p_pair), held)
-    got, takes = send(held, 1)
-    p_sum = copies(p_pair, "z", nz).sum(0)
+    held = take(held, tie(got, p_pair), 0)
+    got = send(held, 1)
+    part = rank // nc
+    p_pair = lax.dynamic_slice_in_dim(p_pair, core * part, part, 0)
+    p_half = copies(p_pair, "z", nz).sum(0)
+    held = take(held, got, 1)
+    got = send(held, 2)
+    p_sum = lax.all_gather(p_half, "c", tiled=True)
 
     u_part = thin_dot(p_sum, activations, ((1,), (1,)))
     err_part = lax.dot_general(
@@ -100,8 +111,6 @@
     packed = jnp.concatenate(
         [u_part, err_part, jnp.pad(gram_part, ((0, 0), (0, 128 - rank)))], 1
     )
-    held = jnp.where(takes, tie(got, packed), held)
-    got, takes = send(held, 2)
     packed = copies(packed, plane, n_mp).sum(0)
     u = packed[:, :toks]
     err = packed[:, toks : toks + cols_dp]
@@ -117,13 +126,13 @@
     hid = hid.reshape(rank, cols_mp)
     half = lax.all_gather(hid, "c").sum(0)
     half = lax.dynamic_slice_in_dim(half, core * cols_dp, cols_dp, 1)
-    held = jnp.where(takes, tie(got, half), held)
-    got, takes = send(held, 3)
+    held = take(held, tie(got, half), 2)
+    got = send(held, 3)
     half = copies(half, "z", nz).sum(0)
     block = jnp.dot(inverse, half, precision=high) / n_dp
-    held = jnp.where(takes, tie(got, block), held)
+    held = take(held, tie(got, block), 3)
     own_grad = jnp.dot(held, activations, preferred_element_type=jnp.float32)
-    base = own_grad + feedback
+    base = lax.optimization_barrier(own_grad + feedback)
     blocks = copies(block, ("x", "y", "c"), n_dp)
     q_next = jnp.transpose(blocks, (1, 0, 2)).reshape(rank, -1).T
     q_mine = lax.dynamic_index_in_dim(blocks, replica, 0, keepdims=False)

time: 127 us -> 125 us (0.984)
  blocking collectives: 7.62 us -> 11.2 us
  other arithmetic: 11.5 us -> 9.4 us
  local copies, waits for them, and re-layouts: 8.33 us -> 6.36 us
  starting transfers between devices: 42.5 us -> 40.8 us
    all_gather x0 -> x1, blocking collectives: none -> 3.83 us  [per_device(): p_sum = lax.all_gather(p_half, 'c', tiled=True)]
    dynamic_slice x4 -> x1, local copies, waits for them, and re-layouts: 2.38 us -> 0.01 us  [per_device(): p_pair = lax.dynamic_slice_in_dim(p_pair, core * part, part, 0)]
    select_n x3, other arithmetic: 6.58 us -> 4.55 us  [take(): return jnp.where(turn == k, got, held)]
    all_to_all x5, starting transfers between devices: 35.8 us -> 34.2 us  [copies(): lax.all_to_all(jnp.broadcast_to(x[None], (count,) + x.shape), axes, 0, 0)]
    dot_general x1, matrix products: 2.03 us -> 0.59 us  [per_device(): own_grad = jnp.dot(held, activations, preferred_element_type=jnp.float32)]
  transfers between devices with their start and end apart: 9 -> 9, of which waited for: 5 -> 5; matrix products, arithmetic and copies ran while one was open for 18% -> 13% of each run, Pallas kernels for 0% -> 0%
where the time goes in v3:
time: 125 us; the launch traced here: 124 us
  waiting for transfers between devices  47.6 us (38%)
  starting transfers between devices  40.8 us (33%)
  blocking collectives  11.2 us (9%)
  other arithmetic  9.4 us (8%)
  matrix products  7.55 us (6%)
  local copies, waits for them, and re-layouts  6.36 us (5%)
    all_to_all x5, waiting for transfers between devices, copies(): lax.all_to_all(jnp.broadcast_to(x[None], (count,) + x.shape), axes, 0, 0)  47.6 us
    all_to_all x5, starting transfers between devices, copies(): lax.all_to_all(jnp.broadcast_to(x[None], (count,) + x.shape), axes, 0, 0)  34.2 us
    ppermute x4, starting transfers between devices, send(): return lax.ppermute(held, ('z', 'c', 'x', 'y'), rounds[k])  6.54 us
    select_n x3, other arithmetic, take(): return jnp.where(turn == k, got, held)  4.55 us
    broadcast_in_dim x5, local copies, waits for them, and re-layouts, copies(): jnp.broadcast_to(x[None], (count,) + x.shape)  3.97 us
    all_gather x1, blocking collectives, per_device(): p_sum = lax.all_gather(p_half, 'c', tiled=True)  3.83 us
    all_gather x1, blocking collectives, per_device(): half = lax.all_gather(hid, 'c').sum(0)  3.73 us
    all_gather x1, blocking collectives, per_device(): p_pair = lax.all_gather(p_part, 'c').sum(0)  3.67 us
  transfers between devices with their start and end apart: 9, of which 5 were waited for; matrix products, arithmetic and copies ran while one was open for 13% of the time, Pallas kernels for 0%

profile of v3, /device:TPU:33, one launch (start us, length us, event | category | flops | bytes accessed | tf_op | source)
XLA Modules:
  0.0 123.8 jit_solution(5918067016278814747)
XLA Ops:
  1.5 1.8 %fusion.14 = f32[24,1024]{1,0:T(8,128)S(1)} fusion(bf16[768,1024]{1,0:T(8,128)(2,1)} %param.6, bf16[8,768]{1,0:T(8,128)(2,1)S(1)} %get-tuple-element.14, bf16[8,768]{1,0:T(8,128)(2,1)S(1)} %get-tuple-element.15, bf16[8,768]{1,0:T(8,128)(2,1)S(1)} %get-tuple-element.13), kind=kOutput, calls=%fused_computation.32 | convolution fusion | flops 37859328 | bytes 1708032 | tf_op jit(solution)/shard_map/dot_general | solution.py:19
  4.2 6.8 %all-to-all-start = ((f32[16,8,1024]{2,1,0:T(8,128)}), f32[16,8,1024]{2,1,0:T(8,128)S(1)}, u32[]{:S(2)}, u32[]{:S(2)}) async-start(f32[16,8,1024]{2,1,0:T(8,128)} %broadcast_in_dim.60), calls=%async_computation | async-start | bytes 1048576 | tf_op jit(solution)/shard_map/all_to_all | solution.py:27
  11.9 1.5 %collective-permute-start = (bf16[384,1024]{1,0:T(8,128)(2,1)}, bf16[384,1024]{1,0:T(8,128)(2,1)}, u32[]{:S(2)}, u32[]{:S(2)}) collective-permute-start(bf16[384,1024]{1,0:T(8,128)(2,1)} %constant_dynamic-slice_fusion.2), channel_id=1, source_target_pairs={{0,8},{33,41},{66,74},{99,107},{132,140},{165,173},{198,206},{231,... | collective-permute-start | bytes 2359304 | tf_op jit(solution)/shard_map/ppermute | solution.py:81
  13.5 7.8 %all-to-all-done = f32[16,8,1024]{2,1,0:T(8,128)S(1)} async-done(((f32[16,8,1024]{2,1,0:T(8,128)}), f32[16,8,1024]{2,1,0:T(8,128)S(1)}, u32[]{:S(2)}, u32[]{:S(2)}) %all-to-all-start) | async-done | bytes 524320 | tf_op jit(solution)/shard_map/all_to_all | solution.py:27
  21.6 1.1 convolution_add_fusion.1
  22.6 3.7 %all-gather = f32[16,384]{1,0:T(8,128)S(1)} all-gather(f32[8,384]{1,0:T(8,128)S(1)} %convolution_add_fusion.1), channel_id=2, replica_groups=mesh['z'=16,'c'=2,'x'=4,'y'=4] {'c'}, dimensions={0}, use_global_device_ids=true | all-gather | bytes 36864 | tf_op jit(solution)/shard_map/all_gather | solution.py:96
  27.0 14.7 %all-to-all-start.1 = ((f32[16,4,384]{2,1,0:T(4,128)}), f32[16,4,384]{2,1,0:T(4,128)S(1)}, u32[]{:S(2)}, u32[]{:S(2)}) async-start(f32[16,4,384]{2,1,0:T(4,128)} %broadcast_in_dim.61), calls=%async_computation.1 | async-start | bytes 196608 | tf_op jit(solution)/shard_map/all_to_all | solution.py:27
  41.6 1.2 broadcast_select_fusion
  42.8 1.6 %collective-permute-start.1 = (bf16[384,1024]{1,0:T(8,128)(2,1)}, bf16[384,1024]{1,0:T(8,128)(2,1)}, u32[]{:S(2)}, u32[]{:S(2)}) collective-permute-start(bf16[384,1024]{1,0:T(8,128)(2,1)} %broadcast_select_fusion), channel_id=1, source_target_pairs={{0,2},{8,10},{33,35},{41,43},{66,64},{74,72},{99,97},{107,105},{13... | collective-permute-start | bytes 2359304 | tf_op jit(solution)/shard_map/ppermute | solution.py:81
  44.4 9.1 %all-to-all-done.1 = f32[16,4,384]{2,1,0:T(4,128)S(1)} async-done(((f32[16,4,384]{2,1,0:T(4,128)}), f32[16,4,384]{2,1,0:T(4,128)S(1)}, u32[]{:S(2)}, u32[]{:S(2)}) %all-to-all-start.1) | async-done | bytes 98336 | tf_op jit(solution)/shard_map/all_to_all | solution.py:27
  53.5 3.8 %all-gather.2 = f32[2,4,384]{2,1,0:T(4,128)S(1)} all-gather(f32[1,4,384]{2,1,0:T(4,128)S(1)} %bitcast.50), channel_id=1, replica_groups=mesh['z'=16,'c'=2,'x'=4,'y'=4] {'c'}, dimensions={0}, use_global_device_ids=true | all-gather | bytes 18432 | tf_op jit(solution)/shard_map/all_gather | solution.py:104
  59.6 4.3 %all-to-all-start.2 = ((f32[16,8,1536]{2,1,0:T(8,128)}), f32[16,8,1536]{2,1,0:T(8,128)}, u32[]{:S(2)}, u32[]{:S(2)}) async-start(f32[16,8,1536]{2,1,0:T(8,128)} %broadcast_in_dim.62), calls=%async_computation.2 | async-start | bytes 1572864 | tf_op jit(solution)/shard_map/all_to_all | solution.py:27
  64.0 2.1 %broadcast_select_fusion.1 = bf16[384,1024]{1,0:T(8,128)(2,1)} fusion(bf16[384,1024]{1,0:T(8,128)(2,1)} %collective-permute-done.1, bf16[384,1024]{1,0:T(8,128)(2,1)} %broadcast_select_fusion, pred[]{:T(512)S(6)} %eq.47), kind=kLoop, calls=%fused_computation.5 | loop fusion | flops 393216 | bytes 2359297 | tf_op jit(solution)/shard_map/jit(_where)/select_n | solution.py:84
  66.1 1.3 %collective-permute-start.2 = (bf16[384,1024]{1,0:T(8,128)(2,1)}, bf16[384,1024]{1,0:T(8,128)(2,1)}, u32[]{:S(2)}, u32[]{:S(2)}) collective-permute-start(bf16[384,1024]{1,0:T(8,128)(2,1)} %broadcast_select_fusion.1), channel_id=1, source_target_pairs={{0,4},{8,12},{2,6},{10,14},{33,37},{41,45},{35,39},{43,47},{66,70}... | collective-permute-start | bytes 2359304 | tf_op jit(solution)/shard_map/ppermute | solution.py:81
  67.4 9.9 %all-to-all-done.2 = f32[16,8,1536]{2,1,0:T(8,128)} async-done(((f32[16,8,1536]{2,1,0:T(8,128)}), f32[16,8,1536]{2,1,0:T(8,128)}, u32[]{:S(2)}, u32[]{:S(2)}) %all-to-all-start.2) | async-done | bytes 786464 | tf_op jit(solution)/shard_map/all_to_all | solution.py:27
  77.2 1.2 reduce_sum.57
  79.8 3.7 %all-gather.1 = f32[16,768]{1,0:T(8,128)S(1)} all-gather(f32[8,768]{1,0:T(8,128)S(1)} %fusion.23), channel_id=3, replica_groups=mesh['z'=16,'c'=2,'x'=4,'y'=4] {'c'}, dimensions={0}, use_global_device_ids=true | all-gather | bytes 73728 | tf_op jit(solution)/shard_map/all_gather | solution.py:127
  84.2 3.7 %all-to-all-start.3 = ((f32[16,8,384]{2,1,0:T(8,128)}), f32[16,8,384]{2,1,0:T(8,128)S(1)}, u32[]{:S(2)}, u32[]{:S(2)}) async-start(f32[16,8,384]{2,1,0:T(8,128)} %broadcast_in_dim.69), calls=%async_computation.3 | async-start | bytes 393216 | tf_op jit(solution)/shard_map/all_to_all | solution.py:27
  89.9 1.2 broadcast_select_fusion.2
  91.1 2.2 %collective-permute-start.3 = (bf16[384,1024]{1,0:T(8,128)(2,1)S(1)}, bf16[384,1024]{1,0:T(8,128)(2,1)}, u32[]{:S(2)}, u32[]{:S(2)}) collective-permute-start(bf16[384,1024]{1,0:T(8,128)(2,1)S(1)} %broadcast_select_fusion.2), channel_id=1, source_target_pairs={{0,1},{8,9},{2,3},{10,11},{4,5},{12,13},{6,7},{14,15},{33,34},{41,... | collective-permute-start | bytes 2359304 | tf_op jit(solution)/shard_map/ppermute | solution.py:81
  93.4 10.6 %all-to-all-done.3 = f32[16,8,384]{2,1,0:T(8,128)S(1)} async-done(((f32[16,8,384]{2,1,0:T(8,128)}), f32[16,8,384]{2,1,0:T(8,128)S(1)}, u32[]{:S(2)}, u32[]{:S(2)}) %all-to-all-start.3) | async-done | bytes 196640 | tf_op jit(solution)/shard_map/all_to_all | solution.py:27
  104.9 4.8 %all-to-all-start.4 = ((f32[32,8,384]{2,1,0:T(8,128)}), f32[32,8,384]{2,1,0:T(8,128)S(1)}, u32[]{:S(2)}, u32[]{:S(2)}) async-start(f32[32,8,384]{2,1,0:T(8,128)} %broadcast_in_dim.70), calls=%async_computation.4 | async-start | bytes 786432 | tf_op jit(solution)/shard_map/all_to_all | solution.py:27
  109.9 10.3 %all-to-all-done.4 = f32[32,8,384]{2,1,0:T(8,128)S(1)} async-done(((f32[32,8,384]{2,1,0:T(8,128)}), f32[32,8,384]{2,1,0:T(8,128)S(1)}, u32[]{:S(2)}, u32[]{:S(2)}) %all-to-all-start.4) | async-done | bytes 393248 | tf_op jit(solution)/shard_map/all_to_all | solution.py:27
  121.3 1.7 %multiply_add_fusion = (f32[384,384]{1,0:T(8,128)}, f32[384,384]{1,0:T(8,128)}) fusion(f32[384,384]{1,0:T(8,128)S(1)} %copy-done.3, f32[384,384]{1,0:T(8,128)S(1)} %convolution_add_fusion, f32[8,384]{1,0:T(8,128)S(1)} %fusion.47, f32[32,8,384]{2,1,0:T(8,128)S(1)} %all-to-all-done.4, s32[]{:T(128)S(6)} %select_n.130), kind=kOutput, calls=%fused_computation.8 | convolution fusion | flops 14598144 | bytes 2383876 | tf_op jit(solution)/shard_map/dot_general | solution.py:140
  (57 shorter events, 12.9 us)
Async XLA Ops:
  0.6 20.7 %copy-start = (bf16[1024,384]{1,0:T(8,128)(2,1)S(1)}, bf16[1024,384]{1,0:T(8,128)(2,1)}, u32[]{:S(2)}) copy-start(bf16[1024,384]{1,0:T(8,128)(2,1)} %param.5) | copy-start | bytes 2359300
  1.5 9.5 %copy-start.1 = (bf16[768,1024]{1,0:T(8,128)(2,1)S(1)}, bf16[768,1024]{1,0:T(8,128)(2,1)}, u32[]{:S(2)}) copy-start(bf16[768,1024]{1,0:T(8,128)(2,1)} %param.6) | copy-start | bytes 4718596
  4.2 17.1 %all-to-all-start = ((f32[16,8,1024]{2,1,0:T(8,128)}), f32[16,8,1024]{2,1,0:T(8,128)S(1)}, u32[]{:S(2)}, u32[]{:S(2)}) async-start(f32[16,8,1024]{2,1,0:T(8,128)} %broadcast_in_dim.60), calls=%async_computation | async-start | bytes 1048576 | tf_op jit(solution)/shard_map/all_to_all | solution.py:27
  10.9 10.6 %copy-start.2 = (f32[384,384]{1,0:T(8,128)S(1)}, f32[384,384]{1,0:T(8,128)}, u32[]{:S(2)}) copy-start(f32[384,384]{1,0:T(8,128)} %param.7) | copy-start | bytes 1769476
  11.9 29.7 %collective-permute-start = (bf16[384,1024]{1,0:T(8,128)(2,1)}, bf16[384,1024]{1,0:T(8,128)(2,1)}, u32[]{:S(2)}, u32[]{:S(2)}) collective-permute-start(bf16[384,1024]{1,0:T(8,128)(2,1)} %constant_dynamic-slice_fusion.2), channel_id=1, source_target_pairs={{0,8},{33,41},{66,74},{99,107},{132,140},{165,173},{198,206},{231,... | collective-permute-start | bytes 2359304 | tf_op jit(solution)/shard_map/ppermute | solution.py:81
  27.0 26.5 %all-to-all-start.1 = ((f32[16,4,384]{2,1,0:T(4,128)}), f32[16,4,384]{2,1,0:T(4,128)S(1)}, u32[]{:S(2)}, u32[]{:S(2)}) async-start(f32[16,4,384]{2,1,0:T(4,128)} %broadcast_in_dim.61), calls=%async_computation.1 | async-start | bytes 196608 | tf_op jit(solution)/shard_map/all_to_all | solution.py:27
  42.8 21.2 %collective-permute-start.1 = (bf16[384,1024]{1,0:T(8,128)(2,1)}, bf16[384,1024]{1,0:T(8,128)(2,1)}, u32[]{:S(2)}, u32[]{:S(2)}) collective-permute-start(bf16[384,1024]{1,0:T(8,128)(2,1)} %broadcast_select_fusion), channel_id=1, source_target_pairs={{0,2},{8,10},{33,35},{41,43},{66,64},{74,72},{99,97},{107,105},{13... | collective-permute-start | bytes 2359304 | tf_op jit(solution)/shard_map/ppermute | solution.py:81
  59.6 17.7 %all-to-all-start.2 = ((f32[16,8,1536]{2,1,0:T(8,128)}), f32[16,8,1536]{2,1,0:T(8,128)}, u32[]{:S(2)}, u32[]{:S(2)}) async-start(f32[16,8,1536]{2,1,0:T(8,128)} %broadcast_in_dim.62), calls=%async_computation.2 | async-start | bytes 1572864 | tf_op jit(solution)/shard_map/all_to_all | solution.py:27
  66.1 23.7 %collective-permute-start.2 = (bf16[384,1024]{1,0:T(8,128)(2,1)}, bf16[384,1024]{1,0:T(8,128)(2,1)}, u32[]{:S(2)}, u32[]{:S(2)}) collective-permute-start(bf16[384,1024]{1,0:T(8,128)(2,1)} %broadcast_select_fusion.1), channel_id=1, source_target_pairs={{0,4},{8,12},{2,6},{10,14},{33,37},{41,45},{35,39},{43,47},{66,70}... | collective-permute-start | bytes 2359304 | tf_op jit(solution)/shard_map/ppermute | solution.py:81
  84.2 19.8 %all-to-all-start.3 = ((f32[16,8,384]{2,1,0:T(8,128)}), f32[16,8,384]{2,1,0:T(8,128)S(1)}, u32[]{:S(2)}, u32[]{:S(2)}) async-start(f32[16,8,384]{2,1,0:T(8,128)} %broadcast_in_dim.69), calls=%async_computation.3 | async-start | bytes 393216 | tf_op jit(solution)/shard_map/all_to_all | solution.py:27
  91.1 29.1 %collective-permute-start.3 = (bf16[384,1024]{1,0:T(8,128)(2,1)S(1)}, bf16[384,1024]{1,0:T(8,128)(2,1)}, u32[]{:S(2)}, u32[]{:S(2)}) collective-permute-start(bf16[384,1024]{1,0:T(8,128)(2,1)S(1)} %broadcast_select_fusion.2), channel_id=1, source_target_pairs={{0,1},{8,9},{2,3},{10,11},{4,5},{12,13},{6,7},{14,15},{33,34},{41,... | collective-permute-start | bytes 2359304 | tf_op jit(solution)/shard_map/ppermute | solution.py:81
  104.9 15.3 %all-to-all-start.4 = ((f32[32,8,384]{2,1,0:T(8,128)}), f32[32,8,384]{2,1,0:T(8,128)S(1)}, u32[]{:S(2)}, u32[]{:S(2)}) async-start(f32[32,8,384]{2,1,0:T(8,128)} %broadcast_in_dim.70), calls=%async_computation.4 | async-start | bytes 786432 | tf_op jit(solution)/shard_map/all_to_all | solution.py:27
  120.2 1.1 copy-start.3

commit v4 on v3

--- a/solution.py
+++ b/solution.py
@@ -1,6 +1,8 @@
 import jax
 import jax.numpy as jnp
 from jax import lax
+from jax.experimental import pallas as pl
+from jax.experimental.pallas import tpu as pltpu
 from jax.sharding import Mesh, PartitionSpec as P
 
 decay_rate = 0.9
@@ -25,6 +27,122 @@
 
 def copies(x, axes, count):
     return lax.all_to_all(jnp.broadcast_to(x[None], (count,) + x.shape), axes, 0, 0)
+
+
+def near(x):
+    return pltpu.with_memory_space_constraint(x, pltpu.VMEM)
+
+
+def local(kernel, outs, micros, *args):
+    whole = pl.BlockSpec(memory_space=pltpu.VMEM)
+    size = sum(a.size * a.dtype.itemsize for a in args)
+    return pl.pallas_call(
+        kernel,
+        out_shape=outs,
+        in_specs=[whole] * len(args),
+        out_specs=[whole] * len(outs),
+        cost_estimate=pl.CostEstimate(
+            flops=int(micros * 1e9), bytes_accessed=size, transcendentals=0
+        ),
+    )(*args)
+
+
+def exact_dot(x, wide, dims):
+    a = x.astype(jnp.bfloat16).astype(jnp.float32)
+    r = x - a
+    b = r.astype(jnp.bfloat16).astype(jnp.float32)
+    parts = jnp.concatenate([a, b, r - b, jnp.zeros_like(x)], 0)
+    y = lax.dot_general(
+        parts.astype(jnp.bfloat16),
+        wide,
+        (dims, ((), ())),
+        preferred_element_type=jnp.float32,
+    )
+    n = x.shape[0]
+    return (y[2 * n : 3 * n] + y[n : 2 * n]) + y[:n]
+
+
+def total(ref, lanes):
+    y = ref[0, :, lanes]
+    for i in range(1, ref.shape[0]):
+        y = y + ref[i, :, lanes]
+    return y
+
+
+def early_kernel(hid, q, feed, err, piece):
+    rows = feed.shape[0]
+    core = lax.axis_index("c")
+    replica = lax.axis_index("z") * lax.axis_size("c") + core
+    own = q[:, pl.ds(pl.multiple_of(replica * rows, rows), rows)]
+    err[...] = jnp.dot(
+        own, feed[...], precision=high, preferred_element_type=jnp.float32
+    )
+    piece[...] = hid[pl.ds(pl.multiple_of(core * rows, rows), rows), :]
+
+
+def left_kernel(got, act, err, out):
+    tokens = total(got, slice(None))
+    out[...] = exact_dot(tokens, act[...], ((1,), (0,))) + err[...]
+
+
+def right_kernel(p_ref, act, feed, out):
+    p = p_ref[...]
+    rank, toks = p.shape[0], act.shape[0]
+    rows = feed.shape[0]
+    u = exact_dot(p, act[...], ((1,), (1,)))
+    across = (((1,), (1,)), ((), ()))
+    err = lax.dot_general(
+        p, feed[...], across, precision=high, preferred_element_type=jnp.float32
+    )
+    square = jnp.concatenate([p, jnp.zeros((128 - rank, p.shape[1]), p.dtype)], 0)
+    gram = lax.dot_general(
+        p, square, across, precision=high, preferred_element_type=jnp.float32
+    )
+    for i in range(out.shape[0]):
+        out[i, :, :toks] = u
+        out[i, :, toks : toks + rows] = err
+        out[i, :, toks + rows :] = gram
+
+
+def hidden_kernel(got, hid, out, gram):
+    toks, rows = hid.shape[1], out.shape[1] // 2
+    u = total(got, slice(0, toks))
+    err = total(got, slice(toks, toks + rows))
+    gram[...] = total(got, slice(toks + rows, None))
+    y = exact_dot(u, hid[...], ((1,), (1,)))
+    shard = lax.axis_index("x") * lax.axis_size("y") + lax.axis_index("y")
+    mine = jnp.where(shard == lax.axis_index("z"), 1.0, 0.0)
+    upper = jnp.where(lax.axis_index("c") == 0, mine, 0.0)
+    lower = mine - upper
+    out[:, :rows] = y[:, :rows] + err * upper
+    out[:, rows:] = y[:, rows:] + err * lower
+
+
+def block_kernel(got, inverse, out):
+    rows = total(got, slice(None))
+    block = jnp.dot(
+        inverse[...], rows, precision=high, preferred_element_type=jnp.float32
+    )
+    block = block * (1.0 / out.shape[0])
+    for i in range(out.shape[0]):
+        out[i] = block
+
+
+def last_kernel(blocks, ortho, base, momentum, feed_out, mom_out, q_out):
+    count, _, rows = blocks.shape
+    replica = lax.axis_index("z") * lax.axis_size("c") + lax.axis_index("c")
+    mine = blocks[replica]
+    approx = lax.dot_general(
+        mine,
+        ortho[...],
+        (((0,), (0,)), ((), ())),
+        precision=high,
+        preferred_element_type=jnp.float32,
+    )
+    feed_out[...] = base[...] - approx
+    mom_out[...] = decay_rate * momentum[...] + approx
+    for i in range(count):
+        q_out[:, i * rows : (i + 1) * rows] = blocks[i]
 
 
 def tie(x, after):
@@ -85,14 +203,30 @@
 
     q_rows = q_start.T
     q_block = lax.dynamic_slice_in_dim(q_rows, shard * cols_mp, cols_mp, 1)
-    q_owned = lax.dynamic_slice_in_dim(q_rows, own_start, cols_dp, 1)
     token_part = thin_dot(q_block, hidden, ((1,), (0,)))
-    hid_late = tie(hidden, token_part)
-    held = lax.dynamic_slice_in_dim(hid_late, core * cols_dp, cols_dp, 0)
+    f32 = jnp.float32
+    act_near, hid_near, feed_near = near(activations), near(hidden), near(feedback)
+    p_err, held = local(
+        early_kernel,
+        [
+            pltpu.VMEM((rank, width), f32),
+            pltpu.VMEM((cols_dp, toks), hidden.dtype),
+        ],
+        1.5,
+        tie(hid_near, token_part),
+        near(q_rows),
+        feed_near,
+    )
     got = send(held, 0)
-    token_q = copies(token_part, plane, n_mp).sum(0)
-    p_err = jnp.dot(q_owned, feedback, precision=high)
-    p_part = thin_dot(token_q, activations, ((1,), (0,))) + p_err
+    tokens = near(copies(token_part, plane, n_mp))
+    (p_part,) = local(
+        left_kernel,
+        [pltpu.VMEM((rank, width), f32)],
+        1,
+        tokens,
+        act_near,
+        p_err,
+    )
     p_pair = lax.all_gather(p_part, "c").sum(0)
     held = take(held, tie(got, p_pair), 0)
     got = send(held, 1)
@@ -103,44 +237,58 @@
     got = send(held, 2)
     p_sum = lax.all_gather(p_half, "c", tiled=True)
 
-    u_part = thin_dot(p_sum, activations, ((1,), (1,)))
-    err_part = lax.dot_general(
-        p_sum, feedback, (((1,), (1,)), ((), ())), precision=high
-    )
-    gram_part = lax.dot_general(p_sum, p_sum, (((1,), (1,)), ((), ())), precision=high)
-    packed = jnp.concatenate(
-        [u_part, err_part, jnp.pad(gram_part, ((0, 0), (0, 128 - rank)))], 1
-    )
-    packed = copies(packed, plane, n_mp).sum(0)
-    u = packed[:, :toks]
-    err = packed[:, toks : toks + cols_dp]
-    gram_mat = packed[:, toks + cols_dp : toks + cols_dp + rank]
+    (packed,) = local(
+        right_kernel,
+        [pltpu.VMEM((n_mp, rank, toks + cols_dp + 128), f32)],
+        2,
+        near(p_sum),
+        act_near,
+        feed_near,
+    )
+    packed = near(lax.all_to_all(packed, plane, 0, 0))
+    hid, gram_mat = local(
+        hidden_kernel,
+        [pltpu.VMEM((rank, cols_mp), f32), pltpu.VMEM((rank, 128), f32)],
+        1,
+        packed,
+        hid_near,
+    )
+    gram_mat = gram_mat[:, :rank]
     factor = jnp.linalg.cholesky(gram_mat)
     inverse = lax.linalg.triangular_solve(
         factor, jnp.eye(rank, dtype=jnp.float32), left_side=True, lower=True
     )
-    hid = thin_dot(u, hidden, ((1,), (1,)))
-    hid = hid.reshape(rank, nc, cols_mp // nc)
-    mine = (shard == root_dev) & (jnp.arange(nc) == core)
-    hid = hid + jnp.where(mine[None, :, None], err[:, None, :], 0.0)
-    hid = hid.reshape(rank, cols_mp)
     half = lax.all_gather(hid, "c").sum(0)
     half = lax.dynamic_slice_in_dim(half, core * cols_dp, cols_dp, 1)
     held = take(held, tie(got, half), 2)
     got = send(held, 3)
-    half = copies(half, "z", nz).sum(0)
-    block = jnp.dot(inverse, half, precision=high) / n_dp
+    half = near(copies(half, "z", nz))
+    (block,) = local(
+        block_kernel,
+        [pltpu.VMEM((n_dp, rank, cols_dp), f32)],
+        1,
+        half,
+        near(inverse),
+    )
     held = take(held, tie(got, block), 3)
     own_grad = jnp.dot(held, activations, preferred_element_type=jnp.float32)
     base = lax.optimization_barrier(own_grad + feedback)
-    blocks = copies(block, ("x", "y", "c"), n_dp)
-    q_next = jnp.transpose(blocks, (1, 0, 2)).reshape(rank, -1).T
-    q_mine = lax.dynamic_index_in_dim(blocks, replica, 0, keepdims=False)
+    blocks = near(lax.all_to_all(block, ("x", "y", "c"), 0, 0))
     ortho = jnp.dot(inverse, p_sum, precision=high)
-    approx = lax.dot_general(q_mine, ortho, (((0,), (0,)), ((), ())), precision=high)
-    new_feedback = base - approx
-    new_momentum = decay_rate * momentum + approx
-    return (new_feedback, new_momentum, q_next)
+    new_feedback, new_momentum, q_next = local(
+        last_kernel,
+        [
+            jax.ShapeDtypeStruct(feedback.shape, f32),
+            jax.ShapeDtypeStruct(momentum.shape, f32),
+            jax.ShapeDtypeStruct(q_rows.shape, f32),
+        ],
+        2,
+        blocks,
+        near(ortho),
+        near(base),
+        near(momentum),
+    )
+    return (new_feedback, new_momentum, q_next.T)
 
 
 def solution(mesh):

time: 125 us -> 122 us (0.976)
  Pallas kernels: 0 us -> 6.85 us
  matrix products: 7.55 us -> 3.97 us
  local copies, waits for them, and re-layouts: 6.36 us -> 3.6 us
  starting transfers between devices: 40.8 us -> 39.4 us
  waiting for transfers between devices: 47.6 us -> 46.3 us
    all_to_all x5 -> x3, waiting for transfers between devices: 47.6 us -> 28 us  [copies(): lax.all_to_all(jnp.broadcast_to(x[None], (count,) + x.shape), axes, 0, 0)]
    all_to_all x0 -> x2, waiting for transfers between devices: none -> 18.3 us  [the longest x1 9.81 us: per_device(): packed = near(lax.all_to_all(packed, plane, 0, 0))]
    all_to_all x5 -> x3, starting transfers between devices: 34.2 us -> 25.2 us  [copies(): lax.all_to_all(jnp.broadcast_to(x[None], (count,) + x.shape), axes, 0, 0)]
    all_to_all x0 -> x2, starting transfers between devices: none -> 8.45 us  [the longest x1 4.84 us: per_device(): blocks = near(lax.all_to_all(block, ('x', 'y', 'c'), 0, 0))]
    pallas_call x0 -> x6, Pallas kernels: none -> 6.85 us  [local(): pl.pallas_call(kernel, out_shape=outs, in_specs=[whole] * len(args), out_...]
    dot_general x5 -> x0, matrix products: 3.65 us -> none  [the longest x1 1.74 us: per_device(): lax.dot_general(q_mine, ortho, (((0,), (0,)), ((), ())), precision=high)]
    broadcast_in_dim x5 -> x3, local copies, waits for them, and re-layouts: 3.97 us -> 2.19 us  [copies(): jnp.broadcast_to(x[None], (count,) + x.shape)]
    dot_general x4 -> x1, matrix products: 3 us -> 1.87 us  [thin_dot(): lax.dot_general(split_parts(x), wide, (dims, ((), ())), preferred_element...]
  transfers between devices with their start and end apart: 9 -> 9, of which waited for: 5 -> 5; matrix products, arithmetic and copies ran while one was open for 13% -> 10% of each run, Pallas kernels for 0% -> 4%
where the time goes in v4:
time: 122 us; the launch traced here: 121 us
  waiting for transfers between devices  46.3 us (38%)
  starting transfers between devices  39.4 us (32%)
  blocking collectives  11.3 us (9%)
  other arithmetic  8.72 us (7%)
  Pallas kernels  6.85 us (6%)
  matrix products  3.97 us (3%)
  local copies, waits for them, and re-layouts  3.6 us (3%)
    all_to_all x3, waiting for transfers between devices, copies(): lax.all_to_all(jnp.broadcast_to(x[None], (count,) + x.shape), axes, 0, 0)  28 us
    all_to_all x3, starting transfers between devices, copies(): lax.all_to_all(jnp.broadcast_to(x[None], (count,) + x.shape), axes, 0, 0)  25.2 us
    all_to_all x1, waiting for transfers between devices, per_device(): packed = near(lax.all_to_all(packed, plane, 0, 0))  9.81 us
    all_to_all x1, waiting for transfers between devices, per_device(): blocks = near(lax.all_to_all(block, ('x', 'y', 'c'), 0, 0))  8.46 us
    pallas_call x6, Pallas kernels, local(): pl.pallas_call(kernel, out_shape=outs, in_specs=[whole] * len(args), out_...  6.85 us
    ppermute x4, starting transfers between devices, send(): return lax.ppermute(held, ('z', 'c', 'x', 'y'), rounds[k])  5.78 us
    select_n x3, other arithmetic, take(): return jnp.where(turn == k, got, held)  5.29 us
    all_to_all x1, starting transfers between devices, per_device(): blocks = near(lax.all_to_all(block, ('x', 'y', 'c'), 0, 0))  4.84 us
  transfers between devices with their start and end apart: 9, of which 5 were waited for; matrix products, arithmetic and copies ran while one was open for 10% of the time, Pallas kernels for 4%

profile of v4, /device:TPU:33, one launch (start us, length us, event | category | flops | bytes accessed | tf_op | source)
XLA Modules:
  0.0 121.1 jit_solution(8206324312951472929)
XLA Ops:
  1.4 1.9 %fusion.2 = f32[24,1024]{1,0:T(8,128)S(1)} fusion(bf16[768,1024]{1,0:T(8,128)(2,1)} %hid.2, bf16[8,768]{1,0:T(8,128)(2,1)S(1)} %get-tuple-element.26, bf16[8,768]{1,0:T(8,128)(2,1)S(1)} %get-tuple-element.27, bf16[8,768]{1,0:T(8,128)(2,1)S(1)} %get-tuple-element.25), kind=kOutput, calls=%fused_computation.7 | convolution fusion | flops 37859328 | bytes 1708032 | tf_op jit(solution)/shard_map/dot_general | solution.py:21
  4.2 6.8 %all-to-all-start = ((f32[16,8,1024]{2,1,0:T(8,128)}), f32[16,8,1024]{2,1,0:T(8,128)}, u32[]{:S(2)}, u32[]{:S(2)}) async-start(f32[16,8,1024]{2,1,0:T(8,128)} %broadcast_in_dim.7), calls=%async_computation | async-start | bytes 1048576 | tf_op jit(solution)/shard_map/all_to_all | solution.py:29
  12.3 9.1 %all-to-all-done.got = f32[16,8,1024]{2,1,0:T(8,128)} async-done(((f32[16,8,1024]{2,1,0:T(8,128)}), f32[16,8,1024]{2,1,0:T(8,128)}, u32[]{:S(2)}, u32[]{:S(2)}) %all-to-all-start) | async-done | bytes 524320 | tf_op jit(solution)/shard_map/all_to_all | solution.py:29
  21.3 1.1 copy-done.2
  22.5 1.3 %shard_map.77 = f32[8,384]{1,0:T(8,128)S(1)} custom-call(f32[16,8,1024]{2,1,0:T(8,128)} %all-to-all-done.got, bf16[1024,384]{1,0:T(8,128)(2,1)S(1)} %copy-done.2, f32[8,384]{1,0:T(8,128)} %copy-done.10), custom_call_target="tpu_custom_call" | custom-call | flops 1000000000 | bytes 1323008 | tf_op jit(solution)/shard_map/pallas_call | solution.py:39
  23.8 3.8 %all-gather = f32[16,384]{1,0:T(8,128)S(1)} all-gather(f32[8,384]{1,0:T(8,128)S(1)} %shard_map.77), channel_id=2, replica_groups=mesh['z'=16,'c'=2,'x'=4,'y'=4] {'c'}, dimensions={0}, use_global_device_ids=true | all-gather | bytes 36864 | tf_op jit(solution)/shard_map/all_gather | solution.py:230
  28.2 14.7 %all-to-all-start.1 = ((f32[16,4,384]{2,1,0:T(4,128)}), f32[16,4,384]{2,1,0:T(4,128)S(1)}, u32[]{:S(2)}, u32[]{:S(2)}) async-start(f32[16,4,384]{2,1,0:T(4,128)} %broadcast_in_dim.8), calls=%async_computation.1 | async-start | bytes 196608 | tf_op jit(solution)/shard_map/all_to_all | solution.py:29
  43.8 1.6 %collective-permute-start.1 = (bf16[384,1024]{1,0:T(8,128)(2,1)}, bf16[384,1024]{1,0:T(8,128)(2,1)}, u32[]{:S(2)}, u32[]{:S(2)}) collective-permute-start(bf16[384,1024]{1,0:T(8,128)(2,1)} %broadcast_select_fusion), channel_id=1, source_target_pairs={{0,2},{8,10},{33,35},{41,43},{66,64},{74,72},{99,97},{107,105},{13... | collective-permute-start | bytes 2359304 | tf_op jit(solution)/shard_map/ppermute | solution.py:199
  45.4 9.3 %all-to-all-done.1 = f32[16,4,384]{2,1,0:T(4,128)S(1)} async-done(((f32[16,4,384]{2,1,0:T(4,128)}), f32[16,4,384]{2,1,0:T(4,128)S(1)}, u32[]{:S(2)}, u32[]{:S(2)}) %all-to-all-start.1) | async-done | bytes 98336 | tf_op jit(solution)/shard_map/all_to_all | solution.py:29
  54.8 3.8 %all-gather.2 = f32[2,4,384]{2,1,0:T(4,128)S(1)} all-gather(f32[1,4,384]{2,1,0:T(4,128)S(1)} %bitcast.29), channel_id=1, replica_groups=mesh['z'=16,'c'=2,'x'=4,'y'=4] {'c'}, dimensions={0}, use_global_device_ids=true | all-gather | bytes 18432 | tf_op jit(solution)/shard_map/all_gather | solution.py:238
  58.6 1.8 %shard_map.78 = f32[16,8,1536]{2,1,0:T(8,128)} custom-call(f32[8,384]{1,0:T(8,128)S(1)} %reshape.21.p_ref, bf16[1024,384]{1,0:T(8,128)(2,1)S(1)} %copy-done.3, f32[384,384]{1,0:T(8,128)S(1)} %copy-done.6), custom_call_target="tpu_custom_call" | custom-call | flops 2000000000 | bytes 1388544 | tf_op jit(solution)/shard_map/pallas_call | solution.py:39
  60.4 3.6 %all-to-all-start.2 = ((f32[16,8,1536]{2,1,0:T(8,128)}), f32[16,8,1536]{2,1,0:T(8,128)S(1)}, u32[]{:S(2)}, u32[]{:S(2)}) async-start(f32[16,8,1536]{2,1,0:T(8,128)} %shard_map.78), calls=%async_computation.2 | async-start | bytes 1572864 | tf_op jit(solution)/shard_map/all_to_all | solution.py:248
  64.1 2.2 %broadcast_select_fusion.1 = bf16[384,1024]{1,0:T(8,128)(2,1)} fusion(bf16[384,1024]{1,0:T(8,128)(2,1)} %collective-permute-done.1, bf16[384,1024]{1,0:T(8,128)(2,1)} %broadcast_select_fusion, pred[]{:T(512)S(6)} %eq.34), kind=kLoop, calls=%fused_computation.3 | loop fusion | flops 393216 | bytes 2359297 | tf_op jit(solution)/shard_map/jit(_where)/select_n | solution.py:202
  66.3 1.3 %collective-permute-start.2 = (bf16[384,1024]{1,0:T(8,128)(2,1)}, bf16[384,1024]{1,0:T(8,128)(2,1)}, u32[]{:S(2)}, u32[]{:S(2)}) collective-permute-start(bf16[384,1024]{1,0:T(8,128)(2,1)} %broadcast_select_fusion.1), channel_id=1, source_target_pairs={{0,4},{8,12},{2,6},{10,14},{33,37},{41,45},{35,39},{43,47},{66,70}... | collective-permute-start | bytes 2359304 | tf_op jit(solution)/shard_map/ppermute | solution.py:199
  67.6 9.8 %all-to-all-done.2.got = f32[16,8,1536]{2,1,0:T(8,128)S(1)} async-done(((f32[16,8,1536]{2,1,0:T(8,128)}), f32[16,8,1536]{2,1,0:T(8,128)S(1)}, u32[]{:S(2)}, u32[]{:S(2)}) %all-to-all-start.2) | async-done | bytes 786464 | tf_op jit(solution)/shard_map/all_to_all | solution.py:248
  78.9 3.7 %all-gather.1 = f32[16,768]{1,0:T(8,128)S(1)} all-gather(f32[8,768]{1,0:T(8,128)S(1)} %get-tuple-element.16), channel_id=3, replica_groups=mesh['z'=16,'c'=2,'x'=4,'y'=4] {'c'}, dimensions={0}, use_global_device_ids=true | all-gather | bytes 73728 | tf_op jit(solution)/shard_map/all_gather | solution.py:261
  83.3 3.7 %all-to-all-start.3 = ((f32[16,8,384]{2,1,0:T(8,128)}), f32[16,8,384]{2,1,0:T(8,128)S(1)}, u32[]{:S(2)}, u32[]{:S(2)}) async-start(f32[16,8,384]{2,1,0:T(8,128)} %broadcast_in_dim.10), calls=%async_computation.3 | async-start | bytes 393216 | tf_op jit(solution)/shard_map/all_to_all | solution.py:29
  87.0 2.1 %broadcast_select_fusion.2 = bf16[384,1024]{1,0:T(8,128)(2,1)} fusion(bf16[384,1024]{1,0:T(8,128)(2,1)} %collective-permute-done.2, bf16[384,1024]{1,0:T(8,128)(2,1)} %broadcast_select_fusion.1, pred[]{:T(512)S(6)} %eq.33), kind=kLoop, calls=%fused_computation.4 | loop fusion | flops 393216 | bytes 2359297 | tf_op jit(solution)/shard_map/jit(_where)/select_n | solution.py:202
  89.1 2.2 %collective-permute-start.3 = (bf16[384,1024]{1,0:T(8,128)(2,1)}, bf16[384,1024]{1,0:T(8,128)(2,1)}, u32[]{:S(2)}, u32[]{:S(2)}) collective-permute-start(bf16[384,1024]{1,0:T(8,128)(2,1)} %broadcast_select_fusion.2), channel_id=1, source_target_pairs={{0,1},{8,9},{2,3},{10,11},{4,5},{12,13},{6,7},{14,15},{33,34},{41,... | collective-permute-start | bytes 2359304 | tf_op jit(solution)/shard_map/ppermute | solution.py:199
  93.4 9.7 %all-to-all-done.3.got = f32[16,8,384]{2,1,0:T(8,128)S(1)} async-done(((f32[16,8,384]{2,1,0:T(8,128)}), f32[16,8,384]{2,1,0:T(8,128)S(1)}, u32[]{:S(2)}, u32[]{:S(2)}) %all-to-all-start.3) | async-done | bytes 196640 | tf_op jit(solution)/shard_map/all_to_all | solution.py:29
  104.0 4.8 %all-to-all-start.4 = ((f32[32,8,384]{2,1,0:T(8,128)}), f32[32,8,384]{2,1,0:T(8,128)S(1)}, u32[]{:S(2)}, u32[]{:S(2)}) async-start(f32[32,8,384]{2,1,0:T(8,128)} %shard_map.80), calls=%async_computation.4 | async-start | bytes 786432 | tf_op jit(solution)/shard_map/all_to_all | solution.py:276
  109.0 1.8 %convolution_add_fusion.base = f32[384,384]{1,0:T(8,128)S(1)} fusion(f32[384,384]{1,0:T(8,128)S(1)} %copy-done.7, bf16[1024,384]{1,0:T(8,128)(2,1)S(1)} %copy-done.4, bf16[384,1024]{1,0:T(8,128)(2,1)} %collective-permute-done.3, bf16[384,1024]{1,0:T(8,128)(2,1)} %broadcast_select_fusion.2, pred[]{:T(512)S(6)} %eq.32), kind=kOutput, calls=%fused_computation | convolution fusion | flops 302530560 | bytes 3538945 | tf_op jit(solution)/shard_map/dot_general | solution.py:274
  110.8 8.5 %all-to-all-done.4.blocks = f32[32,8,384]{2,1,0:T(8,128)S(1)} async-done(((f32[32,8,384]{2,1,0:T(8,128)}), f32[32,8,384]{2,1,0:T(8,128)S(1)}, u32[]{:S(2)}, u32[]{:S(2)}) %all-to-all-start.4) | async-done | bytes 393248 | tf_op jit(solution)/shard_map/all_to_all | solution.py:276
  119.3 1.8 %shard_map.81 = (f32[384,384]{1,0:T(8,128)}, f32[384,384]{1,0:T(8,128)}, f32[8,12288]{1,0:T(8,128)}) custom-call(f32[32,8,384]{2,1,0:T(8,128)S(1)} %all-to-all-done.4.blocks, f32[8,384]{1,0:T(8,128)S(1)} %fusion.14.ortho, f32[384,384]{1,0:T(8,128)S(1)} %convolution_add_fusion.base, f32[384,384]{1,0:T(8,128)S(1)} %copy-done.9), custom_call_target="tpu_custom_call" | custom-call | flops 2000000000 | bytes 1585152 | tf_op jit(solution)/shard_map/pallas_call | solution.py:39
  (52 shorter events, 9.8 us)
Async XLA Ops:
  1.4 9.6 %copy-start = (bf16[768,1024]{1,0:T(8,128)(2,1)S(1)}, bf16[768,1024]{1,0:T(8,128)(2,1)}, u32[]{:S(2)}) copy-start(bf16[768,1024]{1,0:T(8,128)(2,1)} %hid.2) | copy-start | bytes 4718596
  1.4 9.6 %copy-start.5 = (f32[384,384]{1,0:T(8,128)S(1)}, f32[384,384]{1,0:T(8,128)}, u32[]{:S(2)}) copy-start(f32[384,384]{1,0:T(8,128)} %feed.3) | copy-start | bytes 1769476
  1.4 9.6 %copy-start.8 = (f32[12288,8]{0,1:T(8,128)S(1)}, f32[12288,8]{0,1:T(8,128)}, u32[]{:S(2)}) copy-start(f32[12288,8]{0,1:T(8,128)} %param.9) | copy-start | bytes 1179652
  4.2 17.2 %all-to-all-start = ((f32[16,8,1024]{2,1,0:T(8,128)}), f32[16,8,1024]{2,1,0:T(8,128)}, u32[]{:S(2)}, u32[]{:S(2)}) async-start(f32[16,8,1024]{2,1,0:T(8,128)} %broadcast_in_dim.7), calls=%async_computation | async-start | bytes 1048576 | tf_op jit(solution)/shard_map/all_to_all | solution.py:29
  11.4 9.9 %copy-start.10 = (f32[8,384]{1,0:T(8,128)}, f32[8,384]{1,0:T(8,128)S(1)}, u32[]{:S(2)}) copy-start(f32[8,384]{1,0:T(8,128)S(1)} %get-tuple-element.15.err) | copy-start | bytes 36868
  11.4 31.4 %collective-permute-start = (bf16[384,1024]{1,0:T(8,128)(2,1)S(1)}, bf16[384,1024]{1,0:T(8,128)(2,1)S(1)}, u32[]{:S(2)}, u32[]{:S(2)}) collective-permute-start(bf16[384,1024]{1,0:T(8,128)(2,1)S(1)} %get-tuple-element.18), channel_id=1, source_target_pairs={{0,8},{33,41},{66,74},{99,107},{132,140},{165,173},{198,206},{231,... | collective-permute-start | bytes 2359304 | tf_op jit(solution)/shard_map/ppermute | solution.py:199
  21.3 1.1 copy-start.2
  23.8 34.9 %copy-start.3 = (bf16[1024,384]{1,0:T(8,128)(2,1)S(1)}, bf16[1024,384]{1,0:T(8,128)(2,1)}, u32[]{:S(2)}) copy-start(bf16[1024,384]{1,0:T(8,128)(2,1)} %act.3) | copy-start | bytes 2359300
  23.8 34.9 %copy-start.6 = (f32[384,384]{1,0:T(8,128)S(1)}, f32[384,384]{1,0:T(8,128)}, u32[]{:S(2)}) copy-start(f32[384,384]{1,0:T(8,128)} %feed.3) | copy-start | bytes 1769476
  28.2 26.5 %all-to-all-start.1 = ((f32[16,4,384]{2,1,0:T(4,128)}), f32[16,4,384]{2,1,0:T(4,128)S(1)}, u32[]{:S(2)}, u32[]{:S(2)}) async-start(f32[16,4,384]{2,1,0:T(4,128)} %broadcast_in_dim.8), calls=%async_computation.1 | async-start | bytes 196608 | tf_op jit(solution)/shard_map/all_to_all | solution.py:29
  43.8 20.3 %collective-permute-start.1 = (bf16[384,1024]{1,0:T(8,128)(2,1)}, bf16[384,1024]{1,0:T(8,128)(2,1)}, u32[]{:S(2)}, u32[]{:S(2)}) collective-permute-start(bf16[384,1024]{1,0:T(8,128)(2,1)} %broadcast_select_fusion), channel_id=1, source_target_pairs={{0,2},{8,10},{33,35},{41,43},{66,64},{74,72},{99,97},{107,105},{13... | collective-permute-start | bytes 2359304 | tf_op jit(solution)/shard_map/ppermute | solution.py:199
  60.4 17.0 %all-to-all-start.2 = ((f32[16,8,1536]{2,1,0:T(8,128)}), f32[16,8,1536]{2,1,0:T(8,128)S(1)}, u32[]{:S(2)}, u32[]{:S(2)}) async-start(f32[16,8,1536]{2,1,0:T(8,128)} %shard_map.78), calls=%async_computation.2 | async-start | bytes 1572864 | tf_op jit(solution)/shard_map/all_to_all | solution.py:248
  64.1 13.4 %copy-start.1 = (bf16[768,1024]{1,0:T(8,128)(2,1)S(1)}, bf16[768,1024]{1,0:T(8,128)(2,1)}, u32[]{:S(2)}) copy-start(bf16[768,1024]{1,0:T(8,128)(2,1)} %hid.2) | copy-start | bytes 4718596
  66.3 20.7 %collective-permute-start.2 = (bf16[384,1024]{1,0:T(8,128)(2,1)}, bf16[384,1024]{1,0:T(8,128)(2,1)}, u32[]{:S(2)}, u32[]{:S(2)}) collective-permute-start(bf16[384,1024]{1,0:T(8,128)(2,1)} %broadcast_select_fusion.1), channel_id=1, source_target_pairs={{0,4},{8,12},{2,6},{10,14},{33,37},{41,45},{35,39},{43,47},{66,70}... | collective-permute-start | bytes 2359304 | tf_op jit(solution)/shard_map/ppermute | solution.py:199
  83.3 19.8 %all-to-all-start.3 = ((f32[16,8,384]{2,1,0:T(8,128)}), f32[16,8,384]{2,1,0:T(8,128)S(1)}, u32[]{:S(2)}, u32[]{:S(2)}) async-start(f32[16,8,384]{2,1,0:T(8,128)} %broadcast_in_dim.10), calls=%async_computation.3 | async-start | bytes 393216 | tf_op jit(solution)/shard_map/all_to_all | solution.py:29
  89.1 19.9 %collective-permute-start.3 = (bf16[384,1024]{1,0:T(8,128)(2,1)}, bf16[384,1024]{1,0:T(8,128)(2,1)}, u32[]{:S(2)}, u32[]{:S(2)}) collective-permute-start(bf16[384,1024]{1,0:T(8,128)(2,1)} %broadcast_select_fusion.2), channel_id=1, source_target_pairs={{0,1},{8,9},{2,3},{10,11},{4,5},{12,13},{6,7},{14,15},{33,34},{41,... | collective-permute-start | bytes 2359304 | tf_op jit(solution)/shard_map/ppermute | solution.py:199
  93.4 15.6 %copy-start.4 = (bf16[1024,384]{1,0:T(8,128)(2,1)S(1)}, bf16[1024,384]{1,0:T(8,128)(2,1)}, u32[]{:S(2)}) copy-start(bf16[1024,384]{1,0:T(8,128)(2,1)} %act.3) | copy-start | bytes 2359300
  93.4 15.6 %copy-start.7 = (f32[384,384]{1,0:T(8,128)S(1)}, f32[384,384]{1,0:T(8,128)}, u32[]{:S(2)}) copy-start(f32[384,384]{1,0:T(8,128)} %feed.3) | copy-start | bytes 1769476
  104.0 15.3 %all-to-all-start.4 = ((f32[32,8,384]{2,1,0:T(8,128)}), f32[32,8,384]{2,1,0:T(8,128)S(1)}, u32[]{:S(2)}, u32[]{:S(2)}) async-start(f32[32,8,384]{2,1,0:T(8,128)} %shard_map.80), calls=%async_computation.4 | async-start | bytes 786432 | tf_op jit(solution)/shard_map/all_to_all | solution.py:276
  109.0 10.3 %copy-start.9 = (f32[384,384]{1,0:T(8,128)S(1)}, f32[384,384]{1,0:T(8,128)}, u32[]{:S(2)}) copy-start(f32[384,384]{1,0:T(8,128)} %momentum.1) | copy-start | bytes 1769476

commit v5 on v4

--- a/solution.py
+++ b/solution.py
@@ -41,6 +41,7 @@
         out_shape=outs,
         in_specs=[whole] * len(args),
         out_specs=[whole] * len(outs),
+        compiler_params=pltpu.CompilerParams(vmem_limit_bytes=8 * 2**20),
         cost_estimate=pl.CostEstimate(
             flops=int(micros * 1e9), bytes_accessed=size, transcendentals=0
         ),
@@ -69,15 +70,11 @@
     return y
 
 
-def early_kernel(hid, q, feed, err, piece):
-    rows = feed.shape[0]
-    core = lax.axis_index("c")
-    replica = lax.axis_index("z") * lax.axis_size("c") + core
-    own = q[:, pl.ds(pl.multiple_of(replica * rows, rows), rows)]
+def early_kernel(q, feed, act, err, act_out):
     err[...] = jnp.dot(
-        own, feed[...], precision=high, preferred_element_type=jnp.float32
-    )
-    piece[...] = hid[pl.ds(pl.multiple_of(core * rows, rows), rows), :]
+        q[...], feed[...], precision=high, preferred_element_type=jnp.float32
+    )
+    act_out[...] = act[...]
 
 
 def left_kernel(got, act, err, out):
@@ -206,17 +203,20 @@
     token_part = thin_dot(q_block, hidden, ((1,), (0,)))
     f32 = jnp.float32
     act_near, hid_near, feed_near = near(activations), near(hidden), near(feedback)
-    p_err, held = local(
+    q_owned = lax.dynamic_slice_in_dim(q_rows, own_start, cols_dp, 1)
+    p_err, act_near = local(
         early_kernel,
         [
             pltpu.VMEM((rank, width), f32),
-            pltpu.VMEM((cols_dp, toks), hidden.dtype),
+            pltpu.VMEM(activations.shape, activations.dtype),
         ],
         1.5,
-        tie(hid_near, token_part),
-        near(q_rows),
-        feed_near,
-    )
+        near(q_owned),
+        tie(feed_near, token_part),
+        act_near,
+    )
+    hid_late = tie(hidden, p_err)
+    held = lax.dynamic_slice_in_dim(hid_late, core * cols_dp, cols_dp, 0)
     got = send(held, 0)
     tokens = near(copies(token_part, plane, n_mp))
     (p_part,) = local(
@@ -224,8 +224,8 @@
         [pltpu.VMEM((rank, width), f32)],
         1,
         tokens,
-        act_near,
-        p_err,
+        near(act_near),
+        near(p_err),
     )
     p_pair = lax.all_gather(p_part, "c").sum(0)
     held = take(held, tie(got, p_pair), 0)
@@ -242,7 +242,7 @@
         [pltpu.VMEM((n_mp, rank, toks + cols_dp + 128), f32)],
         2,
         near(p_sum),
-        act_near,
+        near(act_near),
         feed_near,
     )
     packed = near(lax.all_to_all(packed, plane, 0, 0))
@@ -254,14 +254,15 @@
         hid_near,
     )
     gram_mat = gram_mat[:, :rank]
-    factor = jnp.linalg.cholesky(gram_mat)
-    inverse = lax.linalg.triangular_solve(
-        factor, jnp.eye(rank, dtype=jnp.float32), left_side=True, lower=True
-    )
     half = lax.all_gather(hid, "c").sum(0)
     half = lax.dynamic_slice_in_dim(half, core * cols_dp, cols_dp, 1)
     held = take(held, tie(got, half), 2)
     got = send(held, 3)
+    gram_mat = tie(gram_mat, half)
+    factor = jnp.linalg.cholesky(gram_mat)
+    inverse = lax.linalg.triangular_solve(
+        factor, jnp.eye(rank, dtype=jnp.float32), left_side=True, lower=True
+    )
     half = near(copies(half, "z", nz))
     (block,) = local(
         block_kernel,
@@ -271,7 +272,7 @@
         near(inverse),
     )
     held = take(held, tie(got, block), 3)
-    own_grad = jnp.dot(held, activations, preferred_element_type=jnp.float32)
+    own_grad = jnp.dot(held, act_near, preferred_element_type=jnp.float32)
     base = lax.optimization_barrier(own_grad + feedback)
     blocks = near(lax.all_to_all(block, ("x", "y", "c"), 0, 0))
     ortho = jnp.dot(inverse, p_sum, precision=high)

time: 122 us -> 121 us (level)
  waiting for transfers between devices: 46.3 us -> 41.7 us
  local copies, waits for them, and re-layouts: 3.6 us -> 6.27 us
    all_to_all x3, waiting for transfers between devices: 28 us -> 23.4 us  [copies(): lax.all_to_all(jnp.broadcast_to(x[None], (count,) + x.shape), axes, 0, 0)]
    dynamic_slice x0 -> x2, local copies, waits for them, and re-layouts: none -> 1.67 us  [the longest x1 0.95 us: per_device(): held = lax.dynamic_slice_in_dim(hid_late, core * cols_dp, cols_dp, 0)]
  transfers between devices with their start and end apart: 9 -> 9, of which waited for: 5 -> 5; matrix products, arithmetic and copies ran while one was open for 10% -> 11% of each run, Pallas kernels for 4% -> 4%
where the time goes in v5:
time: 121 us; the launch traced here: 120 us
  waiting for transfers between devices  41.7 us (34%)
  starting transfers between devices  40.1 us (33%)
  blocking collectives  11.2 us (9%)
  other arithmetic  8.92 us (7%)
  Pallas kernels  6.77 us (6%)
  local copies, waits for them, and re-layouts  6.27 us (5%)
  matrix products  3.88 us (3%)
    all_to_all x3, starting transfers between devices, copies(): lax.all_to_all(jnp.broadcast_to(x[None], (count,) + x.shape), axes, 0, 0)  25.1 us
    all_to_all x3, waiting for transfers between devices, copies(): lax.all_to_all(jnp.broadcast_to(x[None], (count,) + x.shape), axes, 0, 0)  23.4 us
    all_to_all x1, waiting for transfers between devices, per_device(): packed = near(lax.all_to_all(packed, plane, 0, 0))  9.91 us
    all_to_all x1, waiting for transfers between devices, per_device(): blocks = near(lax.all_to_all(block, ('x', 'y', 'c'), 0, 0))  8.46 us
    pallas_call x6, Pallas kernels, local(): pl.pallas_call(kernel, out_shape=outs, in_specs=[whole] * len(args), out_...  6.77 us
    ppermute x4, starting transfers between devices, send(): return lax.ppermute(held, ('z', 'c', 'x', 'y'), rounds[k])  6.54 us
    select_n x3, other arithmetic, take(): return jnp.where(turn == k, got, held)  5.48 us
    all_to_all x1, starting transfers between devices, per_device(): blocks = near(lax.all_to_all(block, ('x', 'y', 'c'), 0, 0))  4.84 us
  transfers between devices with their start and end apart: 9, of which 5 were waited for; matrix products, arithmetic and copies ran while one was open for 11% of the time, Pallas kernels for 4%

profile of v5, /device:TPU:33, one launch (start us, length us, event | category | flops | bytes accessed | tf_op | source)
XLA Modules:
  0.0 119.7 jit_solution(8861419542986829161)
XLA Ops:
  1.4 1.8 %fusion.2 = f32[24,1024]{1,0:T(8,128)S(1)} fusion(bf16[768,1024]{1,0:T(8,128)(2,1)} %hid.1, bf16[8,768]{1,0:T(8,128)(2,1)S(1)} %get-tuple-element.30, bf16[8,768]{1,0:T(8,128)(2,1)S(1)} %get-tuple-element.31, bf16[8,768]{1,0:T(8,128)(2,1)S(1)} %get-tuple-element.29), kind=kOutput, calls=%fused_computation.7 | convolution fusion | flops 37859328 | bytes 1708032 | tf_op jit(solution)/shard_map/dot_general | solution.py:21
  4.0 6.8 %all-to-all-start = ((f32[16,8,1024]{2,1,0:T(8,128)}), f32[16,8,1024]{2,1,0:T(8,128)}, u32[]{:S(2)}, u32[]{:S(2)}) async-start(f32[16,8,1024]{2,1,0:T(8,128)} %broadcast_in_dim.7), calls=%async_computation | async-start | bytes 1048576 | tf_op jit(solution)/shard_map/all_to_all | solution.py:29
  15.1 1.5 %collective-permute-start = (bf16[384,1024]{1,0:T(8,128)(2,1)}, bf16[384,1024]{1,0:T(8,128)(2,1)}, u32[]{:S(2)}, u32[]{:S(2)}) collective-permute-start(bf16[384,1024]{1,0:T(8,128)(2,1)} %constant_dynamic-slice_fusion), channel_id=1, source_target_pairs={{0,8},{33,41},{66,74},{99,107},{132,140},{165,173},{198,206},{231,... | collective-permute-start | bytes 2359304 | tf_op jit(solution)/shard_map/ppermute | solution.py:196
  16.6 4.6 %all-to-all-done.got = f32[16,8,1024]{2,1,0:T(8,128)} async-done(((f32[16,8,1024]{2,1,0:T(8,128)}), f32[16,8,1024]{2,1,0:T(8,128)}, u32[]{:S(2)}, u32[]{:S(2)}) %all-to-all-start) | async-done | bytes 524320 | tf_op jit(solution)/shard_map/all_to_all | solution.py:29
  21.2 1.3 %shard_map.77 = f32[8,384]{1,0:T(8,128)S(1)} custom-call(f32[16,8,1024]{2,1,0:T(8,128)} %all-to-all-done.got, bf16[1024,384]{1,0:T(8,128)(2,1)S(1)} %get-tuple-element.17.act, f32[8,384]{1,0:T(8,128)S(1)} %get-tuple-element.18.err), custom_call_target="tpu_custom_call" | custom-call | flops 1000000000 | bytes 1323008 | tf_op jit(solution)/shard_map/pallas_call | solution.py:39
  22.5 3.6 %all-gather = f32[16,384]{1,0:T(8,128)S(1)} all-gather(f32[8,384]{1,0:T(8,128)S(1)} %shard_map.77), channel_id=2, replica_groups=mesh['z'=16,'c'=2,'x'=4,'y'=4] {'c'}, dimensions={0}, use_global_device_ids=true | all-gather | bytes 36864 | tf_op jit(solution)/shard_map/all_gather | solution.py:230
  26.8 14.7 %all-to-all-start.1 = ((f32[16,4,384]{2,1,0:T(4,128)}), f32[16,4,384]{2,1,0:T(4,128)S(1)}, u32[]{:S(2)}, u32[]{:S(2)}) async-start(f32[16,4,384]{2,1,0:T(4,128)} %broadcast_in_dim.8), calls=%async_computation.1 | async-start | bytes 196608 | tf_op jit(solution)/shard_map/all_to_all | solution.py:29
  42.7 1.5 %collective-permute-start.1 = (bf16[384,1024]{1,0:T(8,128)(2,1)}, bf16[384,1024]{1,0:T(8,128)(2,1)}, u32[]{:S(2)}, u32[]{:S(2)}) collective-permute-start(bf16[384,1024]{1,0:T(8,128)(2,1)} %broadcast_select_fusion), channel_id=1, source_target_pairs={{0,2},{8,10},{33,35},{41,43},{66,64},{74,72},{99,97},{107,105},{13... | collective-permute-start | bytes 2359304 | tf_op jit(solution)/shard_map/ppermute | solution.py:196
  44.2 9.1 %all-to-all-done.1 = f32[16,4,384]{2,1,0:T(4,128)S(1)} async-done(((f32[16,4,384]{2,1,0:T(4,128)}), f32[16,4,384]{2,1,0:T(4,128)S(1)}, u32[]{:S(2)}, u32[]{:S(2)}) %all-to-all-start.1) | async-done | bytes 98336 | tf_op jit(solution)/shard_map/all_to_all | solution.py:29
  53.4 3.8 %all-gather.2 = f32[2,4,384]{2,1,0:T(4,128)S(1)} all-gather(f32[1,4,384]{2,1,0:T(4,128)S(1)} %bitcast.29), channel_id=1, replica_groups=mesh['z'=16,'c'=2,'x'=4,'y'=4] {'c'}, dimensions={0}, use_global_device_ids=true | all-gather | bytes 18432 | tf_op jit(solution)/shard_map/all_gather | solution.py:238
  57.2 1.8 %shard_map.78 = f32[16,8,1536]{2,1,0:T(8,128)} custom-call(f32[8,384]{1,0:T(8,128)S(1)} %reshape.21.p_ref, bf16[1024,384]{1,0:T(8,128)(2,1)S(1)} %get-tuple-element.17.act, f32[384,384]{1,0:T(8,128)S(1)} %copy-done.1), custom_call_target="tpu_custom_call" | custom-call | flops 2000000000 | bytes 1388544 | tf_op jit(solution)/shard_map/pallas_call | solution.py:39
  59.0 3.6 %all-to-all-start.2 = ((f32[16,8,1536]{2,1,0:T(8,128)}), f32[16,8,1536]{2,1,0:T(8,128)S(1)}, u32[]{:S(2)}, u32[]{:S(2)}) async-start(f32[16,8,1536]{2,1,0:T(8,128)} %shard_map.78), calls=%async_computation.2 | async-start | bytes 1572864 | tf_op jit(solution)/shard_map/all_to_all | solution.py:248
  62.6 2.1 %broadcast_select_fusion.1 = bf16[384,1024]{1,0:T(8,128)(2,1)} fusion(bf16[384,1024]{1,0:T(8,128)(2,1)} %collective-permute-done.1, bf16[384,1024]{1,0:T(8,128)(2,1)} %broadcast_select_fusion, pred[]{:T(512)S(6)} %eq.34), kind=kLoop, calls=%fused_computation.3 | loop fusion | flops 393216 | bytes 2359297 | tf_op jit(solution)/shard_map/jit(_where)/select_n | solution.py:199
  64.8 1.3 %collective-permute-start.2 = (bf16[384,1024]{1,0:T(8,128)(2,1)}, bf16[384,1024]{1,0:T(8,128)(2,1)}, u32[]{:S(2)}, u32[]{:S(2)}) collective-permute-start(bf16[384,1024]{1,0:T(8,128)(2,1)} %broadcast_select_fusion.1), channel_id=1, source_target_pairs={{0,4},{8,12},{2,6},{10,14},{33,37},{41,45},{35,39},{43,47},{66,70}... | collective-permute-start | bytes 2359304 | tf_op jit(solution)/shard_map/ppermute | solution.py:196
  66.1 9.9 %all-to-all-done.2.got = f32[16,8,1536]{2,1,0:T(8,128)S(1)} async-done(((f32[16,8,1536]{2,1,0:T(8,128)}), f32[16,8,1536]{2,1,0:T(8,128)S(1)}, u32[]{:S(2)}, u32[]{:S(2)}) %all-to-all-start.2) | async-done | bytes 786464 | tf_op jit(solution)/shard_map/all_to_all | solution.py:248
  76.6 3.7 %all-gather.1 = f32[16,768]{1,0:T(8,128)S(1)} all-gather(f32[8,768]{1,0:T(8,128)S(1)} %get-tuple-element.19), channel_id=3, replica_groups=mesh['z'=16,'c'=2,'x'=4,'y'=4] {'c'}, dimensions={0}, use_global_device_ids=true | all-gather | bytes 73728 | tf_op jit(solution)/shard_map/all_gather | solution.py:257
  81.9 3.7 %all-to-all-start.3 = ((f32[16,8,384]{2,1,0:T(8,128)}), f32[16,8,384]{2,1,0:T(8,128)S(1)}, u32[]{:S(2)}, u32[]{:S(2)}) async-start(f32[16,8,384]{2,1,0:T(8,128)} %broadcast_in_dim.10), calls=%async_computation.3 | async-start | bytes 393216 | tf_op jit(solution)/shard_map/all_to_all | solution.py:29
  85.6 2.1 %broadcast_select_fusion.2 = bf16[384,1024]{1,0:T(8,128)(2,1)} fusion(bf16[384,1024]{1,0:T(8,128)(2,1)} %collective-permute-done.2, bf16[384,1024]{1,0:T(8,128)(2,1)} %broadcast_select_fusion.1, pred[]{:T(512)S(6)} %eq.33), kind=kLoop, calls=%fused_computation.4 | loop fusion | flops 393216 | bytes 2359297 | tf_op jit(solution)/shard_map/jit(_where)/select_n | solution.py:199
  87.7 2.2 %collective-permute-start.3 = (bf16[384,1024]{1,0:T(8,128)(2,1)}, bf16[384,1024]{1,0:T(8,128)(2,1)}, u32[]{:S(2)}, u32[]{:S(2)}) collective-permute-start(bf16[384,1024]{1,0:T(8,128)(2,1)} %broadcast_select_fusion.2), channel_id=1, source_target_pairs={{0,1},{8,9},{2,3},{10,11},{4,5},{12,13},{6,7},{14,15},{33,34},{41,... | collective-permute-start | bytes 2359304 | tf_op jit(solution)/shard_map/ppermute | solution.py:196
  92.0 9.7 %all-to-all-done.3.got = f32[16,8,384]{2,1,0:T(8,128)S(1)} async-done(((f32[16,8,384]{2,1,0:T(8,128)}), f32[16,8,384]{2,1,0:T(8,128)S(1)}, u32[]{:S(2)}, u32[]{:S(2)}) %all-to-all-start.3) | async-done | bytes 196640 | tf_op jit(solution)/shard_map/all_to_all | solution.py:29
  102.6 4.8 %all-to-all-start.4 = ((f32[32,8,384]{2,1,0:T(8,128)}), f32[32,8,384]{2,1,0:T(8,128)S(1)}, u32[]{:S(2)}, u32[]{:S(2)}) async-start(f32[32,8,384]{2,1,0:T(8,128)} %shard_map.80), calls=%async_computation.4 | async-start | bytes 786432 | tf_op jit(solution)/shard_map/all_to_all | solution.py:277
  107.6 1.8 %convolution_add_fusion.base = f32[384,384]{1,0:T(8,128)S(1)} fusion(f32[384,384]{1,0:T(8,128)S(1)} %copy-done.2, bf16[1024,384]{1,0:T(8,128)(2,1)S(1)} %get-tuple-element.17.act, bf16[384,1024]{1,0:T(8,128)(2,1)} %collective-permute-done.3, bf16[384,1024]{1,0:T(8,128)(2,1)} %broadcast_select_fusion.2, pred[]{:T(512)S(6)} %eq.32), kind=kOutput, calls=%fused_computation | convolution fusion | flops 302530560 | bytes 3538945 | tf_op jit(solution)/shard_map/dot_general | solution.py:275
  109.4 8.5 %all-to-all-done.4.blocks = f32[32,8,384]{2,1,0:T(8,128)S(1)} async-done(((f32[32,8,384]{2,1,0:T(8,128)}), f32[32,8,384]{2,1,0:T(8,128)S(1)}, u32[]{:S(2)}, u32[]{:S(2)}) %all-to-all-start.4) | async-done | bytes 393248 | tf_op jit(solution)/shard_map/all_to_all | solution.py:277
  117.8 1.8 %shard_map.81 = (f32[384,384]{1,0:T(8,128)}, f32[384,384]{1,0:T(8,128)}, f32[8,12288]{1,0:T(8,128)}) custom-call(f32[32,8,384]{2,1,0:T(8,128)S(1)} %all-to-all-done.4.blocks, f32[8,384]{1,0:T(8,128)S(1)} %fusion.14.ortho, f32[384,384]{1,0:T(8,128)S(1)} %convolution_add_fusion.base, f32[384,384]{1,0:T(8,128)S(1)} %copy-done.4), custom_call_target="tpu_custom_call" | custom-call | flops 2000000000 | bytes 1585152 | tf_op jit(solution)/shard_map/pallas_call | solution.py:39
  (42 shorter events, 13.1 us)
Async XLA Ops:
  1.4 10.2 %copy-start.1 = (f32[384,384]{1,0:T(8,128)S(1)}, f32[384,384]{1,0:T(8,128)}, u32[]{:S(2)}) copy-start(f32[384,384]{1,0:T(8,128)} %feed.2) | copy-start | bytes 1769476
  4.0 17.2 %all-to-all-start = ((f32[16,8,1024]{2,1,0:T(8,128)}), f32[16,8,1024]{2,1,0:T(8,128)}, u32[]{:S(2)}, u32[]{:S(2)}) async-start(f32[16,8,1024]{2,1,0:T(8,128)} %broadcast_in_dim.7), calls=%async_computation | async-start | bytes 1048576 | tf_op jit(solution)/shard_map/all_to_all | solution.py:29
  11.6 1.1 copy-start.3
  12.7 1.4 %copy-start = (bf16[768,1024]{1,0:T(8,128)(2,1)S(1)}, bf16[768,1024]{1,0:T(8,128)(2,1)}, u32[]{:S(2)}) copy-start(bf16[768,1024]{1,0:T(8,128)(2,1)} %hid.1) | copy-start | bytes 4718596
  15.1 26.4 %collective-permute-start = (bf16[384,1024]{1,0:T(8,128)(2,1)}, bf16[384,1024]{1,0:T(8,128)(2,1)}, u32[]{:S(2)}, u32[]{:S(2)}) collective-permute-start(bf16[384,1024]{1,0:T(8,128)(2,1)} %constant_dynamic-slice_fusion), channel_id=1, source_target_pairs={{0,8},{33,41},{66,74},{99,107},{132,140},{165,173},{198,206},{231,... | collective-permute-start | bytes 2359304 | tf_op jit(solution)/shard_map/ppermute | solution.py:196
  26.8 26.5 %all-to-all-start.1 = ((f32[16,4,384]{2,1,0:T(4,128)}), f32[16,4,384]{2,1,0:T(4,128)S(1)}, u32[]{:S(2)}, u32[]{:S(2)}) async-start(f32[16,4,384]{2,1,0:T(4,128)} %broadcast_in_dim.8), calls=%async_computation.1 | async-start | bytes 196608 | tf_op jit(solution)/shard_map/all_to_all | solution.py:29
  42.7 19.9 %collective-permute-start.1 = (bf16[384,1024]{1,0:T(8,128)(2,1)}, bf16[384,1024]{1,0:T(8,128)(2,1)}, u32[]{:S(2)}, u32[]{:S(2)}) collective-permute-start(bf16[384,1024]{1,0:T(8,128)(2,1)} %broadcast_select_fusion), channel_id=1, source_target_pairs={{0,2},{8,10},{33,35},{41,43},{66,64},{74,72},{99,97},{107,105},{13... | collective-permute-start | bytes 2359304 | tf_op jit(solution)/shard_map/ppermute | solution.py:196
  59.0 17.0 %all-to-all-start.2 = ((f32[16,8,1536]{2,1,0:T(8,128)}), f32[16,8,1536]{2,1,0:T(8,128)S(1)}, u32[]{:S(2)}, u32[]{:S(2)}) async-start(f32[16,8,1536]{2,1,0:T(8,128)} %shard_map.78), calls=%async_computation.2 | async-start | bytes 1572864 | tf_op jit(solution)/shard_map/all_to_all | solution.py:248
  64.8 20.8 %collective-permute-start.2 = (bf16[384,1024]{1,0:T(8,128)(2,1)}, bf16[384,1024]{1,0:T(8,128)(2,1)}, u32[]{:S(2)}, u32[]{:S(2)}) collective-permute-start(bf16[384,1024]{1,0:T(8,128)(2,1)} %broadcast_select_fusion.1), channel_id=1, source_target_pairs={{0,4},{8,12},{2,6},{10,14},{33,37},{41,45},{35,39},{43,47},{66,70}... | collective-permute-start | bytes 2359304 | tf_op jit(solution)/shard_map/ppermute | solution.py:196
  81.9 19.8 %all-to-all-start.3 = ((f32[16,8,384]{2,1,0:T(8,128)}), f32[16,8,384]{2,1,0:T(8,128)S(1)}, u32[]{:S(2)}, u32[]{:S(2)}) async-start(f32[16,8,384]{2,1,0:T(8,128)} %broadcast_in_dim.10), calls=%async_computation.3 | async-start | bytes 393216 | tf_op jit(solution)/shard_map/all_to_all | solution.py:29
  87.7 19.9 %collective-permute-start.3 = (bf16[384,1024]{1,0:T(8,128)(2,1)}, bf16[384,1024]{1,0:T(8,128)(2,1)}, u32[]{:S(2)}, u32[]{:S(2)}) collective-permute-start(bf16[384,1024]{1,0:T(8,128)(2,1)} %broadcast_select_fusion.2), channel_id=1, source_target_pairs={{0,1},{8,9},{2,3},{10,11},{4,5},{12,13},{6,7},{14,15},{33,34},{41,... | collective-permute-start | bytes 2359304 | tf_op jit(solution)/shard_map/ppermute | solution.py:196
  92.0 15.6 %copy-start.2 = (f32[384,384]{1,0:T(8,128)S(1)}, f32[384,384]{1,0:T(8,128)}, u32[]{:S(2)}) copy-start(f32[384,384]{1,0:T(8,128)} %feed.2) | copy-start | bytes 1769476
  102.6 15.3 %all-to-all-start.4 = ((f32[32,8,384]{2,1,0:T(8,128)}), f32[32,8,384]{2,1,0:T(8,128)S(1)}, u32[]{:S(2)}, u32[]{:S(2)}) async-start(f32[32,8,384]{2,1,0:T(8,128)} %shard_map.80), calls=%async_computation.4 | async-start | bytes 786432 | tf_op jit(solution)/shard_map/all_to_all | solution.py:277
  107.5 10.3 %copy-start.4 = (f32[384,384]{1,0:T(8,128)S(1)}, f32[384,384]{1,0:T(8,128)}, u32[]{:S(2)}) copy-start(f32[384,384]{1,0:T(8,128)} %momentum.1) | copy-start | bytes 1769476

commit v6 on v5

--- a/solution.py
+++ b/solution.py
@@ -7,22 +7,6 @@
 
 decay_rate = 0.9
 high = lax.Precision.HIGHEST
-
-
-def split_parts(x):
-    a = lax.reduce_precision(x, 8, 7)
-    r = x - a
-    b = lax.reduce_precision(r, 8, 7)
-    c = r - b
-    return jnp.concatenate([a, b, c], 0).astype(jnp.bfloat16)
-
-
-def thin_dot(x, wide, dims):
-    y = lax.dot_general(
-        split_parts(x), wide, (dims, ((), ())), preferred_element_type=jnp.float32
-    )
-    r = x.shape[0]
-    return (y[2 * r :] + y[r : 2 * r]) + y[:r]
 
 
 def copies(x, axes, count):
@@ -41,23 +25,16 @@
         out_shape=outs,
         in_specs=[whole] * len(args),
         out_specs=[whole] * len(outs),
-        compiler_params=pltpu.CompilerParams(vmem_limit_bytes=8 * 2**20),
+        compiler_params=pltpu.CompilerParams(vmem_limit_bytes=4 * 2**20),
         cost_estimate=pl.CostEstimate(
-            flops=int(micros * 1e9), bytes_accessed=size, transcendentals=0
+            flops=int(micros * 4e9), bytes_accessed=size, transcendentals=0
         ),
     )(*args)
 
 
 def exact_dot(x, wide, dims):
-    a = x.astype(jnp.bfloat16).astype(jnp.float32)
-    r = x - a
-    b = r.astype(jnp.bfloat16).astype(jnp.float32)
-    parts = jnp.concatenate([a, b, r - b, jnp.zeros_like(x)], 0)
     y = lax.dot_general(
-        parts.astype(jnp.bfloat16),
-        wide,
-        (dims, ((), ())),
-        preferred_element_type=jnp.float32,
+        parts_of(x), wide, (dims, ((), ())), preferred_element_type=jnp.float32
     )
     n = x.shape[0]
     return (y[2 * n : 3 * n] + y[n : 2 * n]) + y[:n]
@@ -70,11 +47,57 @@
     return y
 
 
-def early_kernel(q, feed, act, err, act_out):
+def parts_of(x):
+    a = x.astype(jnp.bfloat16).astype(jnp.float32)
+    r = x - a
+    b = r.astype(jnp.bfloat16).astype(jnp.float32)
+    return jnp.concatenate([a, b, r - b, jnp.zeros_like(x)], 0).astype(jnp.bfloat16)
+
+
+def start_kernel(q, hid, out, q_own, piece_out, q_near, held, row, sems, done):
+    rows, own_rows = hid.shape[0], q_own.shape[1]
+    count = sems.shape[0] - 2
+    step = rows // count
+    shard = lax.axis_index("x") * lax.axis_size("y") + lax.axis_index("y")
+    replica = lax.axis_index("z") * lax.axis_size("c") + lax.axis_index("c")
+    mine = q.at[:, pl.ds(pl.multiple_of(shard * rows, rows), rows)]
+    own = q.at[:, pl.ds(pl.multiple_of(replica * own_rows, own_rows), own_rows)]
+    first = pltpu.make_async_copy(mine, q_near, sems.at[count])
+    last = pltpu.make_async_copy(own, q_own, sems.at[count + 1])
+    loads = []
+    for i in range(count):
+        piece = pl.ds(i * step, step)
+        loads.append(pltpu.make_async_copy(hid.at[piece], held.at[piece], sems.at[i]))
+    for load in [first] + loads + [last]:
+        load.start()
+    first.wait()
+    parts = parts_of(q_near[...])
+    y = jnp.zeros((parts.shape[0], hid.shape[1]), jnp.float32)
+    for i in range(count):
+        loads[i].wait()
+        y = y + jnp.dot(
+            parts[:, i * step : (i + 1) * step],
+            held[i * step : (i + 1) * step, :],
+            preferred_element_type=jnp.float32,
+        )
+    n = row.shape[0]
+    row[...] = (y[2 * n : 3 * n] + y[n : 2 * n]) + y[:n]
+    sends = [
+        pltpu.make_async_copy(row, out.at[i], done.at[i]) for i in range(out.shape[0])
+    ]
+    for send in sends:
+        send.start()
+    core = lax.axis_index("c")
+    piece_out[...] = held[pl.ds(pl.multiple_of(core * own_rows, own_rows), own_rows), :]
+    last.wait()
+    for send in sends:
+        send.wait()
+
+
+def early_kernel(q, feed, err):
     err[...] = jnp.dot(
         q[...], feed[...], precision=high, preferred_element_type=jnp.float32
     )
-    act_out[...] = act[...]
 
 
 def left_kernel(got, act, err, out):
@@ -125,21 +148,39 @@
         out[i] = block
 
 
-def last_kernel(blocks, ortho, base, momentum, feed_out, mom_out, q_out):
+def last_kernel(
+    blocks, ortho, base, momentum, feed_out, mom_out, q_out, feed_new, mom_new, sems
+):
     count, _, rows = blocks.shape
+    sends = []
+    for i in range(count):
+        there = q_out.at[:, pl.ds(i * rows, rows)]
+        sends.append(pltpu.make_async_copy(blocks.at[i], there, sems.at[i]))
+    for send in sends:
+        send.start()
     replica = lax.axis_index("z") * lax.axis_size("c") + lax.axis_index("c")
     mine = blocks[replica]
-    approx = lax.dot_general(
-        mine,
-        ortho[...],
-        (((0,), (0,)), ((), ())),
-        precision=high,
-        preferred_element_type=jnp.float32,
-    )
-    feed_out[...] = base[...] - approx
-    mom_out[...] = decay_rate * momentum[...] + approx
-    for i in range(count):
-        q_out[:, i * rows : (i + 1) * rows] = blocks[i]
+    part = feed_new.shape[0] // 3
+    for i in range(3):
+        piece = slice(i * part, (i + 1) * part)
+        approx = lax.dot_general(
+            mine[:, piece],
+            ortho[...],
+            (((0,), (0,)), ((), ())),
+            precision=high,
+            preferred_element_type=jnp.float32,
+        )
+        feed_new[piece] = base[piece] - approx
+        mom_new[piece] = decay_rate * momentum[piece] + approx
+        for j, (here, there) in enumerate(((feed_new, feed_out), (mom_new, mom_out))):
+            span = pl.ds(i * part, part)
+            send = pltpu.make_async_copy(
+                here.at[span], there.at[span], sems.at[count + 2 * i + j]
+            )
+            send.start()
+            sends.append(send)
+    for send in sends:
+        send.wait()
 
 
 def tie(x, after):
@@ -199,26 +240,45 @@
         return jnp.where(turn == k, got, held)
 
     q_rows = q_start.T
-    q_block = lax.dynamic_slice_in_dim(q_rows, shard * cols_mp, cols_mp, 1)
-    token_part = thin_dot(q_block, hidden, ((1,), (0,)))
     f32 = jnp.float32
-    act_near, hid_near, feed_near = near(activations), near(hidden), near(feedback)
-    q_owned = lax.dynamic_slice_in_dim(q_rows, own_start, cols_dp, 1)
-    p_err, act_near = local(
+    whole = pl.BlockSpec(memory_space=pltpu.VMEM)
+    far = pl.BlockSpec(memory_space=pltpu.HBM)
+    token_part, q_owned, held = pl.pallas_call(
+        start_kernel,
+        out_shape=[
+            pltpu.HBM((n_mp, rank, toks), f32),
+            pltpu.VMEM((rank, cols_dp), f32),
+            pltpu.VMEM((cols_dp, toks), hidden.dtype),
+        ],
+        in_specs=[far] * 2,
+        out_specs=[far, whole, whole],
+        scratch_shapes=[
+            pltpu.VMEM((rank, cols_mp), f32),
+            pltpu.VMEM(hidden.shape, hidden.dtype),
+            pltpu.VMEM((rank, toks), f32),
+            pltpu.SemaphoreType.DMA((8,)),
+            pltpu.SemaphoreType.DMA((n_mp,)),
+        ],
+        compiler_params=pltpu.CompilerParams(vmem_limit_bytes=4 * 2**20),
+        cost_estimate=pl.CostEstimate(
+            flops=2 * 10**9, bytes_accessed=3 * 10**6, transcendentals=0
+        ),
+    )(
+        pltpu.with_memory_space_constraint(q_rows, pltpu.HBM),
+        pltpu.with_memory_space_constraint(hidden, pltpu.HBM),
+    )
+    feed_near = near(feedback)
+    act_near = activations
+    (p_err,) = local(
         early_kernel,
-        [
-            pltpu.VMEM((rank, width), f32),
-            pltpu.VMEM(activations.shape, activations.dtype),
-        ],
+        [pltpu.VMEM((rank, width), f32)],
         1.5,
         near(q_owned),
-        tie(feed_near, token_part),
-        act_near,
-    )
-    hid_late = tie(hidden, p_err)
-    held = lax.dynamic_slice_in_dim(hid_late, core * cols_dp, cols_dp, 0)
+        feed_near,
+    )
+    held = tie(held, p_err)
     got = send(held, 0)
-    tokens = near(copies(token_part, plane, n_mp))
+    tokens = near(lax.all_to_all(token_part, plane, 0, 0))
     (p_part,) = local(
         left_kernel,
         [pltpu.VMEM((rank, width), f32)],
@@ -251,14 +311,14 @@
         [pltpu.VMEM((rank, cols_mp), f32), pltpu.VMEM((rank, 128), f32)],
         1,
         packed,
-        hid_near,
+        near(hidden),
     )
     gram_mat = gram_mat[:, :rank]
     half = lax.all_gather(hid, "c").sum(0)
     half = lax.dynamic_slice_in_dim(half, core * cols_dp, cols_dp, 1)
     held = take(held, tie(got, half), 2)
     got = send(held, 3)
-    gram_mat = tie(gram_mat, half)
+    gram_mat = tie(gram_mat, held)
     factor = jnp.linalg.cholesky(gram_mat)
     inverse = lax.linalg.triangular_solve(
         factor, jnp.eye(rank, dtype=jnp.float32), left_side=True, lower=True
@@ -276,19 +336,25 @@
     base = lax.optimization_barrier(own_grad + feedback)
     blocks = near(lax.all_to_all(block, ("x", "y", "c"), 0, 0))
     ortho = jnp.dot(inverse, p_sum, precision=high)
-    new_feedback, new_momentum, q_next = local(
+    new_feedback, new_momentum, q_next = pl.pallas_call(
         last_kernel,
-        [
-            jax.ShapeDtypeStruct(feedback.shape, f32),
-            jax.ShapeDtypeStruct(momentum.shape, f32),
-            jax.ShapeDtypeStruct(q_rows.shape, f32),
+        out_shape=[
+            pltpu.HBM(feedback.shape, f32),
+            pltpu.HBM(momentum.shape, f32),
+            pltpu.HBM(q_rows.shape, f32),
         ],
-        2,
-        blocks,
-        near(ortho),
-        near(base),
-        near(momentum),
-    )
+        in_specs=[whole] * 4,
+        out_specs=[far] * 3,
+        scratch_shapes=[
+            pltpu.VMEM(feedback.shape, f32),
+            pltpu.VMEM(momentum.shape, f32),
+            pltpu.SemaphoreType.DMA((n_dp + 6,)),
+        ],
+        compiler_params=pltpu.CompilerParams(vmem_limit_bytes=4 * 2**20),
+        cost_estimate=pl.CostEstimate(
+            flops=2 * 10**9, bytes_accessed=3 * 10**6, transcendentals=0
+        ),
+    )(blocks, near(ortho), near(base), near(momentum))
     return (new_feedback, new_momentum, q_next.T)
 
 

time: 121 us -> 119 us (0.983)
  waiting for transfers between devices: 41.7 us -> 46.6 us
  local copies, waits for them, and re-layouts: 6.27 us -> 2.97 us
  other arithmetic: 8.92 us -> 6.14 us
  matrix products: 3.88 us -> 2.1 us
  Pallas kernels: 6.77 us -> 8.29 us
    all_to_all x0 -> x1, waiting for transfers between devices: none -> 8.34 us  [per_device(): tokens = near(lax.all_to_all(token_part, plane, 0, 0))]
    all_to_all x3 -> x2, starting transfers between devices: 25.1 us -> 18.3 us  [copies(): lax.all_to_all(jnp.broadcast_to(x[None], (count,) + x.shape), axes, 0, 0)]
    all_to_all x0 -> x1, starting transfers between devices: none -> 6.77 us  [per_device(): tokens = near(lax.all_to_all(token_part, plane, 0, 0))]
    all_to_all x3 -> x2, waiting for transfers between devices: 23.4 us -> 18.9 us  [copies(): lax.all_to_all(jnp.broadcast_to(x[None], (count,) + x.shape), axes, 0, 0)]
    pallas_call x0 -> x2, Pallas kernels: none -> 4.42 us  [the longest x1 2.63 us: per_device(): pl.pallas_call(start_kernel, out_shape=[pltpu.HBM((n_mp, rank, toks), f32...]
    pallas_call x6 -> x5, Pallas kernels: 6.77 us -> 3.87 us  [local(): pl.pallas_call(kernel, out_shape=outs, in_specs=[whole] * len(args), out_...]
    select_n x3, other arithmetic: 5.48 us -> 3.43 us  [take(): return jnp.where(turn == k, got, held)]
    dot_general x1 -> x0, matrix products: 1.79 us -> none  [thin_dot(): lax.dot_general(split_parts(x), wide, (dims, ((), ())), preferred_element...]
  transfers between devices with their start and end apart: 9 -> 9, of which waited for: 5 -> 5; matrix products, arithmetic and copies ran while one was open for 11% -> 8% of each run, Pallas kernels for 4% -> 3%
where the time goes in v6:
time: 119 us; the launch traced here: 118 us
  waiting for transfers between devices  46.6 us (39%)
  starting transfers between devices  40.2 us (34%)
  blocking collectives  11.2 us (9%)
  Pallas kernels  8.29 us (7%)
  other arithmetic  6.14 us (5%)
  local copies, waits for them, and re-layouts  2.97 us (2%)
  matrix products  2.1 us (2%)
    all_to_all x2, waiting for transfers between devices, copies(): lax.all_to_all(jnp.broadcast_to(x[None], (count,) + x.shape), axes, 0, 0)  18.9 us
    all_to_all x2, starting transfers between devices, copies(): lax.all_to_all(jnp.broadcast_to(x[None], (count,) + x.shape), axes, 0, 0)  18.3 us
    all_to_all x1, waiting for transfers between devices, per_device(): packed = near(lax.all_to_all(packed, plane, 0, 0))  10.8 us
    all_to_all x1, waiting for transfers between devices, per_device(): blocks = near(lax.all_to_all(block, ('x', 'y', 'c'), 0, 0))  8.47 us
    all_to_all x1, waiting for transfers between devices, per_device(): tokens = near(lax.all_to_all(token_part, plane, 0, 0))  8.34 us
    all_to_all x1, starting transfers between devices, per_device(): tokens = near(lax.all_to_all(token_part, plane, 0, 0))  6.77 us
    ppermute x4, starting transfers between devices, send(): return lax.ppermute(held, ('z', 'c', 'x', 'y'), rounds[k])  6.6 us
    all_to_all x1, starting transfers between devices, per_device(): blocks = near(lax.all_to_all(block, ('x', 'y', 'c'), 0, 0))  4.84 us
  transfers between devices with their start and end apart: 9, of which 5 were waited for; matrix products, arithmetic and copies ran while one was open for 8% of the time, Pallas kernels for 3%

profile of v6, /device:TPU:33, one launch (start us, length us, event | category | flops | bytes accessed | tf_op | source)
XLA Modules:
  0.0 118.2 jit_solution(3309289406699256675)
XLA Ops:
  0.6 2.6 %shard_map.76 = (f32[16,8,1024]{2,1,0:T(8,128)}, f32[8,384]{1,0:T(8,128)S(1)}, bf16[384,1024]{1,0:T(8,128)(2,1)S(1)}) custom-call(f32[8,12288]{1,0:T(8,128)} %bitcast.21, bf16[768,1024]{1,0:T(8,128)(2,1)} %hid.3), custom_call_target="tpu_custom_call" | custom-call | flops 2000000000 | bytes 3000000 | tf_op jit(solution)/shard_map/pallas_call | solution.py:246
  3.3 6.8 %all-to-all-start = ((f32[16,8,1024]{2,1,0:T(8,128)}), f32[16,8,1024]{2,1,0:T(8,128)S(1)}, u32[]{:S(2)}, u32[]{:S(2)}) async-start(f32[16,8,1024]{2,1,0:T(8,128)} %get-tuple-element.16), calls=%async_computation | async-start | bytes 1048576 | tf_op jit(solution)/shard_map/all_to_all | solution.py:281
  10.5 1.6 %collective-permute-start = (bf16[384,1024]{1,0:T(8,128)(2,1)S(1)}, bf16[384,1024]{1,0:T(8,128)(2,1)}, u32[]{:S(2)}, u32[]{:S(2)}) collective-permute-start(bf16[384,1024]{1,0:T(8,128)(2,1)S(1)} %get-tuple-element.21), channel_id=1, source_target_pairs={{0,8},{33,41},{66,74},{99,107},{132,140},{165,173},{198,206},{231,... | collective-permute-start | bytes 2359304 | tf_op jit(solution)/shard_map/ppermute | solution.py:237
  12.0 8.3 %all-to-all-done.got = f32[16,8,1024]{2,1,0:T(8,128)S(1)} async-done(((f32[16,8,1024]{2,1,0:T(8,128)}), f32[16,8,1024]{2,1,0:T(8,128)S(1)}, u32[]{:S(2)}, u32[]{:S(2)}) %all-to-all-start) | async-done | bytes 524320 | tf_op jit(solution)/shard_map/all_to_all | solution.py:281
  20.6 3.6 %all-gather = f32[16,384]{1,0:T(8,128)S(1)} all-gather(f32[8,384]{1,0:T(8,128)S(1)} %shard_map.78), channel_id=2, replica_groups=mesh['z'=16,'c'=2,'x'=4,'y'=4] {'c'}, dimensions={0}, use_global_device_ids=true | all-gather | bytes 36864 | tf_op jit(solution)/shard_map/all_gather | solution.py:290
  24.9 14.7 %all-to-all-start.1 = ((f32[16,4,384]{2,1,0:T(4,128)}), f32[16,4,384]{2,1,0:T(4,128)S(1)}, u32[]{:S(2)}, u32[]{:S(2)}) async-start(f32[16,4,384]{2,1,0:T(4,128)} %broadcast_in_dim.6), calls=%async_computation.1 | async-start | bytes 196608 | tf_op jit(solution)/shard_map/all_to_all | solution.py:13
  39.7 1.6 %collective-permute-start.1 = (bf16[384,1024]{1,0:T(8,128)(2,1)S(1)}, bf16[384,1024]{1,0:T(8,128)(2,1)}, u32[]{:S(2)}, u32[]{:S(2)}) collective-permute-start(bf16[384,1024]{1,0:T(8,128)(2,1)S(1)} %broadcast_select_fusion), channel_id=1, source_target_pairs={{0,2},{8,10},{33,35},{41,43},{66,64},{74,72},{99,97},{107,105},{13... | collective-permute-start | bytes 2359304 | tf_op jit(solution)/shard_map/ppermute | solution.py:237
  41.2 10.2 %all-to-all-done.1 = f32[16,4,384]{2,1,0:T(4,128)S(1)} async-done(((f32[16,4,384]{2,1,0:T(4,128)}), f32[16,4,384]{2,1,0:T(4,128)S(1)}, u32[]{:S(2)}, u32[]{:S(2)}) %all-to-all-start.1) | async-done | bytes 98336 | tf_op jit(solution)/shard_map/all_to_all | solution.py:13
  51.5 3.8 %all-gather.2 = f32[2,4,384]{2,1,0:T(4,128)S(1)} all-gather(f32[1,4,384]{2,1,0:T(4,128)S(1)} %bitcast.20), channel_id=1, replica_groups=mesh['z'=16,'c'=2,'x'=4,'y'=4] {'c'}, dimensions={0}, use_global_device_ids=true | all-gather | bytes 18432 | tf_op jit(solution)/shard_map/all_gather | solution.py:298
  55.3 1.8 %shard_map.79 = f32[16,8,1536]{2,1,0:T(8,128)} custom-call(f32[8,384]{1,0:T(8,128)S(1)} %reshape.20.p_ref, bf16[1024,384]{1,0:T(8,128)(2,1)S(1)} %copy-done, f32[384,384]{1,0:T(8,128)S(1)} %copy-done.1), custom_call_target="tpu_custom_call" | custom-call | flops 8000000000 | bytes 1388544 | tf_op jit(solution)/shard_map/pallas_call | solution.py:23
  57.1 3.6 %all-to-all-start.2 = ((f32[16,8,1536]{2,1,0:T(8,128)}), f32[16,8,1536]{2,1,0:T(8,128)S(1)}, u32[]{:S(2)}, u32[]{:S(2)}) async-start(f32[16,8,1536]{2,1,0:T(8,128)} %shard_map.79), calls=%async_computation.2 | async-start | bytes 1572864 | tf_op jit(solution)/shard_map/all_to_all | solution.py:308
  60.7 1.2 %broadcast_select_fusion.1 = bf16[384,1024]{1,0:T(8,128)(2,1)S(1)} fusion(bf16[384,1024]{1,0:T(8,128)(2,1)} %collective-permute-done.1, bf16[384,1024]{1,0:T(8,128)(2,1)} %copy-done.4, pred[]{:T(512)S(6)} %eq.33), kind=kLoop, calls=%fused_computation.4 | loop fusion | flops 393216 | bytes 2359297 | tf_op jit(solution)/shard_map/jit(_where)/select_n | solution.py:240
  62.0 1.3 %collective-permute-start.2 = (bf16[384,1024]{1,0:T(8,128)(2,1)S(1)}, bf16[384,1024]{1,0:T(8,128)(2,1)}, u32[]{:S(2)}, u32[]{:S(2)}) collective-permute-start(bf16[384,1024]{1,0:T(8,128)(2,1)S(1)} %broadcast_select_fusion.1), channel_id=1, source_target_pairs={{0,4},{8,12},{2,6},{10,14},{33,37},{41,45},{35,39},{43,47},{66,70}... | collective-permute-start | bytes 2359304 | tf_op jit(solution)/shard_map/ppermute | solution.py:237
  63.3 10.8 %all-to-all-done.2.got = f32[16,8,1536]{2,1,0:T(8,128)S(1)} async-done(((f32[16,8,1536]{2,1,0:T(8,128)}), f32[16,8,1536]{2,1,0:T(8,128)S(1)}, u32[]{:S(2)}, u32[]{:S(2)}) %all-to-all-start.2) | async-done | bytes 786464 | tf_op jit(solution)/shard_map/all_to_all | solution.py:308
  74.1 1.4 %copy-done.2 = bf16[768,1024]{1,0:T(8,128)(2,1)S(1)} copy-done((bf16[768,1024]{1,0:T(8,128)(2,1)S(1)}, bf16[768,1024]{1,0:T(8,128)(2,1)}, u32[]{:S(2)}) %copy-start.2) | copy-done | bytes 1572888
  76.0 3.7 %all-gather.1 = f32[16,768]{1,0:T(8,128)S(1)} all-gather(f32[8,768]{1,0:T(8,128)S(1)} %get-tuple-element.18), channel_id=3, replica_groups=mesh['z'=16,'c'=2,'x'=4,'y'=4] {'c'}, dimensions={0}, use_global_device_ids=true | all-gather | bytes 73728 | tf_op jit(solution)/shard_map/all_gather | solution.py:317
  80.4 3.7 %all-to-all-start.3 = ((f32[16,8,384]{2,1,0:T(8,128)}), f32[16,8,384]{2,1,0:T(8,128)S(1)}, u32[]{:S(2)}, u32[]{:S(2)}) async-start(f32[16,8,384]{2,1,0:T(8,128)} %broadcast_in_dim.7), calls=%async_computation.3 | async-start | bytes 393216 | tf_op jit(solution)/shard_map/all_to_all | solution.py:13
  84.2 2.1 %broadcast_select_fusion.2 = bf16[384,1024]{1,0:T(8,128)(2,1)} fusion(bf16[384,1024]{1,0:T(8,128)(2,1)} %collective-permute-done.2, bf16[384,1024]{1,0:T(8,128)(2,1)S(1)} %broadcast_select_fusion.1, pred[]{:T(512)S(6)} %eq.32), kind=kLoop, calls=%fused_computation.5 | loop fusion | flops 393216 | bytes 2359297 | tf_op jit(solution)/shard_map/jit(_where)/select_n | solution.py:240
  86.4 2.2 %collective-permute-start.3 = (bf16[384,1024]{1,0:T(8,128)(2,1)}, bf16[384,1024]{1,0:T(8,128)(2,1)}, u32[]{:S(2)}, u32[]{:S(2)}) collective-permute-start(bf16[384,1024]{1,0:T(8,128)(2,1)} %broadcast_select_fusion.2), channel_id=1, source_target_pairs={{0,1},{8,9},{2,3},{10,11},{4,5},{12,13},{6,7},{14,15},{33,34},{41,... | collective-permute-start | bytes 2359304 | tf_op jit(solution)/shard_map/ppermute | solution.py:237
  91.5 8.7 %all-to-all-done.3.got = f32[16,8,384]{2,1,0:T(8,128)S(1)} async-done(((f32[16,8,384]{2,1,0:T(8,128)}), f32[16,8,384]{2,1,0:T(8,128)S(1)}, u32[]{:S(2)}, u32[]{:S(2)}) %all-to-all-start.3) | async-done | bytes 196640 | tf_op jit(solution)/shard_map/all_to_all | solution.py:13
  101.2 4.8 %all-to-all-start.4 = ((f32[32,8,384]{2,1,0:T(8,128)}), f32[32,8,384]{2,1,0:T(8,128)S(1)}, u32[]{:S(2)}, u32[]{:S(2)}) async-start(f32[32,8,384]{2,1,0:T(8,128)} %shard_map.81), calls=%async_computation.4 | async-start | bytes 786432 | tf_op jit(solution)/shard_map/all_to_all | solution.py:337
  106.2 1.8 %convolution_add_fusion.base = f32[384,384]{1,0:T(8,128)S(1)} fusion(f32[384,384]{1,0:T(8,128)S(1)} %copy-done.1, bf16[1024,384]{1,0:T(8,128)(2,1)S(1)} %copy-done, bf16[384,1024]{1,0:T(8,128)(2,1)} %collective-permute-done.3, bf16[384,1024]{1,0:T(8,128)(2,1)} %broadcast_select_fusion.2, pred[]{:T(512)S(6)} %eq.35), kind=kOutput, calls=%fused_computation | convolution fusion | flops 302530560 | bytes 3538945 | tf_op jit(solution)/shard_map/dot_general | solution.py:335
  107.9 8.5 %all-to-all-done.4.blocks = f32[32,8,384]{2,1,0:T(8,128)S(1)} async-done(((f32[32,8,384]{2,1,0:T(8,128)}), f32[32,8,384]{2,1,0:T(8,128)S(1)}, u32[]{:S(2)}, u32[]{:S(2)}) %all-to-all-start.4) | async-done | bytes 393248 | tf_op jit(solution)/shard_map/all_to_all | solution.py:337
  116.4 1.8 %shard_map.82 = (f32[384,384]{1,0:T(8,128)}, f32[384,384]{1,0:T(8,128)}, f32[8,12288]{1,0:T(8,128)}) custom-call(f32[32,8,384]{2,1,0:T(8,128)S(1)} %all-to-all-done.4.blocks, f32[8,384]{1,0:T(8,128)S(1)} %fusion.6.ortho, f32[384,384]{1,0:T(8,128)S(1)} %convolution_add_fusion.base, f32[384,384]{1,0:T(8,128)S(1)} %copy-done.3), custom_call_target="tpu_custom_call" | custom-call | flops 2000000000 | bytes 3000000 | tf_op jit(solution)/shard_map/pallas_call | solution.py:339
  (37 shorter events, 6.8 us)
Async XLA Ops:
  0.6 9.4 %copy-start.1 = (f32[384,384]{1,0:T(8,128)S(1)}, f32[384,384]{1,0:T(8,128)}, u32[]{:S(2)}) copy-start(f32[384,384]{1,0:T(8,128)} %feed.3) | copy-start | bytes 1769476
  3.3 17.1 %all-to-all-start = ((f32[16,8,1024]{2,1,0:T(8,128)}), f32[16,8,1024]{2,1,0:T(8,128)S(1)}, u32[]{:S(2)}, u32[]{:S(2)}) async-start(f32[16,8,1024]{2,1,0:T(8,128)} %get-tuple-element.16), calls=%async_computation | async-start | bytes 1048576 | tf_op jit(solution)/shard_map/all_to_all | solution.py:281
  10.1 10.3 %copy-start = (bf16[1024,384]{1,0:T(8,128)(2,1)S(1)}, bf16[1024,384]{1,0:T(8,128)(2,1)}, u32[]{:S(2)}) copy-start(bf16[1024,384]{1,0:T(8,128)(2,1)} %act.3) | copy-start | bytes 2359300
  10.5 29.1 %collective-permute-start = (bf16[384,1024]{1,0:T(8,128)(2,1)S(1)}, bf16[384,1024]{1,0:T(8,128)(2,1)}, u32[]{:S(2)}, u32[]{:S(2)}) collective-permute-start(bf16[384,1024]{1,0:T(8,128)(2,1)S(1)} %get-tuple-element.21), channel_id=1, source_target_pairs={{0,8},{33,41},{66,74},{99,107},{132,140},{165,173},{198,206},{231,... | collective-permute-start | bytes 2359304 | tf_op jit(solution)/shard_map/ppermute | solution.py:237
  24.9 26.5 %all-to-all-start.1 = ((f32[16,4,384]{2,1,0:T(4,128)}), f32[16,4,384]{2,1,0:T(4,128)S(1)}, u32[]{:S(2)}, u32[]{:S(2)}) async-start(f32[16,4,384]{2,1,0:T(4,128)} %broadcast_in_dim.6), calls=%async_computation.1 | async-start | bytes 196608 | tf_op jit(solution)/shard_map/all_to_all | solution.py:13
  39.7 17.4 %copy-start.4 = (bf16[384,1024]{1,0:T(8,128)(2,1)}, bf16[384,1024]{1,0:T(8,128)(2,1)S(1)}, u32[]{:S(2)}) copy-start(bf16[384,1024]{1,0:T(8,128)(2,1)S(1)} %broadcast_select_fusion) | copy-start | bytes 2359300
  39.7 21.1 %collective-permute-start.1 = (bf16[384,1024]{1,0:T(8,128)(2,1)S(1)}, bf16[384,1024]{1,0:T(8,128)(2,1)}, u32[]{:S(2)}, u32[]{:S(2)}) collective-permute-start(bf16[384,1024]{1,0:T(8,128)(2,1)S(1)} %broadcast_select_fusion), channel_id=1, source_target_pairs={{0,2},{8,10},{33,35},{41,43},{66,64},{74,72},{99,97},{107,105},{13... | collective-permute-start | bytes 2359304 | tf_op jit(solution)/shard_map/ppermute | solution.py:237
  57.1 17.0 %all-to-all-start.2 = ((f32[16,8,1536]{2,1,0:T(8,128)}), f32[16,8,1536]{2,1,0:T(8,128)S(1)}, u32[]{:S(2)}, u32[]{:S(2)}) async-start(f32[16,8,1536]{2,1,0:T(8,128)} %shard_map.79), calls=%async_computation.2 | async-start | bytes 1572864 | tf_op jit(solution)/shard_map/all_to_all | solution.py:308
  62.0 22.3 %collective-permute-start.2 = (bf16[384,1024]{1,0:T(8,128)(2,1)S(1)}, bf16[384,1024]{1,0:T(8,128)(2,1)}, u32[]{:S(2)}, u32[]{:S(2)}) collective-permute-start(bf16[384,1024]{1,0:T(8,128)(2,1)S(1)} %broadcast_select_fusion.1), channel_id=1, source_target_pairs={{0,4},{8,12},{2,6},{10,14},{33,37},{41,45},{35,39},{43,47},{66,70}... | collective-permute-start | bytes 2359304 | tf_op jit(solution)/shard_map/ppermute | solution.py:237
  74.1 1.4 %copy-start.2 = (bf16[768,1024]{1,0:T(8,128)(2,1)S(1)}, bf16[768,1024]{1,0:T(8,128)(2,1)}, u32[]{:S(2)}) copy-start(bf16[768,1024]{1,0:T(8,128)(2,1)} %hid.3) | copy-start | bytes 4718596
  80.4 19.8 %all-to-all-start.3 = ((f32[16,8,384]{2,1,0:T(8,128)}), f32[16,8,384]{2,1,0:T(8,128)S(1)}, u32[]{:S(2)}, u32[]{:S(2)}) async-start(f32[16,8,384]{2,1,0:T(8,128)} %broadcast_in_dim.7), calls=%async_computation.3 | async-start | bytes 393216 | tf_op jit(solution)/shard_map/all_to_all | solution.py:13
  86.4 19.8 %collective-permute-start.3 = (bf16[384,1024]{1,0:T(8,128)(2,1)}, bf16[384,1024]{1,0:T(8,128)(2,1)}, u32[]{:S(2)}, u32[]{:S(2)}) collective-permute-start(bf16[384,1024]{1,0:T(8,128)(2,1)} %broadcast_select_fusion.2), channel_id=1, source_target_pairs={{0,1},{8,9},{2,3},{10,11},{4,5},{12,13},{6,7},{14,15},{33,34},{41,... | collective-permute-start | bytes 2359304 | tf_op jit(solution)/shard_map/ppermute | solution.py:237
  101.2 15.3 %all-to-all-start.4 = ((f32[32,8,384]{2,1,0:T(8,128)}), f32[32,8,384]{2,1,0:T(8,128)S(1)}, u32[]{:S(2)}, u32[]{:S(2)}) async-start(f32[32,8,384]{2,1,0:T(8,128)} %shard_map.81), calls=%async_computation.4 | async-start | bytes 786432 | tf_op jit(solution)/shard_map/all_to_all | solution.py:337
  106.1 10.3 %copy-start.3 = (f32[384,384]{1,0:T(8,128)S(1)}, f32[384,384]{1,0:T(8,128)}, u32[]{:S(2)}) copy-start(f32[384,384]{1,0:T(8,128)} %momentum.1) | copy-start | bytes 1769476

commit v7 on v6

--- a/solution.py
+++ b/solution.py
@@ -47,11 +47,15 @@
     return y
 
 
-def parts_of(x):
+def three(x):
     a = x.astype(jnp.bfloat16).astype(jnp.float32)
     r = x - a
     b = r.astype(jnp.bfloat16).astype(jnp.float32)
-    return jnp.concatenate([a, b, r - b, jnp.zeros_like(x)], 0).astype(jnp.bfloat16)
+    return a, b, r - b
+
+
+def parts_of(x):
+    return jnp.concatenate([*three(x), jnp.zeros_like(x)], 0).astype(jnp.bfloat16)
 
 
 def start_kernel(q, hid, out, q_own, piece_out, q_near, held, row, sems, done):
@@ -109,15 +113,26 @@
     p = p_ref[...]
     rank, toks = p.shape[0], act.shape[0]
     rows = feed.shape[0]
-    u = exact_dot(p, act[...], ((1,), (1,)))
     across = (((1,), (1,)), ((), ()))
-    err = lax.dot_general(
-        p, feed[...], across, precision=high, preferred_element_type=jnp.float32
-    )
-    square = jnp.concatenate([p, jnp.zeros((128 - rank, p.shape[1]), p.dtype)], 0)
-    gram = lax.dot_general(
-        p, square, across, precision=high, preferred_element_type=jnp.float32
-    )
+    parts = parts_of(p)
+    y = lax.dot_general(
+        parts, act[...], across, preferred_element_type=jnp.float32
+    )
+    n = rank
+    u = (y[2 * n : 3 * n] + y[n : 2 * n]) + y[:n]
+    e, f, g = (
+        lax.dot_general(
+            parts, v.astype(jnp.bfloat16), across, preferred_element_type=jnp.float32
+        )
+        for v in three(feed[...])
+    )
+    small = (g[:n] + f[n : 2 * n]) + e[2 * n : 3 * n]
+    err = (small + (f[:n] + e[n : 2 * n])) + e[:n]
+    lane = lax.broadcasted_iota(jnp.int32, (rank, 128), 1)
+    gram = jnp.zeros((rank, 128), jnp.float32)
+    for i in range(rank):
+        column = jnp.sum(p * p[i : i + 1], axis=1, keepdims=True)
+        gram = jnp.where(lane == i, column, gram)
     for i in range(out.shape[0]):
         out[i, :, :toks] = u
         out[i, :, toks : toks + rows] = err
@@ -140,9 +155,10 @@
 
 def block_kernel(got, inverse, out):
     rows = total(got, slice(None))
-    block = jnp.dot(
-        inverse[...], rows, precision=high, preferred_element_type=jnp.float32
-    )
+    inv = inverse[...]
+    block = inv[:, 0:1] * rows[0:1]
+    for i in range(1, rows.shape[0]):
+        block = block + inv[:, i : i + 1] * rows[i : i + 1]
     block = block * (1.0 / out.shape[0])
     for i in range(out.shape[0]):
         out[i] = block
@@ -159,15 +175,17 @@
     for send in sends:
         send.start()
     replica = lax.axis_index("z") * lax.axis_size("c") + lax.axis_index("c")
-    mine = blocks[replica]
+    a, b, c = three(blocks[replica])
+    left = jnp.concatenate([c, b, a, b, a, a], 0).astype(jnp.bfloat16)
+    a, b, c = three(ortho[...])
+    right = jnp.concatenate([a, b, c, a, b, a], 0).astype(jnp.bfloat16)
     part = feed_new.shape[0] // 3
     for i in range(3):
         piece = slice(i * part, (i + 1) * part)
         approx = lax.dot_general(
-            mine[:, piece],
-            ortho[...],
+            left[:, piece],
+            right,
             (((0,), (0,)), ((), ())),
-            precision=high,
             preferred_element_type=jnp.float32,
         )
         feed_new[piece] = base[piece] - approx

time: 119 us -> 118 us (level)
  no operation moved by 1% of the time
where the time goes in v7:
time: 118 us
  waiting for transfers between devices  46.6 us (39%)
  starting transfers between devices  40.2 us (34%)
  blocking collectives  11.2 us (9%)
  Pallas kernels  7.75 us (7%)
  other arithmetic  6.14 us (5%)
  local copies, waits for them, and re-layouts  2.97 us (3%)
  matrix products  2.09 us (2%)
    all_to_all x2, waiting for transfers between devices, copies(): lax.all_to_all(jnp.broadcast_to(x[None], (count,) + x.shape), axes, 0, 0)  18.9 us
    all_to_all x2, starting transfers between devices, copies(): lax.all_to_all(jnp.broadcast_to(x[None], (count,) + x.shape), axes, 0, 0)  18.3 us
    all_to_all x1, waiting for transfers between devices, per_device(): packed = near(lax.all_to_all(packed, plane, 0, 0))  10.8 us
    all_to_all x1, waiting for transfers between devices, per_device(): blocks = near(lax.all_to_all(block, ('x', 'y', 'c'), 0, 0))  8.47 us
    all_to_all x1, waiting for transfers between devices, per_device(): tokens = near(lax.all_to_all(token_part, plane, 0, 0))  8.34 us
    all_to_all x1, starting transfers between devices, per_device(): tokens = near(lax.all_to_all(token_part, plane, 0, 0))  6.77 us
    ppermute x4, starting transfers between devices, send(): return lax.ppermute(held, ('z', 'c', 'x', 'y'), rounds[k])  6.6 us
    all_to_all x1, starting transfers between devices, per_device(): blocks = near(lax.all_to_all(block, ('x', 'y', 'c'), 0, 0))  4.84 us
  transfers between devices with their start and end apart: 9, of which 5 were waited for; matrix products, arithmetic and copies ran while one was open for 8% of the time, Pallas kernels for 3%

profile of v7, /device:TPU:33, one launch (start us, length us, event | category | flops | bytes accessed | tf_op | source)
XLA Modules:
  0.0 117.7 jit_solution(14912303079409498746)
XLA Ops:
  0.6 2.6 %shard_map.76 = (f32[16,8,1024]{2,1,0:T(8,128)}, f32[8,384]{1,0:T(8,128)S(1)}, bf16[384,1024]{1,0:T(8,128)(2,1)S(1)}) custom-call(f32[8,12288]{1,0:T(8,128)} %bitcast.21, bf16[768,1024]{1,0:T(8,128)(2,1)} %hid.3), custom_call_target="tpu_custom_call" | custom-call | flops 2000000000 | bytes 3000000 | tf_op jit(solution)/shard_map/pallas_call | solution.py:264
  3.3 6.8 %all-to-all-start = ((f32[16,8,1024]{2,1,0:T(8,128)}), f32[16,8,1024]{2,1,0:T(8,128)S(1)}, u32[]{:S(2)}, u32[]{:S(2)}) async-start(f32[16,8,1024]{2,1,0:T(8,128)} %get-tuple-element.16), calls=%async_computation | async-start | bytes 1048576 | tf_op jit(solution)/shard_map/all_to_all | solution.py:299
  10.5 1.6 %collective-permute-start = (bf16[384,1024]{1,0:T(8,128)(2,1)S(1)}, bf16[384,1024]{1,0:T(8,128)(2,1)}, u32[]{:S(2)}, u32[]{:S(2)}) collective-permute-start(bf16[384,1024]{1,0:T(8,128)(2,1)S(1)} %get-tuple-element.21), channel_id=1, source_target_pairs={{0,8},{33,41},{66,74},{99,107},{132,140},{165,173},{198,206},{231,... | collective-permute-start | bytes 2359304 | tf_op jit(solution)/shard_map/ppermute | solution.py:255
  12.0 8.3 %all-to-all-done.got = f32[16,8,1024]{2,1,0:T(8,128)S(1)} async-done(((f32[16,8,1024]{2,1,0:T(8,128)}), f32[16,8,1024]{2,1,0:T(8,128)S(1)}, u32[]{:S(2)}, u32[]{:S(2)}) %all-to-all-start) | async-done | bytes 524320 | tf_op jit(solution)/shard_map/all_to_all | solution.py:299
  20.6 3.6 %all-gather = f32[16,384]{1,0:T(8,128)S(1)} all-gather(f32[8,384]{1,0:T(8,128)S(1)} %shard_map.78), channel_id=2, replica_groups=mesh['z'=16,'c'=2,'x'=4,'y'=4] {'c'}, dimensions={0}, use_global_device_ids=true | all-gather | bytes 36864 | tf_op jit(solution)/shard_map/all_gather | solution.py:308
  24.9 14.7 %all-to-all-start.1 = ((f32[16,4,384]{2,1,0:T(4,128)}), f32[16,4,384]{2,1,0:T(4,128)S(1)}, u32[]{:S(2)}, u32[]{:S(2)}) async-start(f32[16,4,384]{2,1,0:T(4,128)} %broadcast_in_dim.6), calls=%async_computation.1 | async-start | bytes 196608 | tf_op jit(solution)/shard_map/all_to_all | solution.py:13
  39.7 1.6 %collective-permute-start.1 = (bf16[384,1024]{1,0:T(8,128)(2,1)S(1)}, bf16[384,1024]{1,0:T(8,128)(2,1)}, u32[]{:S(2)}, u32[]{:S(2)}) collective-permute-start(bf16[384,1024]{1,0:T(8,128)(2,1)S(1)} %broadcast_select_fusion), channel_id=1, source_target_pairs={{0,2},{8,10},{33,35},{41,43},{66,64},{74,72},{99,97},{107,105},{13... | collective-permute-start | bytes 2359304 | tf_op jit(solution)/shard_map/ppermute | solution.py:255
  41.2 10.2 %all-to-all-done.1 = f32[16,4,384]{2,1,0:T(4,128)S(1)} async-done(((f32[16,4,384]{2,1,0:T(4,128)}), f32[16,4,384]{2,1,0:T(4,128)S(1)}, u32[]{:S(2)}, u32[]{:S(2)}) %all-to-all-start.1) | async-done | bytes 98336 | tf_op jit(solution)/shard_map/all_to_all | solution.py:13
  51.5 3.8 %all-gather.2 = f32[2,4,384]{2,1,0:T(4,128)S(1)} all-gather(f32[1,4,384]{2,1,0:T(4,128)S(1)} %bitcast.20), channel_id=1, replica_groups=mesh['z'=16,'c'=2,'x'=4,'y'=4] {'c'}, dimensions={0}, use_global_device_ids=true | all-gather | bytes 18432 | tf_op jit(solution)/shard_map/all_gather | solution.py:316
  55.3 1.5 %shard_map.79 = f32[16,8,1536]{2,1,0:T(8,128)} custom-call(f32[8,384]{1,0:T(8,128)S(1)} %reshape.20.p_ref, bf16[1024,384]{1,0:T(8,128)(2,1)S(1)} %copy-done, f32[384,384]{1,0:T(8,128)S(1)} %copy-done.1), custom_call_target="tpu_custom_call" | custom-call | flops 8000000000 | bytes 1388544 | tf_op jit(solution)/shard_map/pallas_call | solution.py:23
  56.9 3.6 %all-to-all-start.2 = ((f32[16,8,1536]{2,1,0:T(8,128)}), f32[16,8,1536]{2,1,0:T(8,128)S(1)}, u32[]{:S(2)}, u32[]{:S(2)}) async-start(f32[16,8,1536]{2,1,0:T(8,128)} %shard_map.79), calls=%async_computation.2 | async-start | bytes 1572864 | tf_op jit(solution)/shard_map/all_to_all | solution.py:326
  60.5 1.2 %broadcast_select_fusion.1 = bf16[384,1024]{1,0:T(8,128)(2,1)S(1)} fusion(bf16[384,1024]{1,0:T(8,128)(2,1)} %collective-permute-done.1, bf16[384,1024]{1,0:T(8,128)(2,1)} %copy-done.4, pred[]{:T(512)S(6)} %eq.33), kind=kLoop, calls=%fused_computation.4 | loop fusion | flops 393216 | bytes 2359297 | tf_op jit(solution)/shard_map/jit(_where)/select_n | solution.py:258
  61.7 1.3 %collective-permute-start.2 = (bf16[384,1024]{1,0:T(8,128)(2,1)S(1)}, bf16[384,1024]{1,0:T(8,128)(2,1)}, u32[]{:S(2)}, u32[]{:S(2)}) collective-permute-start(bf16[384,1024]{1,0:T(8,128)(2,1)S(1)} %broadcast_select_fusion.1), channel_id=1, source_target_pairs={{0,4},{8,12},{2,6},{10,14},{33,37},{41,45},{35,39},{43,47},{66,70}... | collective-permute-start | bytes 2359304 | tf_op jit(solution)/shard_map/ppermute | solution.py:255
  63.0 10.8 %all-to-all-done.2.got = f32[16,8,1536]{2,1,0:T(8,128)S(1)} async-done(((f32[16,8,1536]{2,1,0:T(8,128)}), f32[16,8,1536]{2,1,0:T(8,128)S(1)}, u32[]{:S(2)}, u32[]{:S(2)}) %all-to-all-start.2) | async-done | bytes 786464 | tf_op jit(solution)/shard_map/all_to_all | solution.py:326
  73.8 1.4 %copy-done.2 = bf16[768,1024]{1,0:T(8,128)(2,1)S(1)} copy-done((bf16[768,1024]{1,0:T(8,128)(2,1)S(1)}, bf16[768,1024]{1,0:T(8,128)(2,1)}, u32[]{:S(2)}) %copy-start.2) | copy-done | bytes 1572888
  75.8 3.7 %all-gather.1 = f32[16,768]{1,0:T(8,128)S(1)} all-gather(f32[8,768]{1,0:T(8,128)S(1)} %get-tuple-element.18), channel_id=3, replica_groups=mesh['z'=16,'c'=2,'x'=4,'y'=4] {'c'}, dimensions={0}, use_global_device_ids=true | all-gather | bytes 73728 | tf_op jit(solution)/shard_map/all_gather | solution.py:335
  80.2 3.7 %all-to-all-start.3 = ((f32[16,8,384]{2,1,0:T(8,128)}), f32[16,8,384]{2,1,0:T(8,128)S(1)}, u32[]{:S(2)}, u32[]{:S(2)}) async-start(f32[16,8,384]{2,1,0:T(8,128)} %broadcast_in_dim.7), calls=%async_computation.3 | async-start | bytes 393216 | tf_op jit(solution)/shard_map/all_to_all | solution.py:13
  84.0 2.1 %broadcast_select_fusion.2 = bf16[384,1024]{1,0:T(8,128)(2,1)} fusion(bf16[384,1024]{1,0:T(8,128)(2,1)} %collective-permute-done.2, bf16[384,1024]{1,0:T(8,128)(2,1)S(1)} %broadcast_select_fusion.1, pred[]{:T(512)S(6)} %eq.32), kind=kLoop, calls=%fused_computation.5 | loop fusion | flops 393216 | bytes 2359297 | tf_op jit(solution)/shard_map/jit(_where)/select_n | solution.py:258
  86.1 2.2 %collective-permute-start.3 = (bf16[384,1024]{1,0:T(8,128)(2,1)}, bf16[384,1024]{1,0:T(8,128)(2,1)}, u32[]{:S(2)}, u32[]{:S(2)}) collective-permute-start(bf16[384,1024]{1,0:T(8,128)(2,1)} %broadcast_select_fusion.2), channel_id=1, source_target_pairs={{0,1},{8,9},{2,3},{10,11},{4,5},{12,13},{6,7},{14,15},{33,34},{41,... | collective-permute-start | bytes 2359304 | tf_op jit(solution)/shard_map/ppermute | solution.py:255
  91.2 8.7 %all-to-all-done.3.got = f32[16,8,384]{2,1,0:T(8,128)S(1)} async-done(((f32[16,8,384]{2,1,0:T(8,128)}), f32[16,8,384]{2,1,0:T(8,128)S(1)}, u32[]{:S(2)}, u32[]{:S(2)}) %all-to-all-start.3) | async-done | bytes 196640 | tf_op jit(solution)/shard_map/all_to_all | solution.py:13
  100.8 4.8 %all-to-all-start.4 = ((f32[32,8,384]{2,1,0:T(8,128)}), f32[32,8,384]{2,1,0:T(8,128)S(1)}, u32[]{:S(2)}, u32[]{:S(2)}) async-start(f32[32,8,384]{2,1,0:T(8,128)} %shard_map.81), calls=%async_computation.4 | async-start | bytes 786432 | tf_op jit(solution)/shard_map/all_to_all | solution.py:355
  105.8 1.8 %convolution_add_fusion.base = f32[384,384]{1,0:T(8,128)S(1)} fusion(f32[384,384]{1,0:T(8,128)S(1)} %copy-done.1, bf16[1024,384]{1,0:T(8,128)(2,1)S(1)} %copy-done, bf16[384,1024]{1,0:T(8,128)(2,1)} %collective-permute-done.3, bf16[384,1024]{1,0:T(8,128)(2,1)} %broadcast_select_fusion.2, pred[]{:T(512)S(6)} %eq.35), kind=kOutput, calls=%fused_computation | convolution fusion | flops 302530560 | bytes 3538945 | tf_op jit(solution)/shard_map/dot_general | solution.py:353
  107.6 8.5 %all-to-all-done.4.blocks = f32[32,8,384]{2,1,0:T(8,128)S(1)} async-done(((f32[32,8,384]{2,1,0:T(8,128)}), f32[32,8,384]{2,1,0:T(8,128)S(1)}, u32[]{:S(2)}, u32[]{:S(2)}) %all-to-all-start.4) | async-done | bytes 393248 | tf_op jit(solution)/shard_map/all_to_all | solution.py:355
  116.1 1.6 %shard_map.82 = (f32[384,384]{1,0:T(8,128)}, f32[384,384]{1,0:T(8,128)}, f32[8,12288]{1,0:T(8,128)}) custom-call(f32[32,8,384]{2,1,0:T(8,128)S(1)} %all-to-all-done.4.blocks, f32[8,384]{1,0:T(8,128)S(1)} %fusion.6.ortho, f32[384,384]{1,0:T(8,128)S(1)} %convolution_add_fusion.base, f32[384,384]{1,0:T(8,128)S(1)} %copy-done.3), custom_call_target="tpu_custom_call" | custom-call | flops 2000000000 | bytes 3000000 | tf_op jit(solution)/shard_map/pallas_call | solution.py:357
  (37 shorter events, 6.7 us)
Async XLA Ops:
  0.6 9.4 %copy-start.1 = (f32[384,384]{1,0:T(8,128)S(1)}, f32[384,384]{1,0:T(8,128)}, u32[]{:S(2)}) copy-start(f32[384,384]{1,0:T(8,128)} %feed.3) | copy-start | bytes 1769476
  3.3 17.1 %all-to-all-start = ((f32[16,8,1024]{2,1,0:T(8,128)}), f32[16,8,1024]{2,1,0:T(8,128)S(1)}, u32[]{:S(2)}, u32[]{:S(2)}) async-start(f32[16,8,1024]{2,1,0:T(8,128)} %get-tuple-element.16), calls=%async_computation | async-start | bytes 1048576 | tf_op jit(solution)/shard_map/all_to_all | solution.py:299
  10.1 10.3 %copy-start = (bf16[1024,384]{1,0:T(8,128)(2,1)S(1)}, bf16[1024,384]{1,0:T(8,128)(2,1)}, u32[]{:S(2)}) copy-start(bf16[1024,384]{1,0:T(8,128)(2,1)} %act.3) | copy-start | bytes 2359300
  10.5 29.1 %collective-permute-start = (bf16[384,1024]{1,0:T(8,128)(2,1)S(1)}, bf16[384,1024]{1,0:T(8,128)(2,1)}, u32[]{:S(2)}, u32[]{:S(2)}) collective-permute-start(bf16[384,1024]{1,0:T(8,128)(2,1)S(1)} %get-tuple-element.21), channel_id=1, source_target_pairs={{0,8},{33,41},{66,74},{99,107},{132,140},{165,173},{198,206},{231,... | collective-permute-start | bytes 2359304 | tf_op jit(solution)/shard_map/ppermute | solution.py:255
  24.9 26.5 %all-to-all-start.1 = ((f32[16,4,384]{2,1,0:T(4,128)}), f32[16,4,384]{2,1,0:T(4,128)S(1)}, u32[]{:S(2)}, u32[]{:S(2)}) async-start(f32[16,4,384]{2,1,0:T(4,128)} %broadcast_in_dim.6), calls=%async_computation.1 | async-start | bytes 196608 | tf_op jit(solution)/shard_map/all_to_all | solution.py:13
  39.7 17.2 %copy-start.4 = (bf16[384,1024]{1,0:T(8,128)(2,1)}, bf16[384,1024]{1,0:T(8,128)(2,1)S(1)}, u32[]{:S(2)}) copy-start(bf16[384,1024]{1,0:T(8,128)(2,1)S(1)} %broadcast_select_fusion) | copy-start | bytes 2359300
  39.7 20.8 %collective-permute-start.1 = (bf16[384,1024]{1,0:T(8,128)(2,1)S(1)}, bf16[384,1024]{1,0:T(8,128)(2,1)}, u32[]{:S(2)}, u32[]{:S(2)}) collective-permute-start(bf16[384,1024]{1,0:T(8,128)(2,1)S(1)} %broadcast_select_fusion), channel_id=1, source_target_pairs={{0,2},{8,10},{33,35},{41,43},{66,64},{74,72},{99,97},{107,105},{13... | collective-permute-start | bytes 2359304 | tf_op jit(solution)/shard_map/ppermute | solution.py:255
  56.9 17.0 %all-to-all-start.2 = ((f32[16,8,1536]{2,1,0:T(8,128)}), f32[16,8,1536]{2,1,0:T(8,128)S(1)}, u32[]{:S(2)}, u32[]{:S(2)}) async-start(f32[16,8,1536]{2,1,0:T(8,128)} %shard_map.79), calls=%async_computation.2 | async-start | bytes 1572864 | tf_op jit(solution)/shard_map/all_to_all | solution.py:326
  61.7 22.3 %collective-permute-start.2 = (bf16[384,1024]{1,0:T(8,128)(2,1)S(1)}, bf16[384,1024]{1,0:T(8,128)(2,1)}, u32[]{:S(2)}, u32[]{:S(2)}) collective-permute-start(bf16[384,1024]{1,0:T(8,128)(2,1)S(1)} %broadcast_select_fusion.1), channel_id=1, source_target_pairs={{0,4},{8,12},{2,6},{10,14},{33,37},{41,45},{35,39},{43,47},{66,70}... | collective-permute-start | bytes 2359304 | tf_op jit(solution)/shard_map/ppermute | solution.py:255
  73.8 1.4 %copy-start.2 = (bf16[768,1024]{1,0:T(8,128)(2,1)S(1)}, bf16[768,1024]{1,0:T(8,128)(2,1)}, u32[]{:S(2)}) copy-start(bf16[768,1024]{1,0:T(8,128)(2,1)} %hid.3) | copy-start | bytes 4718596
  80.2 19.8 %all-to-all-start.3 = ((f32[16,8,384]{2,1,0:T(8,128)}), f32[16,8,384]{2,1,0:T(8,128)S(1)}, u32[]{:S(2)}, u32[]{:S(2)}) async-start(f32[16,8,384]{2,1,0:T(8,128)} %broadcast_in_dim.7), calls=%async_computation.3 | async-start | bytes 393216 | tf_op jit(solution)/shard_map/all_to_all | solution.py:13
  86.1 19.7 %collective-permute-start.3 = (bf16[384,1024]{1,0:T(8,128)(2,1)}, bf16[384,1024]{1,0:T(8,128)(2,1)}, u32[]{:S(2)}, u32[]{:S(2)}) collective-permute-start(bf16[384,1024]{1,0:T(8,128)(2,1)} %broadcast_select_fusion.2), channel_id=1, source_target_pairs={{0,1},{8,9},{2,3},{10,11},{4,5},{12,13},{6,7},{14,15},{33,34},{41,... | collective-permute-start | bytes 2359304 | tf_op jit(solution)/shard_map/ppermute | solution.py:255
  100.8 15.3 %all-to-all-start.4 = ((f32[32,8,384]{2,1,0:T(8,128)}), f32[32,8,384]{2,1,0:T(8,128)S(1)}, u32[]{:S(2)}, u32[]{:S(2)}) async-start(f32[32,8,384]{2,1,0:T(8,128)} %shard_map.81), calls=%async_computation.4 | async-start | bytes 786432 | tf_op jit(solution)/shard_map/all_to_all | solution.py:355
  105.8 10.3 %copy-start.3 = (f32[384,384]{1,0:T(8,128)S(1)}, f32[384,384]{1,0:T(8,128)}, u32[]{:S(2)}) copy-start(f32[384,384]{1,0:T(8,128)} %momentum.1) | copy-start | bytes 1769476

commit v8 on v7

--- a/solution.py
+++ b/solution.py
@@ -139,18 +139,26 @@
         out[i, :, toks + rows :] = gram
 
 
-def hidden_kernel(got, hid, out, gram):
+def hidden_kernel(got, hid, low, out, gram):
     toks, rows = hid.shape[1], out.shape[1] // 2
     u = total(got, slice(0, toks))
     err = total(got, slice(toks, toks + rows))
     gram[...] = total(got, slice(toks + rows, None))
-    y = exact_dot(u, hid[...], ((1,), (1,)))
+    parts = parts_of(u)
     shard = lax.axis_index("x") * lax.axis_size("y") + lax.axis_index("y")
     mine = jnp.where(shard == lax.axis_index("z"), 1.0, 0.0)
     upper = jnp.where(lax.axis_index("c") == 0, mine, 0.0)
     lower = mine - upper
-    out[:, :rows] = y[:, :rows] + err * upper
-    out[:, rows:] = y[:, rows:] + err * lower
+    n = out.shape[0]
+    for i, (half, weight) in enumerate(((hid, upper), (low, lower))):
+        y = lax.dot_general(
+            parts,
+            half[...],
+            (((1,), (1,)), ((), ())),
+            preferred_element_type=jnp.float32,
+        )
+        y = (y[2 * n : 3 * n] + y[n : 2 * n]) + y[:n]
+        out[:, i * rows : (i + 1) * rows] = y + err * weight
 
 
 def block_kernel(got, inverse, out):
@@ -323,13 +331,16 @@
         near(act_near),
         feed_near,
     )
+    hid_late = tie(hidden, packed)
+    hid_top, hid_low = hid_late[:cols_dp], hid_late[cols_dp:]
     packed = near(lax.all_to_all(packed, plane, 0, 0))
     hid, gram_mat = local(
         hidden_kernel,
         [pltpu.VMEM((rank, cols_mp), f32), pltpu.VMEM((rank, 128), f32)],
         1,
         packed,
-        near(hidden),
+        near(hid_top),
+        near(hid_low),
     )
     gram_mat = gram_mat[:, :rank]
     half = lax.all_gather(hid, "c").sum(0)

time: 118 us -> 117 us (level)
  local copies, waits for them, and re-layouts: 2.97 us -> 1.69 us
    unnamed x11, local copies, waits for them, and re-layouts: 1.44 us -> 0.04 us
where the time goes in v8:
time: 117 us; the launch traced here: 116 us
  waiting for transfers between devices  46.7 us (40%)
  starting transfers between devices  40.1 us (34%)
  blocking collectives  11.2 us (10%)
  Pallas kernels  7.79 us (7%)
  other arithmetic  5.93 us (5%)
  matrix products  2.1 us (2%)
  local copies, waits for them, and re-layouts  1.69 us (1%)
    all_to_all x2, waiting for transfers between devices, copies(): lax.all_to_all(jnp.broadcast_to(x[None], (count,) + x.shape), axes, 0, 0)  18.9 us
    all_to_all x2, starting transfers between devices, copies(): lax.all_to_all(jnp.broadcast_to(x[None], (count,) + x.shape), axes, 0, 0)  18.3 us
    all_to_all x1, waiting for transfers between devices, per_device(): packed = near(lax.all_to_all(packed, plane, 0, 0))  10.9 us
    all_to_all x1, waiting for transfers between devices, per_device(): blocks = near(lax.all_to_all(block, ('x', 'y', 'c'), 0, 0))  8.46 us
    all_to_all x1, waiting for transfers between devices, per_device(): tokens = near(lax.all_to_all(token_part, plane, 0, 0))  8.34 us
    all_to_all x1, starting transfers between devices, per_device(): tokens = near(lax.all_to_all(token_part, plane, 0, 0))  6.77 us
    ppermute x4, starting transfers between devices, send(): return lax.ppermute(held, ('z', 'c', 'x', 'y'), rounds[k])  6.56 us
    all_to_all x1, starting transfers between devices, per_device(): blocks = near(lax.all_to_all(block, ('x', 'y', 'c'), 0, 0))  4.84 us
  transfers between devices with their start and end apart: 9, of which 5 were waited for; matrix products, arithmetic and copies ran while one was open for 8% of the time, Pallas kernels for 3%

profile of v8, /device:TPU:33, one launch (start us, length us, event | category | flops | bytes accessed | tf_op | source)
XLA Modules:
  0.0 116.3 jit_solution(83175854473531515)
XLA Ops:
  0.6 2.6 %shard_map.76 = (f32[16,8,1024]{2,1,0:T(8,128)}, f32[8,384]{1,0:T(8,128)S(1)}, bf16[384,1024]{1,0:T(8,128)(2,1)S(1)}) custom-call(f32[8,12288]{1,0:T(8,128)} %bitcast.21, bf16[768,1024]{1,0:T(8,128)(2,1)} %hid.1), custom_call_target="tpu_custom_call" | custom-call | flops 2000000000 | bytes 3000000 | tf_op jit(solution)/shard_map/pallas_call | solution.py:272
  3.3 6.8 %all-to-all-start = ((f32[16,8,1024]{2,1,0:T(8,128)}), f32[16,8,1024]{2,1,0:T(8,128)S(1)}, u32[]{:S(2)}, u32[]{:S(2)}) async-start(f32[16,8,1024]{2,1,0:T(8,128)} %get-tuple-element.17), calls=%async_computation | async-start | bytes 1048576 | tf_op jit(solution)/shard_map/all_to_all | solution.py:307
  10.5 1.6 %collective-permute-start = (bf16[384,1024]{1,0:T(8,128)(2,1)S(1)}, bf16[384,1024]{1,0:T(8,128)(2,1)}, u32[]{:S(2)}, u32[]{:S(2)}) collective-permute-start(bf16[384,1024]{1,0:T(8,128)(2,1)S(1)} %get-tuple-element.23), channel_id=1, source_target_pairs={{0,8},{33,41},{66,74},{99,107},{132,140},{165,173},{198,206},{231,... | collective-permute-start | bytes 2359304 | tf_op jit(solution)/shard_map/ppermute | solution.py:263
  12.0 8.3 %all-to-all-done.got = f32[16,8,1024]{2,1,0:T(8,128)S(1)} async-done(((f32[16,8,1024]{2,1,0:T(8,128)}), f32[16,8,1024]{2,1,0:T(8,128)S(1)}, u32[]{:S(2)}, u32[]{:S(2)}) %all-to-all-start) | async-done | bytes 524320 | tf_op jit(solution)/shard_map/all_to_all | solution.py:307
  20.6 3.6 %all-gather = f32[16,384]{1,0:T(8,128)S(1)} all-gather(f32[8,384]{1,0:T(8,128)S(1)} %shard_map.78), channel_id=2, replica_groups=mesh['z'=16,'c'=2,'x'=4,'y'=4] {'c'}, dimensions={0}, use_global_device_ids=true | all-gather | bytes 36864 | tf_op jit(solution)/shard_map/all_gather | solution.py:316
  24.9 14.7 %all-to-all-start.1 = ((f32[16,4,384]{2,1,0:T(4,128)}), f32[16,4,384]{2,1,0:T(4,128)S(1)}, u32[]{:S(2)}, u32[]{:S(2)}) async-start(f32[16,4,384]{2,1,0:T(4,128)} %broadcast_in_dim.6), calls=%async_computation.1 | async-start | bytes 196608 | tf_op jit(solution)/shard_map/all_to_all | solution.py:13
  39.7 1.6 %collective-permute-start.1 = (bf16[384,1024]{1,0:T(8,128)(2,1)S(1)}, bf16[384,1024]{1,0:T(8,128)(2,1)}, u32[]{:S(2)}, u32[]{:S(2)}) collective-permute-start(bf16[384,1024]{1,0:T(8,128)(2,1)S(1)} %broadcast_select_fusion), channel_id=1, source_target_pairs={{0,2},{8,10},{33,35},{41,43},{66,64},{74,72},{99,97},{107,105},{13... | collective-permute-start | bytes 2359304 | tf_op jit(solution)/shard_map/ppermute | solution.py:263
  41.2 10.2 %all-to-all-done.1 = f32[16,4,384]{2,1,0:T(4,128)S(1)} async-done(((f32[16,4,384]{2,1,0:T(4,128)}), f32[16,4,384]{2,1,0:T(4,128)S(1)}, u32[]{:S(2)}, u32[]{:S(2)}) %all-to-all-start.1) | async-done | bytes 98336 | tf_op jit(solution)/shard_map/all_to_all | solution.py:13
  51.5 3.8 %all-gather.2 = f32[2,4,384]{2,1,0:T(4,128)S(1)} all-gather(f32[1,4,384]{2,1,0:T(4,128)S(1)} %bitcast.20), channel_id=1, replica_groups=mesh['z'=16,'c'=2,'x'=4,'y'=4] {'c'}, dimensions={0}, use_global_device_ids=true | all-gather | bytes 18432 | tf_op jit(solution)/shard_map/all_gather | solution.py:324
  55.3 1.5 %shard_map.79 = f32[16,8,1536]{2,1,0:T(8,128)} custom-call(f32[8,384]{1,0:T(8,128)S(1)} %reshape.20.p_ref, bf16[1024,384]{1,0:T(8,128)(2,1)S(1)} %copy-done, f32[384,384]{1,0:T(8,128)S(1)} %copy-done.1), custom_call_target="tpu_custom_call" | custom-call | flops 8000000000 | bytes 1388544 | tf_op jit(solution)/shard_map/pallas_call | solution.py:23
  56.9 3.6 %all-to-all-start.2 = ((f32[16,8,1536]{2,1,0:T(8,128)}), f32[16,8,1536]{2,1,0:T(8,128)S(1)}, u32[]{:S(2)}, u32[]{:S(2)}) async-start(f32[16,8,1536]{2,1,0:T(8,128)} %shard_map.79), calls=%async_computation.2 | async-start | bytes 1572864 | tf_op jit(solution)/shard_map/all_to_all | solution.py:336
  60.5 1.0 broadcast_select_fusion.1
  61.5 1.3 %collective-permute-start.2 = (bf16[384,1024]{1,0:T(8,128)(2,1)}, bf16[384,1024]{1,0:T(8,128)(2,1)}, u32[]{:S(2)}, u32[]{:S(2)}) collective-permute-start(bf16[384,1024]{1,0:T(8,128)(2,1)} %broadcast_select_fusion.1), channel_id=1, source_target_pairs={{0,4},{8,12},{2,6},{10,14},{33,37},{41,45},{35,39},{43,47},{66,70}... | collective-permute-start | bytes 2359304 | tf_op jit(solution)/shard_map/ppermute | solution.py:263
  62.9 10.9 %all-to-all-done.2.got = f32[16,8,1536]{2,1,0:T(8,128)S(1)} async-done(((f32[16,8,1536]{2,1,0:T(8,128)}), f32[16,8,1536]{2,1,0:T(8,128)S(1)}, u32[]{:S(2)}, u32[]{:S(2)}) %all-to-all-start.2) | async-done | bytes 786464 | tf_op jit(solution)/shard_map/all_to_all | solution.py:336
  74.4 3.7 %all-gather.1 = f32[16,768]{1,0:T(8,128)S(1)} all-gather(f32[8,768]{1,0:T(8,128)S(1)} %get-tuple-element.20), channel_id=3, replica_groups=mesh['z'=16,'c'=2,'x'=4,'y'=4] {'c'}, dimensions={0}, use_global_device_ids=true | all-gather | bytes 73728 | tf_op jit(solution)/shard_map/all_gather | solution.py:346
  78.8 3.7 %all-to-all-start.3 = ((f32[16,8,384]{2,1,0:T(8,128)}), f32[16,8,384]{2,1,0:T(8,128)S(1)}, u32[]{:S(2)}, u32[]{:S(2)}) async-start(f32[16,8,384]{2,1,0:T(8,128)} %broadcast_in_dim.7), calls=%async_computation.3 | async-start | bytes 393216 | tf_op jit(solution)/shard_map/all_to_all | solution.py:13
  82.6 2.1 %broadcast_select_fusion.2 = bf16[384,1024]{1,0:T(8,128)(2,1)} fusion(bf16[384,1024]{1,0:T(8,128)(2,1)} %collective-permute-done.2, bf16[384,1024]{1,0:T(8,128)(2,1)} %broadcast_select_fusion.1, pred[]{:T(512)S(6)} %eq.32), kind=kLoop, calls=%fused_computation.5 | loop fusion | flops 393216 | bytes 2359297 | tf_op jit(solution)/shard_map/jit(_where)/select_n | solution.py:266
  84.7 2.2 %collective-permute-start.3 = (bf16[384,1024]{1,0:T(8,128)(2,1)}, bf16[384,1024]{1,0:T(8,128)(2,1)}, u32[]{:S(2)}, u32[]{:S(2)}) collective-permute-start(bf16[384,1024]{1,0:T(8,128)(2,1)} %broadcast_select_fusion.2), channel_id=1, source_target_pairs={{0,1},{8,9},{2,3},{10,11},{4,5},{12,13},{6,7},{14,15},{33,34},{41,... | collective-permute-start | bytes 2359304 | tf_op jit(solution)/shard_map/ppermute | solution.py:263
  89.9 8.7 %all-to-all-done.3.got = f32[16,8,384]{2,1,0:T(8,128)S(1)} async-done(((f32[16,8,384]{2,1,0:T(8,128)}), f32[16,8,384]{2,1,0:T(8,128)S(1)}, u32[]{:S(2)}, u32[]{:S(2)}) %all-to-all-start.3) | async-done | bytes 196640 | tf_op jit(solution)/shard_map/all_to_all | solution.py:13
  98.6 0.9 shard_map.81
  99.4 4.8 %all-to-all-start.4 = ((f32[32,8,384]{2,1,0:T(8,128)}), f32[32,8,384]{2,1,0:T(8,128)S(1)}, u32[]{:S(2)}, u32[]{:S(2)}) async-start(f32[32,8,384]{2,1,0:T(8,128)} %shard_map.81), calls=%async_computation.4 | async-start | bytes 786432 | tf_op jit(solution)/shard_map/all_to_all | solution.py:366
  104.4 1.8 %convolution_add_fusion.base = f32[384,384]{1,0:T(8,128)S(1)} fusion(f32[384,384]{1,0:T(8,128)S(1)} %copy-done.2, bf16[1024,384]{1,0:T(8,128)(2,1)S(1)} %copy-done, bf16[384,1024]{1,0:T(8,128)(2,1)} %collective-permute-done.3, bf16[384,1024]{1,0:T(8,128)(2,1)} %broadcast_select_fusion.2, pred[]{:T(512)S(6)} %eq.35), kind=kOutput, calls=%fused_computation | convolution fusion | flops 302530560 | bytes 3538945 | tf_op jit(solution)/shard_map/dot_general | solution.py:364
  106.2 8.5 %all-to-all-done.4.blocks = f32[32,8,384]{2,1,0:T(8,128)S(1)} async-done(((f32[32,8,384]{2,1,0:T(8,128)}), f32[32,8,384]{2,1,0:T(8,128)S(1)}, u32[]{:S(2)}, u32[]{:S(2)}) %all-to-all-start.4) | async-done | bytes 393248 | tf_op jit(solution)/shard_map/all_to_all | solution.py:366
  114.7 1.6 %shard_map.82 = (f32[384,384]{1,0:T(8,128)}, f32[384,384]{1,0:T(8,128)}, f32[8,12288]{1,0:T(8,128)}) custom-call(f32[32,8,384]{2,1,0:T(8,128)S(1)} %all-to-all-done.4.blocks, f32[8,384]{1,0:T(8,128)S(1)} %fusion.7.ortho, f32[384,384]{1,0:T(8,128)S(1)} %convolution_add_fusion.base, f32[384,384]{1,0:T(8,128)S(1)} %copy-done.3), custom_call_target="tpu_custom_call" | custom-call | flops 2000000000 | bytes 3000000 | tf_op jit(solution)/shard_map/pallas_call | solution.py:368
  (38 shorter events, 6.0 us)
Async XLA Ops:
  0.6 9.4 %copy-start.1 = (f32[384,384]{1,0:T(8,128)S(1)}, f32[384,384]{1,0:T(8,128)}, u32[]{:S(2)}) copy-start(f32[384,384]{1,0:T(8,128)} %feed.3) | copy-start | bytes 1769476
  3.3 17.1 %all-to-all-start = ((f32[16,8,1024]{2,1,0:T(8,128)}), f32[16,8,1024]{2,1,0:T(8,128)S(1)}, u32[]{:S(2)}, u32[]{:S(2)}) async-start(f32[16,8,1024]{2,1,0:T(8,128)} %get-tuple-element.17), calls=%async_computation | async-start | bytes 1048576 | tf_op jit(solution)/shard_map/all_to_all | solution.py:307
  10.1 10.3 %copy-start = (bf16[1024,384]{1,0:T(8,128)(2,1)S(1)}, bf16[1024,384]{1,0:T(8,128)(2,1)}, u32[]{:S(2)}) copy-start(bf16[1024,384]{1,0:T(8,128)(2,1)} %act.3) | copy-start | bytes 2359300
  10.5 29.1 %collective-permute-start = (bf16[384,1024]{1,0:T(8,128)(2,1)S(1)}, bf16[384,1024]{1,0:T(8,128)(2,1)}, u32[]{:S(2)}, u32[]{:S(2)}) collective-permute-start(bf16[384,1024]{1,0:T(8,128)(2,1)S(1)} %get-tuple-element.23), channel_id=1, source_target_pairs={{0,8},{33,41},{66,74},{99,107},{132,140},{165,173},{198,206},{231,... | collective-permute-start | bytes 2359304 | tf_op jit(solution)/shard_map/ppermute | solution.py:263
  24.9 26.5 %all-to-all-start.1 = ((f32[16,4,384]{2,1,0:T(4,128)}), f32[16,4,384]{2,1,0:T(4,128)S(1)}, u32[]{:S(2)}, u32[]{:S(2)}) async-start(f32[16,4,384]{2,1,0:T(4,128)} %broadcast_in_dim.6), calls=%async_computation.1 | async-start | bytes 196608 | tf_op jit(solution)/shard_map/all_to_all | solution.py:13
  39.7 20.8 %collective-permute-start.1 = (bf16[384,1024]{1,0:T(8,128)(2,1)S(1)}, bf16[384,1024]{1,0:T(8,128)(2,1)}, u32[]{:S(2)}, u32[]{:S(2)}) collective-permute-start(bf16[384,1024]{1,0:T(8,128)(2,1)S(1)} %broadcast_select_fusion), channel_id=1, source_target_pairs={{0,2},{8,10},{33,35},{41,43},{66,64},{74,72},{99,97},{107,105},{13... | collective-permute-start | bytes 2359304 | tf_op jit(solution)/shard_map/ppermute | solution.py:263
  56.9 17.0 %all-to-all-start.2 = ((f32[16,8,1536]{2,1,0:T(8,128)}), f32[16,8,1536]{2,1,0:T(8,128)S(1)}, u32[]{:S(2)}, u32[]{:S(2)}) async-start(f32[16,8,1536]{2,1,0:T(8,128)} %shard_map.79), calls=%async_computation.2 | async-start | bytes 1572864 | tf_op jit(solution)/shard_map/all_to_all | solution.py:336
  60.5 2.3 %copy-start.4 = (bf16[768,1024]{1,0:T(8,128)(2,1)S(1)}, bf16[768,1024]{1,0:T(8,128)(2,1)}, u32[]{:S(2)}) copy-start(bf16[768,1024]{1,0:T(8,128)(2,1)} %hid.1) | copy-start | bytes 4718596
  61.5 21.1 %collective-permute-start.2 = (bf16[384,1024]{1,0:T(8,128)(2,1)}, bf16[384,1024]{1,0:T(8,128)(2,1)}, u32[]{:S(2)}, u32[]{:S(2)}) collective-permute-start(bf16[384,1024]{1,0:T(8,128)(2,1)} %broadcast_select_fusion.1), channel_id=1, source_target_pairs={{0,4},{8,12},{2,6},{10,14},{33,37},{41,45},{35,39},{43,47},{66,70}... | collective-permute-start | bytes 2359304 | tf_op jit(solution)/shard_map/ppermute | solution.py:263
  78.8 19.8 %all-to-all-start.3 = ((f32[16,8,384]{2,1,0:T(8,128)}), f32[16,8,384]{2,1,0:T(8,128)S(1)}, u32[]{:S(2)}, u32[]{:S(2)}) async-start(f32[16,8,384]{2,1,0:T(8,128)} %broadcast_in_dim.7), calls=%async_computation.3 | async-start | bytes 393216 | tf_op jit(solution)/shard_map/all_to_all | solution.py:13
  84.7 19.7 %collective-permute-start.3 = (bf16[384,1024]{1,0:T(8,128)(2,1)}, bf16[384,1024]{1,0:T(8,128)(2,1)}, u32[]{:S(2)}, u32[]{:S(2)}) collective-permute-start(bf16[384,1024]{1,0:T(8,128)(2,1)} %broadcast_select_fusion.2), channel_id=1, source_target_pairs={{0,1},{8,9},{2,3},{10,11},{4,5},{12,13},{6,7},{14,15},{33,34},{41,... | collective-permute-start | bytes 2359304 | tf_op jit(solution)/shard_map/ppermute | solution.py:263
  89.9 14.6 %copy-start.2 = (f32[384,384]{1,0:T(8,128)S(1)}, f32[384,384]{1,0:T(8,128)}, u32[]{:S(2)}) copy-start(f32[384,384]{1,0:T(8,128)} %feed.3) | copy-start | bytes 1769476
  99.4 15.3 %all-to-all-start.4 = ((f32[32,8,384]{2,1,0:T(8,128)}), f32[32,8,384]{2,1,0:T(8,128)S(1)}, u32[]{:S(2)}, u32[]{:S(2)}) async-start(f32[32,8,384]{2,1,0:T(8,128)} %shard_map.81), calls=%async_computation.4 | async-start | bytes 786432 | tf_op jit(solution)/shard_map/all_to_all | solution.py:366
  104.4 10.3 %copy-start.3 = (f32[384,384]{1,0:T(8,128)S(1)}, f32[384,384]{1,0:T(8,128)}, u32[]{:S(2)}) copy-start(f32[384,384]{1,0:T(8,128)} %momentum.1) | copy-start | bytes 1769476

commit v9 on v8

--- a/solution.py
+++ b/solution.py
@@ -161,6 +161,22 @@
         out[:, i * rows : (i + 1) * rows] = y + err * weight
 
 
+def ranks_kernel(got, out):
+    y = total(got, slice(None))
+    part = out.shape[1]
+    y = jnp.where(lax.axis_index("c") == 0, y[:part], y[part:])
+    for i in range(out.shape[0]):
+        out[i] = y
+
+
+def half_kernel(got, out):
+    rows = out.shape[2]
+    y = total(got, slice(None))
+    y = jnp.where(lax.axis_index("c") == 0, y[:, :rows], y[:, rows:])
+    for i in range(out.shape[0]):
+        out[i] = y
+
+
 def block_kernel(got, inverse, out):
     rows = total(got, slice(None))
     inv = inverse[...]
@@ -282,7 +298,7 @@
             pltpu.VMEM((rank, cols_mp), f32),
             pltpu.VMEM(hidden.shape, hidden.dtype),
             pltpu.VMEM((rank, toks), f32),
-            pltpu.SemaphoreType.DMA((8,)),
+            pltpu.SemaphoreType.DMA((5,)),
             pltpu.SemaphoreType.DMA((n_mp,)),
         ],
         compiler_params=pltpu.CompilerParams(vmem_limit_bytes=4 * 2**20),
@@ -313,12 +329,16 @@
         near(act_near),
         near(p_err),
     )
-    p_pair = lax.all_gather(p_part, "c").sum(0)
+    part = rank // nc
+    (p_pair,) = local(
+        ranks_kernel,
+        [pltpu.VMEM((nz, part, width), f32)],
+        1,
+        near(lax.all_gather(p_part, "c")),
+    )
     held = take(held, tie(got, p_pair), 0)
     got = send(held, 1)
-    part = rank // nc
-    p_pair = lax.dynamic_slice_in_dim(p_pair, core * part, part, 0)
-    p_half = copies(p_pair, "z", nz).sum(0)
+    p_half = lax.all_to_all(p_pair, "z", 0, 0).sum(0)
     held = take(held, got, 1)
     got = send(held, 2)
     p_sum = lax.all_gather(p_half, "c", tiled=True)
@@ -343,8 +363,12 @@
         near(hid_low),
     )
     gram_mat = gram_mat[:, :rank]
-    half = lax.all_gather(hid, "c").sum(0)
-    half = lax.dynamic_slice_in_dim(half, core * cols_dp, cols_dp, 1)
+    (half,) = local(
+        half_kernel,
+        [pltpu.VMEM((nz, rank, cols_dp), f32)],
+        1,
+        near(lax.all_gather(hid, "c")),
+    )
     held = take(held, tie(got, half), 2)
     got = send(held, 3)
     gram_mat = tie(gram_mat, held)
@@ -352,7 +376,7 @@
     inverse = lax.linalg.triangular_solve(
         factor, jnp.eye(rank, dtype=jnp.float32), left_side=True, lower=True
     )
-    half = near(copies(half, "z", nz))
+    half = near(lax.all_to_all(half, "z", 0, 0))
     (block,) = local(
         block_kernel,
         [pltpu.VMEM((n_dp, rank, cols_dp), f32)],

time: 117 us -> 117 us (level)
  Pallas kernels: 7.79 us -> 9.22 us
  local copies, waits for them, and re-layouts: 1.69 us -> 0.33 us
    pallas_call x5 -> x7, Pallas kernels: 3.59 us -> 4.96 us  [local(): pl.pallas_call(kernel, out_shape=outs, in_specs=[whole] * len(args), out_...]
    broadcast_in_dim x2 -> x0, local copies, waits for them, and re-layouts: 1.35 us -> none  [copies(): jnp.broadcast_to(x[None], (count,) + x.shape)]
  transfers between devices with their start and end apart: 9 -> 9, of which waited for: 5 -> 5; matrix products, arithmetic and copies ran while one was open for 8% -> 7% of each run, Pallas kernels for 3% -> 4%
where the time goes in v9:
time: 117 us; the launch traced here: 116 us
  waiting for transfers between devices  46.6 us (40%)
  starting transfers between devices  40.1 us (34%)
  blocking collectives  11.2 us (10%)
  Pallas kernels  9.22 us (8%)
  other arithmetic  5.98 us (5%)
  matrix products  2.09 us (2%)
    all_to_all x1, starting transfers between devices, per_device(): p_half = lax.all_to_all(p_pair, 'z', 0, 0).sum(0)  14.7 us
    all_to_all x1, waiting for transfers between devices, per_device(): packed = near(lax.all_to_all(packed, plane, 0, 0))  10.9 us
    all_to_all x1, waiting for transfers between devices, per_device(): p_half = lax.all_to_all(p_pair, 'z', 0, 0).sum(0)  10.2 us
    all_to_all x1, waiting for transfers between devices, per_device(): half = near(lax.all_to_all(half, 'z', 0, 0))  8.69 us
    all_to_all x1, waiting for transfers between devices, per_device(): blocks = near(lax.all_to_all(block, ('x', 'y', 'c'), 0, 0))  8.47 us
    all_to_all x1, waiting for transfers between devices, per_device(): tokens = near(lax.all_to_all(token_part, plane, 0, 0))  8.31 us
    all_to_all x1, starting transfers between devices, per_device(): tokens = near(lax.all_to_all(token_part, plane, 0, 0))  6.77 us
    ppermute x4, starting transfers between devices, send(): return lax.ppermute(held, ('z', 'c', 'x', 'y'), rounds[k])  6.61 us
  transfers between devices with their start and end apart: 9, of which 5 were waited for; matrix products, arithmetic and copies ran while one was open for 7% of the time, Pallas kernels for 4%

profile of v9, /device:TPU:33, one launch (start us, length us, event | category | flops | bytes accessed | tf_op | source)
XLA Modules:
  0.0 116.3 jit_solution(17413988470701825947)
XLA Ops:
  0.6 2.7 %shard_map.76 = (f32[16,8,1024]{2,1,0:T(8,128)}, f32[8,384]{1,0:T(8,128)S(1)}, bf16[384,1024]{1,0:T(8,128)(2,1)S(1)}) custom-call(f32[8,12288]{1,0:T(8,128)} %bitcast.21, bf16[768,1024]{1,0:T(8,128)(2,1)} %hid.1), custom_call_target="tpu_custom_call" | custom-call | flops 2000000000 | bytes 3000000 | tf_op jit(solution)/shard_map/pallas_call | solution.py:288
  3.3 6.8 %all-to-all-start = ((f32[16,8,1024]{2,1,0:T(8,128)}), f32[16,8,1024]{2,1,0:T(8,128)S(1)}, u32[]{:S(2)}, u32[]{:S(2)}) async-start(f32[16,8,1024]{2,1,0:T(8,128)} %get-tuple-element.17), calls=%async_computation | async-start | bytes 1048576 | tf_op jit(solution)/shard_map/all_to_all | solution.py:323
  10.5 1.6 %collective-permute-start = (bf16[384,1024]{1,0:T(8,128)(2,1)S(1)}, bf16[384,1024]{1,0:T(8,128)(2,1)}, u32[]{:S(2)}, u32[]{:S(2)}) collective-permute-start(bf16[384,1024]{1,0:T(8,128)(2,1)S(1)} %get-tuple-element.23), channel_id=1, source_target_pairs={{0,8},{33,41},{66,74},{99,107},{132,140},{165,173},{198,206},{231,... | collective-permute-start | bytes 2359304 | tf_op jit(solution)/shard_map/ppermute | solution.py:279
  12.1 8.3 %all-to-all-done.got = f32[16,8,1024]{2,1,0:T(8,128)S(1)} async-done(((f32[16,8,1024]{2,1,0:T(8,128)}), f32[16,8,1024]{2,1,0:T(8,128)S(1)}, u32[]{:S(2)}, u32[]{:S(2)}) %all-to-all-start) | async-done | bytes 524320 | tf_op jit(solution)/shard_map/all_to_all | solution.py:323
  20.7 3.6 %all-gather = f32[16,384]{1,0:T(8,128)S(1)} all-gather(f32[8,384]{1,0:T(8,128)S(1)} %shard_map.78), channel_id=2, replica_groups=mesh['z'=16,'c'=2,'x'=4,'y'=4] {'c'}, dimensions={0}, use_global_device_ids=true | all-gather | bytes 36864 | tf_op jit(solution)/shard_map/all_gather | solution.py:337
  24.9 14.7 %all-to-all-start.1 = ((f32[16,4,384]{2,1,0:T(4,128)}), f32[16,4,384]{2,1,0:T(4,128)S(1)}, u32[]{:S(2)}, u32[]{:S(2)}) async-start(f32[16,4,384]{2,1,0:T(4,128)} %shard_map.79), calls=%async_computation.1 | async-start | bytes 196608 | tf_op jit(solution)/shard_map/all_to_all | solution.py:341
  39.7 1.5 %collective-permute-start.1 = (bf16[384,1024]{1,0:T(8,128)(2,1)S(1)}, bf16[384,1024]{1,0:T(8,128)(2,1)}, u32[]{:S(2)}, u32[]{:S(2)}) collective-permute-start(bf16[384,1024]{1,0:T(8,128)(2,1)S(1)} %broadcast_select_fusion), channel_id=1, source_target_pairs={{0,2},{8,10},{33,35},{41,43},{66,64},{74,72},{99,97},{107,105},{13... | collective-permute-start | bytes 2359304 | tf_op jit(solution)/shard_map/ppermute | solution.py:279
  41.3 10.2 %all-to-all-done.1 = f32[16,4,384]{2,1,0:T(4,128)S(1)} async-done(((f32[16,4,384]{2,1,0:T(4,128)}), f32[16,4,384]{2,1,0:T(4,128)S(1)}, u32[]{:S(2)}, u32[]{:S(2)}) %all-to-all-start.1) | async-done | bytes 98336 | tf_op jit(solution)/shard_map/all_to_all | solution.py:341
  51.5 3.8 %all-gather.2 = f32[2,4,384]{2,1,0:T(4,128)S(1)} all-gather(f32[1,4,384]{2,1,0:T(4,128)S(1)} %bitcast.20), channel_id=1, replica_groups=mesh['z'=16,'c'=2,'x'=4,'y'=4] {'c'}, dimensions={0}, use_global_device_ids=true | all-gather | bytes 18432 | tf_op jit(solution)/shard_map/all_gather | solution.py:344
  55.3 1.6 %shard_map.80 = f32[16,8,1536]{2,1,0:T(8,128)} custom-call(f32[8,384]{1,0:T(8,128)S(1)} %reshape.18.p_ref, bf16[1024,384]{1,0:T(8,128)(2,1)S(1)} %copy-done, f32[384,384]{1,0:T(8,128)S(1)} %copy-done.1), custom_call_target="tpu_custom_call" | custom-call | flops 8000000000 | bytes 1388544 | tf_op jit(solution)/shard_map/pallas_call | solution.py:23
  56.9 3.6 %all-to-all-start.2 = ((f32[16,8,1536]{2,1,0:T(8,128)}), f32[16,8,1536]{2,1,0:T(8,128)S(1)}, u32[]{:S(2)}, u32[]{:S(2)}) async-start(f32[16,8,1536]{2,1,0:T(8,128)} %shard_map.80), calls=%async_computation.2 | async-start | bytes 1572864 | tf_op jit(solution)/shard_map/all_to_all | solution.py:356
  60.6 1.0 broadcast_select_fusion.1
  61.6 1.3 %collective-permute-start.2 = (bf16[384,1024]{1,0:T(8,128)(2,1)}, bf16[384,1024]{1,0:T(8,128)(2,1)}, u32[]{:S(2)}, u32[]{:S(2)}) collective-permute-start(bf16[384,1024]{1,0:T(8,128)(2,1)} %broadcast_select_fusion.1), channel_id=1, source_target_pairs={{0,4},{8,12},{2,6},{10,14},{33,37},{41,45},{35,39},{43,47},{66,70}... | collective-permute-start | bytes 2359304 | tf_op jit(solution)/shard_map/ppermute | solution.py:279
  63.0 10.9 %all-to-all-done.2.got = f32[16,8,1536]{2,1,0:T(8,128)S(1)} async-done(((f32[16,8,1536]{2,1,0:T(8,128)}), f32[16,8,1536]{2,1,0:T(8,128)S(1)}, u32[]{:S(2)}, u32[]{:S(2)}) %all-to-all-start.2) | async-done | bytes 786464 | tf_op jit(solution)/shard_map/all_to_all | solution.py:356
  74.5 3.7 %all-gather.1 = f32[16,768]{1,0:T(8,128)S(1)} all-gather(f32[8,768]{1,0:T(8,128)S(1)} %get-tuple-element.20), channel_id=3, replica_groups=mesh['z'=16,'c'=2,'x'=4,'y'=4] {'c'}, dimensions={0}, use_global_device_ids=true | all-gather | bytes 73728 | tf_op jit(solution)/shard_map/all_gather | solution.py:370
  78.9 3.7 %all-to-all-start.3 = ((f32[16,8,384]{2,1,0:T(8,128)}), f32[16,8,384]{2,1,0:T(8,128)S(1)}, u32[]{:S(2)}, u32[]{:S(2)}) async-start(f32[16,8,384]{2,1,0:T(8,128)} %shard_map.82), calls=%async_computation.3 | async-start | bytes 393216 | tf_op jit(solution)/shard_map/all_to_all | solution.py:379
  82.7 2.2 %broadcast_select_fusion.2 = bf16[384,1024]{1,0:T(8,128)(2,1)} fusion(bf16[384,1024]{1,0:T(8,128)(2,1)} %collective-permute-done.2, bf16[384,1024]{1,0:T(8,128)(2,1)} %broadcast_select_fusion.1, pred[]{:T(512)S(6)} %eq.32), kind=kLoop, calls=%fused_computation.5 | loop fusion | flops 393216 | bytes 2359297 | tf_op jit(solution)/shard_map/jit(_where)/select_n | solution.py:282
  84.8 2.2 %collective-permute-start.3 = (bf16[384,1024]{1,0:T(8,128)(2,1)}, bf16[384,1024]{1,0:T(8,128)(2,1)}, u32[]{:S(2)}, u32[]{:S(2)}) collective-permute-start(bf16[384,1024]{1,0:T(8,128)(2,1)} %broadcast_select_fusion.2), channel_id=1, source_target_pairs={{0,1},{8,9},{2,3},{10,11},{4,5},{12,13},{6,7},{14,15},{33,34},{41,... | collective-permute-start | bytes 2359304 | tf_op jit(solution)/shard_map/ppermute | solution.py:279
  90.0 8.7 %all-to-all-done.3.got = f32[16,8,384]{2,1,0:T(8,128)S(1)} async-done(((f32[16,8,384]{2,1,0:T(8,128)}), f32[16,8,384]{2,1,0:T(8,128)S(1)}, u32[]{:S(2)}, u32[]{:S(2)}) %all-to-all-start.3) | async-done | bytes 196640 | tf_op jit(solution)/shard_map/all_to_all | solution.py:379
  98.6 0.9 shard_map.83
  99.5 4.8 %all-to-all-start.4 = ((f32[32,8,384]{2,1,0:T(8,128)}), f32[32,8,384]{2,1,0:T(8,128)S(1)}, u32[]{:S(2)}, u32[]{:S(2)}) async-start(f32[32,8,384]{2,1,0:T(8,128)} %shard_map.83), calls=%async_computation.4 | async-start | bytes 786432 | tf_op jit(solution)/shard_map/all_to_all | solution.py:390
  104.5 1.8 %convolution_add_fusion.base = f32[384,384]{1,0:T(8,128)S(1)} fusion(f32[384,384]{1,0:T(8,128)S(1)} %copy-done.2, bf16[1024,384]{1,0:T(8,128)(2,1)S(1)} %copy-done, bf16[384,1024]{1,0:T(8,128)(2,1)} %collective-permute-done.3, bf16[384,1024]{1,0:T(8,128)(2,1)} %broadcast_select_fusion.2, pred[]{:T(512)S(6)} %eq.35), kind=kOutput, calls=%fused_computation | convolution fusion | flops 302530560 | bytes 3538945 | tf_op jit(solution)/shard_map/dot_general | solution.py:388
  106.3 8.5 %all-to-all-done.4.blocks = f32[32,8,384]{2,1,0:T(8,128)S(1)} async-done(((f32[32,8,384]{2,1,0:T(8,128)}), f32[32,8,384]{2,1,0:T(8,128)S(1)}, u32[]{:S(2)}, u32[]{:S(2)}) %all-to-all-start.4) | async-done | bytes 393248 | tf_op jit(solution)/shard_map/all_to_all | solution.py:390
  114.7 1.6 %shard_map.84 = (f32[384,384]{1,0:T(8,128)}, f32[384,384]{1,0:T(8,128)}, f32[8,12288]{1,0:T(8,128)}) custom-call(f32[32,8,384]{2,1,0:T(8,128)S(1)} %all-to-all-done.4.blocks, f32[8,384]{1,0:T(8,128)S(1)} %fusion.7.ortho, f32[384,384]{1,0:T(8,128)S(1)} %convolution_add_fusion.base, f32[384,384]{1,0:T(8,128)S(1)} %copy-done.3), custom_call_target="tpu_custom_call" | custom-call | flops 2000000000 | bytes 3000000 | tf_op jit(solution)/shard_map/pallas_call | solution.py:392
  (34 shorter events, 6.0 us)
Async XLA Ops:
  0.6 9.5 %copy-start.1 = (f32[384,384]{1,0:T(8,128)S(1)}, f32[384,384]{1,0:T(8,128)}, u32[]{:S(2)}) copy-start(f32[384,384]{1,0:T(8,128)} %feed.3) | copy-start | bytes 1769476
  3.3 17.1 %all-to-all-start = ((f32[16,8,1024]{2,1,0:T(8,128)}), f32[16,8,1024]{2,1,0:T(8,128)S(1)}, u32[]{:S(2)}, u32[]{:S(2)}) async-start(f32[16,8,1024]{2,1,0:T(8,128)} %get-tuple-element.17), calls=%async_computation | async-start | bytes 1048576 | tf_op jit(solution)/shard_map/all_to_all | solution.py:323
  10.1 10.3 %copy-start = (bf16[1024,384]{1,0:T(8,128)(2,1)S(1)}, bf16[1024,384]{1,0:T(8,128)(2,1)}, u32[]{:S(2)}) copy-start(bf16[1024,384]{1,0:T(8,128)(2,1)} %act.3) | copy-start | bytes 2359300
  10.5 29.1 %collective-permute-start = (bf16[384,1024]{1,0:T(8,128)(2,1)S(1)}, bf16[384,1024]{1,0:T(8,128)(2,1)}, u32[]{:S(2)}, u32[]{:S(2)}) collective-permute-start(bf16[384,1024]{1,0:T(8,128)(2,1)S(1)} %get-tuple-element.23), channel_id=1, source_target_pairs={{0,8},{33,41},{66,74},{99,107},{132,140},{165,173},{198,206},{231,... | collective-permute-start | bytes 2359304 | tf_op jit(solution)/shard_map/ppermute | solution.py:279
  24.9 26.5 %all-to-all-start.1 = ((f32[16,4,384]{2,1,0:T(4,128)}), f32[16,4,384]{2,1,0:T(4,128)S(1)}, u32[]{:S(2)}, u32[]{:S(2)}) async-start(f32[16,4,384]{2,1,0:T(4,128)} %shard_map.79), calls=%async_computation.1 | async-start | bytes 196608 | tf_op jit(solution)/shard_map/all_to_all | solution.py:341
  39.7 20.9 %collective-permute-start.1 = (bf16[384,1024]{1,0:T(8,128)(2,1)S(1)}, bf16[384,1024]{1,0:T(8,128)(2,1)}, u32[]{:S(2)}, u32[]{:S(2)}) collective-permute-start(bf16[384,1024]{1,0:T(8,128)(2,1)S(1)} %broadcast_select_fusion), channel_id=1, source_target_pairs={{0,2},{8,10},{33,35},{41,43},{66,64},{74,72},{99,97},{107,105},{13... | collective-permute-start | bytes 2359304 | tf_op jit(solution)/shard_map/ppermute | solution.py:279
  56.9 17.0 %all-to-all-start.2 = ((f32[16,8,1536]{2,1,0:T(8,128)}), f32[16,8,1536]{2,1,0:T(8,128)S(1)}, u32[]{:S(2)}, u32[]{:S(2)}) async-start(f32[16,8,1536]{2,1,0:T(8,128)} %shard_map.80), calls=%async_computation.2 | async-start | bytes 1572864 | tf_op jit(solution)/shard_map/all_to_all | solution.py:356
  60.6 2.3 %copy-start.4 = (bf16[768,1024]{1,0:T(8,128)(2,1)S(1)}, bf16[768,1024]{1,0:T(8,128)(2,1)}, u32[]{:S(2)}) copy-start(bf16[768,1024]{1,0:T(8,128)(2,1)} %hid.1) | copy-start | bytes 4718596
  61.6 21.1 %collective-permute-start.2 = (bf16[384,1024]{1,0:T(8,128)(2,1)}, bf16[384,1024]{1,0:T(8,128)(2,1)}, u32[]{:S(2)}, u32[]{:S(2)}) collective-permute-start(bf16[384,1024]{1,0:T(8,128)(2,1)} %broadcast_select_fusion.1), channel_id=1, source_target_pairs={{0,4},{8,12},{2,6},{10,14},{33,37},{41,45},{35,39},{43,47},{66,70}... | collective-permute-start | bytes 2359304 | tf_op jit(solution)/shard_map/ppermute | solution.py:279
  78.9 19.8 %all-to-all-start.3 = ((f32[16,8,384]{2,1,0:T(8,128)}), f32[16,8,384]{2,1,0:T(8,128)S(1)}, u32[]{:S(2)}, u32[]{:S(2)}) async-start(f32[16,8,384]{2,1,0:T(8,128)} %shard_map.82), calls=%async_computation.3 | async-start | bytes 393216 | tf_op jit(solution)/shard_map/all_to_all | solution.py:379
  84.8 19.6 %collective-permute-start.3 = (bf16[384,1024]{1,0:T(8,128)(2,1)}, bf16[384,1024]{1,0:T(8,128)(2,1)}, u32[]{:S(2)}, u32[]{:S(2)}) collective-permute-start(bf16[384,1024]{1,0:T(8,128)(2,1)} %broadcast_select_fusion.2), channel_id=1, source_target_pairs={{0,1},{8,9},{2,3},{10,11},{4,5},{12,13},{6,7},{14,15},{33,34},{41,... | collective-permute-start | bytes 2359304 | tf_op jit(solution)/shard_map/ppermute | solution.py:279
  90.0 14.5 %copy-start.2 = (f32[384,384]{1,0:T(8,128)S(1)}, f32[384,384]{1,0:T(8,128)}, u32[]{:S(2)}) copy-start(f32[384,384]{1,0:T(8,128)} %feed.3) | copy-start | bytes 1769476
  99.5 15.2 %all-to-all-start.4 = ((f32[32,8,384]{2,1,0:T(8,128)}), f32[32,8,384]{2,1,0:T(8,128)S(1)}, u32[]{:S(2)}, u32[]{:S(2)}) async-start(f32[32,8,384]{2,1,0:T(8,128)} %shard_map.83), calls=%async_computation.4 | async-start | bytes 786432 | tf_op jit(solution)/shard_map/all_to_all | solution.py:390
  104.5 10.3 %copy-start.3 = (f32[384,384]{1,0:T(8,128)S(1)}, f32[384,384]{1,0:T(8,128)}, u32[]{:S(2)}) copy-start(f32[384,384]{1,0:T(8,128)} %momentum.1) | copy-start | bytes 1769476

commit v10 on v9

--- a/solution.py
+++ b/solution.py
@@ -189,15 +189,20 @@
 
 
 def last_kernel(
-    blocks, ortho, base, momentum, feed_out, mom_out, q_out, feed_new, mom_new, sems
+    blocks, ortho, base, momentum, feed_out, mom_out, q_out, feed_new, mom_new, q_new, sems
 ):
     count, _, rows = blocks.shape
     sends = []
+    group = count // 4
     for i in range(count):
-        there = q_out.at[:, pl.ds(i * rows, rows)]
-        sends.append(pltpu.make_async_copy(blocks.at[i], there, sems.at[i]))
-    for send in sends:
-        send.start()
+        q_new[:, i * rows : (i + 1) * rows] = blocks[i]
+        if (i + 1) % group == 0:
+            span = pl.ds((i + 1 - group) * rows, group * rows)
+            send = pltpu.make_async_copy(
+                q_new.at[:, span], q_out.at[:, span], sems.at[i // group]
+            )
+            send.start()
+            sends.append(send)
     replica = lax.axis_index("z") * lax.axis_size("c") + lax.axis_index("c")
     a, b, c = three(blocks[replica])
     left = jnp.concatenate([c, b, a, b, a, a], 0).astype(jnp.bfloat16)
@@ -217,7 +222,7 @@
         for j, (here, there) in enumerate(((feed_new, feed_out), (mom_new, mom_out))):
             span = pl.ds(i * part, part)
             send = pltpu.make_async_copy(
-                here.at[span], there.at[span], sems.at[count + 2 * i + j]
+                here.at[span], there.at[span], sems.at[4 + 2 * i + j]
             )
             send.start()
             sends.append(send)
@@ -401,7 +406,8 @@
         scratch_shapes=[
             pltpu.VMEM(feedback.shape, f32),
             pltpu.VMEM(momentum.shape, f32),
-            pltpu.SemaphoreType.DMA((n_dp + 6,)),
+            pltpu.VMEM(q_rows.shape, f32),
+            pltpu.SemaphoreType.DMA((10,)),
         ],
         compiler_params=pltpu.CompilerParams(vmem_limit_bytes=4 * 2**20),
         cost_estimate=pl.CostEstimate(

time: 117 us -> 117 us (level)
  no operation moved by 1% of the time
where the time goes in v10:
time: 117 us; the launch traced here: 116 us
  waiting for transfers between devices  46.6 us (40%)
  starting transfers between devices  40.1 us (34%)
  blocking collectives  11.2 us (10%)
  Pallas kernels  9.01 us (8%)
  other arithmetic  5.98 us (5%)
  matrix products  2.09 us (2%)
    all_to_all x1, starting transfers between devices, per_device(): p_half = lax.all_to_all(p_pair, 'z', 0, 0).sum(0)  14.7 us
    all_to_all x1, waiting for transfers between devices, per_device(): packed = near(lax.all_to_all(packed, plane, 0, 0))  10.9 us
    all_to_all x1, waiting for transfers between devices, per_device(): p_half = lax.all_to_all(p_pair, 'z', 0, 0).sum(0)  10.2 us
    all_to_all x1, waiting for transfers between devices, per_device(): half = near(lax.all_to_all(half, 'z', 0, 0))  8.69 us
    all_to_all x1, waiting for transfers between devices, per_device(): blocks = near(lax.all_to_all(block, ('x', 'y', 'c'), 0, 0))  8.47 us
    all_to_all x1, waiting for transfers between devices, per_device(): tokens = near(lax.all_to_all(token_part, plane, 0, 0))  8.31 us
    all_to_all x1, starting transfers between devices, per_device(): tokens = near(lax.all_to_all(token_part, plane, 0, 0))  6.77 us
    ppermute x4, starting transfers between devices, send(): return lax.ppermute(held, ('z', 'c', 'x', 'y'), rounds[k])  6.61 us
  transfers between devices with their start and end apart: 9, of which 5 were waited for; matrix products, arithmetic and copies ran while one was open for 7% of the time, Pallas kernels for 4%

profile of v10, /device:TPU:33, one launch (start us, length us, event | category | flops | bytes accessed | tf_op | source)
XLA Modules:
  0.0 116.1 jit_solution(6944197968878887583)
XLA Ops:
  0.6 2.7 %shard_map.76 = (f32[16,8,1024]{2,1,0:T(8,128)}, f32[8,384]{1,0:T(8,128)S(1)}, bf16[384,1024]{1,0:T(8,128)(2,1)S(1)}) custom-call(f32[8,12288]{1,0:T(8,128)} %bitcast.21, bf16[768,1024]{1,0:T(8,128)(2,1)} %hid.1), custom_call_target="tpu_custom_call" | custom-call | flops 2000000000 | bytes 3000000 | tf_op jit(solution)/shard_map/pallas_call | solution.py:293
  3.3 6.8 %all-to-all-start = ((f32[16,8,1024]{2,1,0:T(8,128)}), f32[16,8,1024]{2,1,0:T(8,128)S(1)}, u32[]{:S(2)}, u32[]{:S(2)}) async-start(f32[16,8,1024]{2,1,0:T(8,128)} %get-tuple-element.17), calls=%async_computation | async-start | bytes 1048576 | tf_op jit(solution)/shard_map/all_to_all | solution.py:328
  10.5 1.6 %collective-permute-start = (bf16[384,1024]{1,0:T(8,128)(2,1)S(1)}, bf16[384,1024]{1,0:T(8,128)(2,1)}, u32[]{:S(2)}, u32[]{:S(2)}) collective-permute-start(bf16[384,1024]{1,0:T(8,128)(2,1)S(1)} %get-tuple-element.23), channel_id=1, source_target_pairs={{0,8},{33,41},{66,74},{99,107},{132,140},{165,173},{198,206},{231,... | collective-permute-start | bytes 2359304 | tf_op jit(solution)/shard_map/ppermute | solution.py:284
  12.1 8.3 %all-to-all-done.got = f32[16,8,1024]{2,1,0:T(8,128)S(1)} async-done(((f32[16,8,1024]{2,1,0:T(8,128)}), f32[16,8,1024]{2,1,0:T(8,128)S(1)}, u32[]{:S(2)}, u32[]{:S(2)}) %all-to-all-start) | async-done | bytes 524320 | tf_op jit(solution)/shard_map/all_to_all | solution.py:328
  20.7 3.6 %all-gather = f32[16,384]{1,0:T(8,128)S(1)} all-gather(f32[8,384]{1,0:T(8,128)S(1)} %shard_map.78), channel_id=2, replica_groups=mesh['z'=16,'c'=2,'x'=4,'y'=4] {'c'}, dimensions={0}, use_global_device_ids=true | all-gather | bytes 36864 | tf_op jit(solution)/shard_map/all_gather | solution.py:342
  24.9 14.7 %all-to-all-start.1 = ((f32[16,4,384]{2,1,0:T(4,128)}), f32[16,4,384]{2,1,0:T(4,128)S(1)}, u32[]{:S(2)}, u32[]{:S(2)}) async-start(f32[16,4,384]{2,1,0:T(4,128)} %shard_map.79), calls=%async_computation.1 | async-start | bytes 196608 | tf_op jit(solution)/shard_map/all_to_all | solution.py:346
  39.7 1.5 %collective-permute-start.1 = (bf16[384,1024]{1,0:T(8,128)(2,1)S(1)}, bf16[384,1024]{1,0:T(8,128)(2,1)}, u32[]{:S(2)}, u32[]{:S(2)}) collective-permute-start(bf16[384,1024]{1,0:T(8,128)(2,1)S(1)} %broadcast_select_fusion), channel_id=1, source_target_pairs={{0,2},{8,10},{33,35},{41,43},{66,64},{74,72},{99,97},{107,105},{13... | collective-permute-start | bytes 2359304 | tf_op jit(solution)/shard_map/ppermute | solution.py:284
  41.3 10.2 %all-to-all-done.1 = f32[16,4,384]{2,1,0:T(4,128)S(1)} async-done(((f32[16,4,384]{2,1,0:T(4,128)}), f32[16,4,384]{2,1,0:T(4,128)S(1)}, u32[]{:S(2)}, u32[]{:S(2)}) %all-to-all-start.1) | async-done | bytes 98336 | tf_op jit(solution)/shard_map/all_to_all | solution.py:346
  51.5 3.8 %all-gather.2 = f32[2,4,384]{2,1,0:T(4,128)S(1)} all-gather(f32[1,4,384]{2,1,0:T(4,128)S(1)} %bitcast.20), channel_id=1, replica_groups=mesh['z'=16,'c'=2,'x'=4,'y'=4] {'c'}, dimensions={0}, use_global_device_ids=true | all-gather | bytes 18432 | tf_op jit(solution)/shard_map/all_gather | solution.py:349
  55.3 1.6 %shard_map.80 = f32[16,8,1536]{2,1,0:T(8,128)} custom-call(f32[8,384]{1,0:T(8,128)S(1)} %reshape.18.p_ref, bf16[1024,384]{1,0:T(8,128)(2,1)S(1)} %copy-done, f32[384,384]{1,0:T(8,128)S(1)} %copy-done.1), custom_call_target="tpu_custom_call" | custom-call | flops 8000000000 | bytes 1388544 | tf_op jit(solution)/shard_map/pallas_call | solution.py:23
  56.9 3.6 %all-to-all-start.2 = ((f32[16,8,1536]{2,1,0:T(8,128)}), f32[16,8,1536]{2,1,0:T(8,128)S(1)}, u32[]{:S(2)}, u32[]{:S(2)}) async-start(f32[16,8,1536]{2,1,0:T(8,128)} %shard_map.80), calls=%async_computation.2 | async-start | bytes 1572864 | tf_op jit(solution)/shard_map/all_to_all | solution.py:361
  60.6 1.0 broadcast_select_fusion.1
  61.6 1.3 %collective-permute-start.2 = (bf16[384,1024]{1,0:T(8,128)(2,1)}, bf16[384,1024]{1,0:T(8,128)(2,1)}, u32[]{:S(2)}, u32[]{:S(2)}) collective-permute-start(bf16[384,1024]{1,0:T(8,128)(2,1)} %broadcast_select_fusion.1), channel_id=1, source_target_pairs={{0,4},{8,12},{2,6},{10,14},{33,37},{41,45},{35,39},{43,47},{66,70}... | collective-permute-start | bytes 2359304 | tf_op jit(solution)/shard_map/ppermute | solution.py:284
  63.0 10.9 %all-to-all-done.2.got = f32[16,8,1536]{2,1,0:T(8,128)S(1)} async-done(((f32[16,8,1536]{2,1,0:T(8,128)}), f32[16,8,1536]{2,1,0:T(8,128)S(1)}, u32[]{:S(2)}, u32[]{:S(2)}) %all-to-all-start.2) | async-done | bytes 786464 | tf_op jit(solution)/shard_map/all_to_all | solution.py:361
  74.5 3.7 %all-gather.1 = f32[16,768]{1,0:T(8,128)S(1)} all-gather(f32[8,768]{1,0:T(8,128)S(1)} %get-tuple-element.20), channel_id=3, replica_groups=mesh['z'=16,'c'=2,'x'=4,'y'=4] {'c'}, dimensions={0}, use_global_device_ids=true | all-gather | bytes 73728 | tf_op jit(solution)/shard_map/all_gather | solution.py:375
  78.9 3.7 %all-to-all-start.3 = ((f32[16,8,384]{2,1,0:T(8,128)}), f32[16,8,384]{2,1,0:T(8,128)S(1)}, u32[]{:S(2)}, u32[]{:S(2)}) async-start(f32[16,8,384]{2,1,0:T(8,128)} %shard_map.82), calls=%async_computation.3 | async-start | bytes 393216 | tf_op jit(solution)/shard_map/all_to_all | solution.py:384
  82.7 2.2 %broadcast_select_fusion.2 = bf16[384,1024]{1,0:T(8,128)(2,1)} fusion(bf16[384,1024]{1,0:T(8,128)(2,1)} %collective-permute-done.2, bf16[384,1024]{1,0:T(8,128)(2,1)} %broadcast_select_fusion.1, pred[]{:T(512)S(6)} %eq.32), kind=kLoop, calls=%fused_computation.5 | loop fusion | flops 393216 | bytes 2359297 | tf_op jit(solution)/shard_map/jit(_where)/select_n | solution.py:287
  84.8 2.2 %collective-permute-start.3 = (bf16[384,1024]{1,0:T(8,128)(2,1)}, bf16[384,1024]{1,0:T(8,128)(2,1)}, u32[]{:S(2)}, u32[]{:S(2)}) collective-permute-start(bf16[384,1024]{1,0:T(8,128)(2,1)} %broadcast_select_fusion.2), channel_id=1, source_target_pairs={{0,1},{8,9},{2,3},{10,11},{4,5},{12,13},{6,7},{14,15},{33,34},{41,... | collective-permute-start | bytes 2359304 | tf_op jit(solution)/shard_map/ppermute | solution.py:284
  90.0 8.7 %all-to-all-done.3.got = f32[16,8,384]{2,1,0:T(8,128)S(1)} async-done(((f32[16,8,384]{2,1,0:T(8,128)}), f32[16,8,384]{2,1,0:T(8,128)S(1)}, u32[]{:S(2)}, u32[]{:S(2)}) %all-to-all-start.3) | async-done | bytes 196640 | tf_op jit(solution)/shard_map/all_to_all | solution.py:384
  98.6 0.9 shard_map.83
  99.5 4.8 %all-to-all-start.4 = ((f32[32,8,384]{2,1,0:T(8,128)}), f32[32,8,384]{2,1,0:T(8,128)S(1)}, u32[]{:S(2)}, u32[]{:S(2)}) async-start(f32[32,8,384]{2,1,0:T(8,128)} %shard_map.83), calls=%async_computation.4 | async-start | bytes 786432 | tf_op jit(solution)/shard_map/all_to_all | solution.py:395
  104.5 1.8 %convolution_add_fusion.base = f32[384,384]{1,0:T(8,128)S(1)} fusion(f32[384,384]{1,0:T(8,128)S(1)} %copy-done.2, bf16[1024,384]{1,0:T(8,128)(2,1)S(1)} %copy-done, bf16[384,1024]{1,0:T(8,128)(2,1)} %collective-permute-done.3, bf16[384,1024]{1,0:T(8,128)(2,1)} %broadcast_select_fusion.2, pred[]{:T(512)S(6)} %eq.35), kind=kOutput, calls=%fused_computation | convolution fusion | flops 302530560 | bytes 3538945 | tf_op jit(solution)/shard_map/dot_general | solution.py:393
  106.3 8.5 %all-to-all-done.4.blocks = f32[32,8,384]{2,1,0:T(8,128)S(1)} async-done(((f32[32,8,384]{2,1,0:T(8,128)}), f32[32,8,384]{2,1,0:T(8,128)S(1)}, u32[]{:S(2)}, u32[]{:S(2)}) %all-to-all-start.4) | async-done | bytes 393248 | tf_op jit(solution)/shard_map/all_to_all | solution.py:395
  114.7 1.4 %shard_map.84 = (f32[384,384]{1,0:T(8,128)}, f32[384,384]{1,0:T(8,128)}, f32[8,12288]{1,0:T(8,128)}) custom-call(f32[32,8,384]{2,1,0:T(8,128)S(1)} %all-to-all-done.4.blocks, f32[8,384]{1,0:T(8,128)S(1)} %fusion.7.ortho, f32[384,384]{1,0:T(8,128)S(1)} %convolution_add_fusion.base, f32[384,384]{1,0:T(8,128)S(1)} %copy-done.3), custom_call_target="tpu_custom_call" | custom-call | flops 2000000000 | bytes 3000000 | tf_op jit(solution)/shard_map/pallas_call | solution.py:397
  (34 shorter events, 6.0 us)
Async XLA Ops:
  0.6 9.5 %copy-start.1 = (f32[384,384]{1,0:T(8,128)S(1)}, f32[384,384]{1,0:T(8,128)}, u32[]{:S(2)}) copy-start(f32[384,384]{1,0:T(8,128)} %feed.3) | copy-start | bytes 1769476
  3.3 17.1 %all-to-all-start = ((f32[16,8,1024]{2,1,0:T(8,128)}), f32[16,8,1024]{2,1,0:T(8,128)S(1)}, u32[]{:S(2)}, u32[]{:S(2)}) async-start(f32[16,8,1024]{2,1,0:T(8,128)} %get-tuple-element.17), calls=%async_computation | async-start | bytes 1048576 | tf_op jit(solution)/shard_map/all_to_all | solution.py:328
  10.1 10.3 %copy-start = (bf16[1024,384]{1,0:T(8,128)(2,1)S(1)}, bf16[1024,384]{1,0:T(8,128)(2,1)}, u32[]{:S(2)}) copy-start(bf16[1024,384]{1,0:T(8,128)(2,1)} %act.3) | copy-start | bytes 2359300
  10.5 29.1 %collective-permute-start = (bf16[384,1024]{1,0:T(8,128)(2,1)S(1)}, bf16[384,1024]{1,0:T(8,128)(2,1)}, u32[]{:S(2)}, u32[]{:S(2)}) collective-permute-start(bf16[384,1024]{1,0:T(8,128)(2,1)S(1)} %get-tuple-element.23), channel_id=1, source_target_pairs={{0,8},{33,41},{66,74},{99,107},{132,140},{165,173},{198,206},{231,... | collective-permute-start | bytes 2359304 | tf_op jit(solution)/shard_map/ppermute | solution.py:284
  24.9 26.5 %all-to-all-start.1 = ((f32[16,4,384]{2,1,0:T(4,128)}), f32[16,4,384]{2,1,0:T(4,128)S(1)}, u32[]{:S(2)}, u32[]{:S(2)}) async-start(f32[16,4,384]{2,1,0:T(4,128)} %shard_map.79), calls=%async_computation.1 | async-start | bytes 196608 | tf_op jit(solution)/shard_map/all_to_all | solution.py:346
  39.7 20.9 %collective-permute-start.1 = (bf16[384,1024]{1,0:T(8,128)(2,1)S(1)}, bf16[384,1024]{1,0:T(8,128)(2,1)}, u32[]{:S(2)}, u32[]{:S(2)}) collective-permute-start(bf16[384,1024]{1,0:T(8,128)(2,1)S(1)} %broadcast_select_fusion), channel_id=1, source_target_pairs={{0,2},{8,10},{33,35},{41,43},{66,64},{74,72},{99,97},{107,105},{13... | collective-permute-start | bytes 2359304 | tf_op jit(solution)/shard_map/ppermute | solution.py:284
  56.9 17.0 %all-to-all-start.2 = ((f32[16,8,1536]{2,1,0:T(8,128)}), f32[16,8,1536]{2,1,0:T(8,128)S(1)}, u32[]{:S(2)}, u32[]{:S(2)}) async-start(f32[16,8,1536]{2,1,0:T(8,128)} %shard_map.80), calls=%async_computation.2 | async-start | bytes 1572864 | tf_op jit(solution)/shard_map/all_to_all | solution.py:361
  60.6 2.3 %copy-start.4 = (bf16[768,1024]{1,0:T(8,128)(2,1)S(1)}, bf16[768,1024]{1,0:T(8,128)(2,1)}, u32[]{:S(2)}) copy-start(bf16[768,1024]{1,0:T(8,128)(2,1)} %hid.1) | copy-start | bytes 4718596
  61.6 21.1 %collective-permute-start.2 = (bf16[384,1024]{1,0:T(8,128)(2,1)}, bf16[384,1024]{1,0:T(8,128)(2,1)}, u32[]{:S(2)}, u32[]{:S(2)}) collective-permute-start(bf16[384,1024]{1,0:T(8,128)(2,1)} %broadcast_select_fusion.1), channel_id=1, source_target_pairs={{0,4},{8,12},{2,6},{10,14},{33,37},{41,45},{35,39},{43,47},{66,70}... | collective-permute-start | bytes 2359304 | tf_op jit(solution)/shard_map/ppermute | solution.py:284
  78.9 19.8 %all-to-all-start.3 = ((f32[16,8,384]{2,1,0:T(8,128)}), f32[16,8,384]{2,1,0:T(8,128)S(1)}, u32[]{:S(2)}, u32[]{:S(2)}) async-start(f32[16,8,384]{2,1,0:T(8,128)} %shard_map.82), calls=%async_computation.3 | async-start | bytes 393216 | tf_op jit(solution)/shard_map/all_to_all | solution.py:384
  84.8 19.6 %collective-permute-start.3 = (bf16[384,1024]{1,0:T(8,128)(2,1)}, bf16[384,1024]{1,0:T(8,128)(2,1)}, u32[]{:S(2)}, u32[]{:S(2)}) collective-permute-start(bf16[384,1024]{1,0:T(8,128)(2,1)} %broadcast_select_fusion.2), channel_id=1, source_target_pairs={{0,1},{8,9},{2,3},{10,11},{4,5},{12,13},{6,7},{14,15},{33,34},{41,... | collective-permute-start | bytes 2359304 | tf_op jit(solution)/shard_map/ppermute | solution.py:284
  90.0 14.5 %copy-start.2 = (f32[384,384]{1,0:T(8,128)S(1)}, f32[384,384]{1,0:T(8,128)}, u32[]{:S(2)}) copy-start(f32[384,384]{1,0:T(8,128)} %feed.3) | copy-start | bytes 1769476
  99.5 15.2 %all-to-all-start.4 = ((f32[32,8,384]{2,1,0:T(8,128)}), f32[32,8,384]{2,1,0:T(8,128)S(1)}, u32[]{:S(2)}, u32[]{:S(2)}) async-start(f32[32,8,384]{2,1,0:T(8,128)} %shard_map.83), calls=%async_computation.4 | async-start | bytes 786432 | tf_op jit(solution)/shard_map/all_to_all | solution.py:395
  104.5 10.3 %copy-start.3 = (f32[384,384]{1,0:T(8,128)S(1)}, f32[384,384]{1,0:T(8,128)}, u32[]{:S(2)}) copy-start(f32[384,384]{1,0:T(8,128)} %momentum.1) | copy-start | bytes 1769476
